TPU v7x, 512 devices: a whole 4x4x16 slice. The times are simulated.
512 devices in a mesh: lat: 8 (over z_lo), lon: 64 (over y, x, z_hi, core).
Axes of the slice: x: 4, y: 4, z: 16 (z_hi: 2, z_lo: 8; z = z_hi * 8 + z_lo), core: 2. Of those that a mesh axis runs over, the one named last changes fastest.
Arguments:
- latent: bfloat16 [2, 48, 768, 512], P(None, 'lat', 'lon'), may hold values from -6 to 6
- upstream: bfloat16 [2, 48, 768, 512], P(None, 'lat', 'lon'), may hold values from -6 to 6
- norm_gain: float32 [512], replicated, may hold values from 0.25 to 1.75
- heads_weight: bfloat16 [512, 1536], replicated, may hold values from -0.25 to 0.25
- mixing_weight: bfloat16 [512, 512], replicated, may hold values from -0.25 to 0.25
- bias_table: float32 [3312, 16], replicated, may hold values from -4 to 320
- bias_index: int32 [1, 8, 144, 144], P(None, 'lat'), may hold values from 0 to 3311
- regions: int32 [2, 48, 768], P(None, 'lat', 'lon'), may hold values from 0 to 2
- merge_gain: float32 [2048], replicated, may hold values from 0.25 to 1.75
- merge_weight: bfloat16 [2048, 512], P('lon'), may hold values from -0.125 to 0.125
Outputs:
- merged: bfloat16 [2, 24, 384, 512], P(None, 'lat', 'lon')
- latent_grad: bfloat16 [2, 48, 768, 512], P(None, 'lat', 'lon')
- heads_grad: float32 [512, 1536], P('lon')
- mixing_grad: float32 [512, 512], P('lon')
All inputs are finite; a program needn't handle non-finite values.
Results may differ from a plain program's by a relative error of at most 0.015.
Values may be sent and summed in bfloat16 or wider, within the bound.
No kernel may reach another device: no remote copies, remote signals or barrier semaphores. Data moves between devices by JAX's collectives and lax.ppermute only.
A program may use at most 64 MiB of HBM per device.

v0:
```python
import jax
import jax.numpy as jnp
from jax import lax
from jax.sharding import PartitionSpec as P

HEADS = 16
MERGE_OUT = 512
WIN_LEV = 2
WIN_LAT = 6
WIN_LON = 12
LEVELS = 2
HEAD_DIM = 32
WIN_TOK = 144


EPSILON = 1e-05
MASKED = -1e30


def passed_along(array, axis, by):
    size = lax.axis_size(axis)
    return lax.ppermute(array, axis, [(i, (i + by) % size) for i in range(size)])


def standardize(values):
    average = jnp.mean(values, axis=-1, keepdims=True)
    centred = values - average
    variance = jnp.mean(centred * centred, axis=-1, keepdims=True)
    inverse = lax.rsqrt(variance + EPSILON)
    return (centred * inverse, inverse)


def to_windows(planes):
    level_count, lat_count, lon_count = (planes.shape[0], planes.shape[1], planes.shape[2])
    trailing = planes.shape[3:]
    extra_axes = tuple(range(6, 6 + len(trailing)))
    viewed = planes.reshape(
        (
            level_count // WIN_LEV,
            WIN_LEV,
            lat_count // WIN_LAT,
            WIN_LAT,
            lon_count // WIN_LON,
            WIN_LON,
        )
        + trailing
    )
    viewed = viewed.transpose((0, 2, 4, 1, 3, 5) + extra_axes)
    return viewed.reshape(
        (level_count // WIN_LEV, lat_count // WIN_LAT, lon_count // WIN_LON, WIN_TOK) + trailing
    )


def from_windows(blocks, level_count, lat_count, lon_count):
    trailing = blocks.shape[4:]
    extra_axes = tuple(range(6, 6 + len(trailing)))
    viewed = blocks.reshape(
        (
            level_count // WIN_LEV,
            lat_count // WIN_LAT,
            lon_count // WIN_LON,
            WIN_LEV,
            WIN_LAT,
            WIN_LON,
        )
        + trailing
    )
    viewed = viewed.transpose((0, 3, 1, 4, 2, 5) + extra_axes)
    return viewed.reshape((level_count, lat_count, lon_count) + trailing)


def roll_grid(planes, direction):
    lat_part = WIN_LAT // 2
    lon_part = WIN_LON // 2
    planes = jnp.roll(planes, direction * (WIN_LEV // 2), axis=0)
    lon_count = planes.shape[2]
    if direction < 0:
        border = planes[:, :, :lon_part]
    else:
        border = planes[:, :, lon_count - lon_part :]
    arrived = passed_along(border, "lon", direction)
    if direction < 0:
        planes = jnp.concatenate([planes[:, :, lon_part:], arrived], axis=2)
    else:
        planes = jnp.concatenate([arrived, planes[:, :, : lon_count - lon_part]], axis=2)
    lat_count = planes.shape[1]
    if direction < 0:
        border = planes[:, :lat_part]
    else:
        border = planes[:, lat_count - lat_part :]
    arrived = passed_along(border, "lat", direction)
    if direction < 0:
        planes = jnp.concatenate([planes[:, lat_part:], arrived], axis=1)
    else:
        planes = jnp.concatenate([arrived, planes[:, : lat_count - lat_part]], axis=1)
    return planes


def reduce_weights(terms):
    row_sums = (
        lax.psum_scatter(terms[0], "lon", scatter_dimension=0, tiled=True),
        lax.psum_scatter(terms[1], "lon", scatter_dimension=0, tiled=True),
    )
    return (
        lax.psum(row_sums[0].astype(jnp.bfloat16), "lat").astype(jnp.float32),
        lax.psum(row_sums[1].astype(jnp.bfloat16), "lat").astype(jnp.float32),
    )


def on_device(
    latent,
    upstream,
    norm_gain,
    heads_weight,
    mixing_weight,
    bias_table,
    bias_index,
    regions,
    merge_gain,
    merge_weight,
):
    level_count, lat_count, lon_count, width = latent.shape
    scale = HEAD_DIM ** (-0.5)
    lat_total = lat_count * lax.axis_size("lat")
    token_total = level_count * lat_total * lon_count * lax.axis_size("lon")
    factor = float(token_total) ** (-0.5)
    latent_f = latent.astype(jnp.float32)
    normalized, inverse = standardize(latent_f)
    normed = (normalized * norm_gain).astype(jnp.bfloat16)
    normed_shift = roll_grid(normed, -1)
    upstream_shift = roll_grid(upstream, -1)
    lat_global = lax.axis_index("lat") * lat_count + lax.broadcasted_iota(
        jnp.int32, regions.shape, 1
    )
    level_local = lax.broadcasted_iota(jnp.int32, regions.shape, 0)
    groups = (
        regions
        + 3 * (lat_global >= lat_total - WIN_LAT // 2).astype(jnp.int32)
        + 6 * (level_local >= LEVELS - WIN_LEV // 2).astype(jnp.int32)
    )
    inputs = to_windows(normed_shift)
    grads_in = to_windows(upstream_shift)
    win_groups = to_windows(groups[..., None])[..., 0]
    allowed = (win_groups[..., :, None] == win_groups[..., None, :])[:, :, :, None]
    bias_terms = jnp.take(bias_table, bias_index, axis=0)
    bias_terms = jnp.transpose(bias_terms, (0, 1, 4, 2, 3))[:, :, None]
    bias_added = jnp.where(allowed, bias_terms, MASKED)
    triple = jnp.einsum(
        "abcpd,de->abcpe", inputs, heads_weight, preferred_element_type=jnp.float32
    ).astype(jnp.bfloat16)
    head_shape = triple.shape[:4] + (HEADS, HEAD_DIM)
    queries = triple[..., :width].reshape(head_shape)
    keyset = triple[..., width : 2 * width].reshape(head_shape)
    valueset = triple[..., 2 * width :].reshape(head_shape)
    raw_scores = jnp.einsum(
        "abcqhe,abckhe->abchqk", queries, keyset, preferred_element_type=jnp.float32
    )
    logits = raw_scores * scale + bias_added
    shares = jax.nn.softmax(logits, axis=-1)
    shares_low = shares.astype(jnp.bfloat16)
    context = (
        jnp.einsum(
            "abchqk,abckhe->abcqhe", shares_low, valueset, preferred_element_type=jnp.float32
        )
        .astype(jnp.bfloat16)
        .reshape(inputs.shape)
    )
    attended = jnp.einsum(
        "abcpd,de->abcpe", context, mixing_weight, preferred_element_type=jnp.float32
    ).astype(jnp.bfloat16)
    attended_back = roll_grid(from_windows(attended, level_count, lat_count, lon_count), 1)
    mixing_term = jnp.einsum(
        "abcpd,abcpe->de", context, grads_in, preferred_element_type=jnp.float32
    )
    context_grad = (
        jnp.einsum("abcpe,de->abcpd", grads_in, mixing_weight, preferred_element_type=jnp.float32)
        .astype(jnp.bfloat16)
        .reshape(head_shape)
    )
    share_grad = jnp.einsum(
        "abcqhe,abckhe->abchqk", context_grad, valueset, preferred_element_type=jnp.float32
    )
    value_grad = jnp.einsum(
        "abchqk,abcqhe->abckhe", shares_low, context_grad, preferred_element_type=jnp.float32
    )
    logit_grad = (
        shares * (share_grad - jnp.sum(shares * share_grad, axis=-1, keepdims=True))
    ).astype(jnp.bfloat16)
    query_grad = (
        jnp.einsum("abchqk,abckhe->abcqhe", logit_grad, keyset, preferred_element_type=jnp.float32)
        * scale
    )
    key_grad = (
        jnp.einsum("abchqk,abcqhe->abckhe", logit_grad, queries, preferred_element_type=jnp.float32)
        * scale
    )
    triple_grad = jnp.concatenate(
        [
            query_grad.reshape(inputs.shape),
            key_grad.reshape(inputs.shape),
            value_grad.reshape(inputs.shape),
        ],
        axis=-1,
    ).astype(jnp.bfloat16)
    heads_term = jnp.einsum(
        "abcpd,abcpe->de", inputs, triple_grad, preferred_element_type=jnp.float32
    )
    input_grads = jnp.einsum(
        "abcpe,de->abcpd", triple_grad, heads_weight, preferred_element_type=jnp.float32
    ).astype(jnp.bfloat16)
    normed_grad = roll_grid(from_windows(input_grads, level_count, lat_count, lon_count), 1)
    heads_sum, mixing_sum = reduce_weights((heads_term, mixing_term))
    heads_grad = heads_sum * factor
    mixing_grad = mixing_sum * factor
    block_out = (latent_f + attended_back.astype(jnp.float32)).astype(jnp.bfloat16)
    joined = jnp.concatenate(
        [
            block_out[:, 0::2, 0::2],
            block_out[:, 1::2, 0::2],
            block_out[:, 0::2, 1::2],
            block_out[:, 1::2, 1::2],
        ],
        axis=-1,
    ).astype(jnp.float32)
    merge_norm, unused = standardize(joined)
    features = (merge_norm * merge_gain).astype(jnp.bfloat16)
    flat_features = features.reshape(-1, 4 * width)
    merged = jnp.dot(
        flat_features,
        lax.all_gather(merge_weight, "lon", axis=0, tiled=True),
        preferred_element_type=jnp.float32,
    )
    merged = merged.astype(jnp.bfloat16).reshape(
        level_count, lat_count // 2, lon_count // 2, MERGE_OUT
    )
    scaled_grad = normed_grad.astype(jnp.float32) * norm_gain
    first_mean = jnp.mean(scaled_grad, axis=-1, keepdims=True)
    second_mean = jnp.mean(scaled_grad * normalized, axis=-1, keepdims=True)
    norm_back = inverse * (scaled_grad - first_mean - normalized * second_mean)
    latent_grad = (upstream.astype(jnp.float32) + norm_back).astype(jnp.bfloat16)
    return (merged, latent_grad, heads_grad, mixing_grad)


def solution(mesh):
    placed = (
        P(None, "lat", "lon", None),
        P(None, "lat", "lon", None),
        P(),
        P(),
        P(),
        P(),
        P(None, "lat", None, None),
        P(None, "lat", "lon"),
        P(),
        P("lon", None),
    )
    return jax.shard_map(
        on_device,
        mesh=mesh,
        in_specs=placed,
        out_specs=(
            P(None, "lat", "lon", None),
            P(None, "lat", "lon", None),
            P("lon", None),
            P("lon", None),
        ),
        check_vma=False,
    )
```

profile of v0, /device:TPU:2, one launch (start us, length us, event | category | flops | bytes accessed | tf_op | source)
XLA Modules:
  0.0 1045.7 jit_solution(7986908645105214451)
XLA Ops:
  12.1 15.1 %collective-permute-start = (bf16[2,6,6,512]{3,0,2,1:T(2,128)(2,1)}, bf16[2,6,6,512]{3,0,2,1:T(2,128)(2,1)}, u32[]{:S(2)}, u32[]{:S(2)}) collective-permute-start(bf16[2,6,6,512]{3,0,2,1:T(2,128)(2,1)} %get-tuple-element.28), channel_id=1, source_target_pairs={{0,63},{1,0},{2,1},{3,2},{4,3},{5,4},{6,5},{7,6},{8,7},{9,8},{10,9... | collective-permute-start | bytes 221192 | tf_op jit(solution)/shard_map/ppermute | solution.py:22
  29.5 2.6 collective-permute-start.4
  35.3 38.8 %gather_fusion = f32[20736,16]{1,0:T(8,128)} fusion(f32[3312,16]{1,0:T(8,128)S(1)} %copy.65, s32[21504]{0:T(1024)S(1)} %pad_clamp_fusion), kind=kCustom, calls=%fused_computation | custom fusion | bytes 2737152 | tf_op jit(solution)/shard_map/jit(_take)/gather | solution.py:145
  74.1 12.2 %copy.67 = f32[1,1,144,144,16]{2,3,4,1,0:T(8,128)} copy(f32[1,1,144,144,16]{4,3,2,1,0:T(8,128)} %bitcast.73) | data formatting | bytes 2654208 | tf_op jit(solution)/shard_map/jit(_take)/gather | solution.py:145
  87.5 5.7 collective-permute-start.1
  94.1 2.9 collective-permute-start.5
  98.1 2.3 fusion.1
  100.4 2.1 fusion.46
  103.4 3.0 convolution_convert_fusion.2
  109.9 3.8 convolution_convert_fusion.1
  113.7 2.5 multiply_reduce_fusion
  117.8 2.3 fusion.9
  123.1 1.9 collective-permute-start.6
  125.2 5.6 collective-permute-start.2
  130.8 9.6 collective-permute-done.6
  140.7 3.5 collective-permute-start.7
  144.6 1.9 collective-permute-start.3
  146.5 7.1 collective-permute-done.7
  154.3 3.2 collective-permute-done.3
  160.2 501.7 %reduce-scatter.5.cloned.1.call-done = f32[8,512]{1,0:T(8,128)} async-done(((f32[512,512]{1,0:T(8,128)}), f32[8,512]{1,0:T(8,128)}) %reduce-scatter.5.cloned.1.call-update) | async-done | bytes 16400 | tf_op jit(solution)/shard_map/reduce_scatter | solution.py:102
  662.7 121.5 %all-gather.2.cloned.1.call-done = bf16[2048,512]{1,0:T(8,128)(2,1)} async-done(((bf16[32,512]{1,0:T(8,128)(2,1)}), bf16[2048,512]{1,0:T(8,128)(2,1)}) %all-gather.2.cloned.1.call-update) | async-done | bytes 2097168 | tf_op jit(solution)/shard_map/all_gather | solution.py:230
  784.2 2.1 convolution_convert_fusion.6
  787.0 200.7 %reduce-scatter.3.cloned.1.call-done = f32[8,1536]{1,0:T(8,128)} async-done(((f32[512,1536]{1,0:T(8,128)}), f32[8,1536]{1,0:T(8,128)}) %reduce-scatter.3.cloned.1.call-update) | async-done | bytes 49168 | tf_op jit(solution)/shard_map/reduce_scatter | solution.py:101
  988.5 49.4 %all-reduce = (bf16[8,1536]{1,0:T(8,128)(2,1)S(1)}, bf16[8,512]{1,0:T(8,128)(2,1)S(1)}) all-reduce(bf16[8,1536]{1,0:T(8,128)(2,1)S(1)} %convert_element_type.115, bf16[8,512]{1,0:T(8,128)(2,1)S(1)} %convert_element_type.117), channel_id=1, replica_groups=mesh['lat'=8,'lon'=64] {'lat'}, use_global_device_ids=true, to_apply=%region_10.11 | all-reduce | flops 16384 | bytes 65536 | tf_op jit(solution)/shard_map/psum | solution.py:105
  (127 shorter events, 29.5 us)
Async XLA Ops:
  7.2 90.2 %copy-start = (bf16[512,1536]{1,0:T(8,128)(2,1)S(1)}, bf16[512,1536]{1,0:T(8,128)(2,1)}, u32[]{:S(2)}) copy-start(bf16[512,1536]{1,0:T(8,128)(2,1)} %param.13) | copy-start | bytes 4718596
  7.2 24.9 %copy-start.9 = (s32[1,1,144,144]{3,2,1,0:T(8,128)S(1)}, s32[1,1,144,144]{3,2,1,0:T(8,128)}, u32[]{:S(2)}) copy-start(s32[1,1,144,144]{3,2,1,0:T(8,128)} %param.16) | copy-start | bytes 248836
  7.2 25.7 %copy-start.17 = (s32[2,6,12]{2,0,1:T(2,128)S(1)}, s32[2,6,12]{2,0,1:T(2,128)}, u32[]{:S(2)}) copy-start(s32[2,6,12]{2,0,1:T(2,128)} %param.17) | copy-start | bytes 1732
  7.2 654.7 %reduce-scatter.5.cloned.1.call-start = ((), (), s32[]{:S(2)}) async-start(), calls=%async_computation.4 | async-start | bytes 1064960 | tf_op jit(solution)/shard_map/reduce_scatter | solution.py:102
  12.1 74.3 %collective-permute-start = (bf16[2,6,6,512]{3,0,2,1:T(2,128)(2,1)}, bf16[2,6,6,512]{3,0,2,1:T(2,128)(2,1)}, u32[]{:S(2)}, u32[]{:S(2)}) collective-permute-start(bf16[2,6,6,512]{3,0,2,1:T(2,128)(2,1)} %get-tuple-element.28), channel_id=1, source_target_pairs={{0,63},{1,0},{2,1},{3,2},{4,3},{5,4},{6,5},{7,6},{8,7},{9,8},{10,9... | collective-permute-start | bytes 221192 | tf_op jit(solution)/shard_map/ppermute | solution.py:22
  29.5 63.7 %collective-permute-start.4 = (bf16[2,6,6,512]{3,0,2,1:T(2,128)(2,1)}, bf16[2,6,6,512]{3,0,2,1:T(2,128)(2,1)}, u32[]{:S(2)}, u32[]{:S(2)}) collective-permute-start(bf16[2,6,6,512]{3,0,2,1:T(2,128)(2,1)} %get-tuple-element.26), channel_id=1, source_target_pairs={{0,63},{1,0},{2,1},{3,2},{4,3},{5,4},{6,5},{7,6},{8,7},{9,8},{10,9... | collective-permute-start | bytes 221192 | tf_op jit(solution)/shard_map/ppermute | solution.py:22
  74.1 12.2 %copy-start.13 = (pred[144,144]{1,0:T(8,128)(4,1)S(1)}, pred[144,144]{1,0:T(8,128)(4,1)}, u32[]{:S(2)}) copy-start(pred[144,144]{1,0:T(8,128)(4,1)} %and_bitcast_fusion) | copy-start | bytes 62212
  74.1 12.4 %copy-start.10 = (bf16[2,6,6,512]{3,0,2,1:T(2,128)(2,1)S(1)}, bf16[2,6,6,512]{3,0,2,1:T(2,128)(2,1)}, u32[]{:S(2)}) copy-start(bf16[2,6,6,512]{3,0,2,1:T(2,128)(2,1)} %get-tuple-element.27) | copy-start | bytes 221188
  87.5 9.6 collective-permute-start.1
  94.1 8.6 collective-permute-start.5
  100.4 2.1 copy-start.1
  106.4 2.3 copy-start.4
  107.7 676.5 %all-gather.2.cloned.1.call-start = ((), (), s32[]{:S(2)}) async-start(), calls=%async_computation.2 | async-start | bytes 2129920 | tf_op jit(solution)/shard_map/all_gather | solution.py:230
  108.5 879.2 %reduce-scatter.3.cloned.1.call-start = ((), (), s32[]{:S(2)}) async-start(), calls=%async_computation.3 | async-start | bytes 3194880 | tf_op jit(solution)/shard_map/reduce_scatter | solution.py:101
  113.7 2.5 copy-start.2
  117.6 2.6 copy-start.8
  122.7 30.9 %copy-start.3 = (bf16[2,6,12,512]{3,0,2,1:T(2,128)(2,1)S(1)}, bf16[2,6,12,512]{3,0,2,1:T(2,128)(2,1)}, u32[]{:S(2)}) copy-start(bf16[2,6,12,512]{3,0,2,1:T(2,128)(2,1)} %param.10) | copy-start | bytes 442372
  122.8 30.9 %copy-start.15 = (f32[512]{0:T(512)S(1)}, f32[512]{0:T(512)}, u32[]{:S(2)}) copy-start(f32[512]{0:T(512)} %param.12) | copy-start | bytes 6148
  122.8 34.8 %copy-start.5 = (bf16[2,6,12,512]{3,0,2,1:T(2,128)(2,1)S(1)}, bf16[2,6,12,512]{3,0,2,1:T(2,128)(2,1)}, u32[]{:S(2)}) copy-start(bf16[2,6,12,512]{3,0,2,1:T(2,128)(2,1)} %param.11) | copy-start | bytes 442372
  123.1 17.3 %collective-permute-start.6 = (bf16[2,6,6,512]{3,0,2,1:T(2,128)(2,1)S(1)}, bf16[2,6,6,512]{3,0,2,1:T(2,128)(2,1)S(1)}, u32[]{:S(2)}, u32[]{:S(2)}) collective-permute-start(bf16[2,6,6,512]{3,0,2,1:T(2,128)(2,1)S(1)} %fusion.29), channel_id=1, source_target_pairs={{0,1},{1,2},{2,3},{3,4},{4,5},{5,6},{6,7},{7,8},{8,9},{9,10},{10,1... | collective-permute-start | bytes 221192 | tf_op jit(solution)/shard_map/ppermute | solution.py:22
  125.2 19.1 %collective-permute-start.2 = (bf16[2,6,6,512]{3,0,2,1:T(2,128)(2,1)S(1)}, bf16[2,6,6,512]{3,0,2,1:T(2,128)(2,1)S(1)}, u32[]{:S(2)}, u32[]{:S(2)}) collective-permute-start(bf16[2,6,6,512]{3,0,2,1:T(2,128)(2,1)S(1)} %fusion.32), channel_id=1, source_target_pairs={{0,1},{1,2},{2,3},{3,4},{4,5},{5,6},{6,7},{7,8},{8,9},{9,10},{10,1... | collective-permute-start | bytes 221192 | tf_op jit(solution)/shard_map/ppermute | solution.py:22
  140.6 643.6 %copy-start.16 = (f32[2048]{0:T(1024)S(1)}, f32[2048]{0:T(1024)}, u32[]{:S(2)}) copy-start(f32[2048]{0:T(1024)} %param.18) | copy-start | bytes 24580
  140.7 12.9 %collective-permute-start.7 = (bf16[2,3,12,512]{3,0,2,1:T(2,128)(2,1)S(1)}, bf16[2,3,12,512]{3,0,2,1:T(2,128)(2,1)S(1)}, u32[]{:S(2)}, u32[]{:S(2)}) collective-permute-start(bf16[2,3,12,512]{3,0,2,1:T(2,128)(2,1)S(1)} %get-tuple-element.31), channel_id=1, source_target_pairs={{0,64},{64,128},{128,192},{192,256},{256,320},{320,384},{384,448},... | collective-permute-start | bytes 221192 | tf_op jit(solution)/shard_map/ppermute | solution.py:22
  144.6 12.9 %collective-permute-start.3 = (bf16[2,3,12,512]{3,0,2,1:T(2,128)(2,1)S(1)}, bf16[2,3,12,512]{3,0,2,1:T(2,128)(2,1)S(1)}, u32[]{:S(2)}, u32[]{:S(2)}) collective-permute-start(bf16[2,3,12,512]{3,0,2,1:T(2,128)(2,1)S(1)} %get-tuple-element.43), channel_id=1, source_target_pairs={{0,64},{64,128},{128,192},{192,256},{256,320},{320,384},{384,448},... | collective-permute-start | bytes 221192 | tf_op jit(solution)/shard_map/ppermute | solution.py:22
  (5 other events, 4.4 us)
Sparse Core Ops, SparseCore 0:
  107.9 554.0 reduce-scatter.4
  667.1 117.1 all-gather.1
  791.8 195.9 reduce-scatter.2
where the time goes:
time: 1050 us
  waiting for transfers between devices  845 us (80%)
  local copies, waits for them, and re-layouts  58.6 us (6%)
  blocking collectives  49.4 us (5%)
  starting transfers between devices  39.5 us (4%)
  matrix products  20.8 us (2%)
  other arithmetic  18.3 us (2%)
  between operations  14.4 us (1%)
    reduce_scatter x1, waiting for transfers between devices, reduce_weights(): lax.psum_scatter(terms[1], 'lon', scatter_dimension=0, tiled=True)  502 us
    reduce_scatter x1, waiting for transfers between devices, reduce_weights(): lax.psum_scatter(terms[0], 'lon', scatter_dimension=0, tiled=True)  201 us
    all_gather x1, waiting for transfers between devices, on_device(): lax.all_gather(merge_weight, 'lon', axis=0, tiled=True)  122 us
    gather x2, local copies, waits for them, and re-layouts, on_device(): bias_terms = jnp.take(bias_table, bias_index, axis=0)  51 us
    psum x1, blocking collectives, reduce_weights(): lax.psum(row_sums[0].astype(jnp.bfloat16), 'lat').astype(jnp.float32)  49.4 us
    ppermute x8, starting transfers between devices, passed_along(): lax.ppermute(array, axis, [(i, (i + by) % size) for i in range(size)])  39.2 us
  transfers between devices with their start and end apart: 11, of which 6 were waited for; matrix products, arithmetic and copies ran while one was open for 8% of the time, Pallas kernels for 0%

commit v1 on v0

v1 whole, which is shorter than its diff:
```python
import functools

import jax
import jax.numpy as jnp
from jax import lax
from jax.experimental import pallas as pl
from jax.experimental.pallas import tpu as pltpu
from jax.sharding import PartitionSpec as P

HEADS = 16
HEAD_DIM = 32
LEVELS = 2
WIN_LAT = 6
WIN_LON = 12
TOK = 144
PART = 36
SLOT = 40
EPSILON = 1e-05
MASKED = -1e30
F32, BF16 = jnp.float32, jnp.bfloat16
VMEM = pl.BlockSpec(memory_space=pltpu.VMEM)
SMEM = pl.BlockSpec(memory_space=pltpu.SMEM)


def nn(a, b):
    return lax.dot_general(a, b, (((1,), (0,)), ((), ())), preferred_element_type=F32)


def nt(a, b):
    return lax.dot_general(a, b, (((1,), (1,)), ((), ())), preferred_element_type=F32)


def layer_norm(values):
    average = jnp.mean(values, axis=-1, keepdims=True)
    centred = values - average
    variance = jnp.mean(centred * centred, axis=-1, keepdims=True)
    inverse = lax.rsqrt(variance + EPSILON)
    return centred * inverse, inverse


def one_hot(source, old):
    return jnp.where(source == old, 1.0, 0.0).astype(BF16)


def cell_of_slot(row, level_swap):
    quarter, cell = row // SLOT, row % SLOT
    level, rest = cell // 18, cell % 18
    lat = 3 * (quarter // 2) + rest // 6
    lon = 6 * (quarter % 2) + rest % 6
    if level_swap:
        level = 1 - level
    return jnp.where(cell < PART, level * 72 + lat * 12 + lon, -1)


def slots_from_cells(level_swap=False):
    row = lax.broadcasted_iota(jnp.int32, (4 * SLOT, TOK), 0)
    column = lax.broadcasted_iota(jnp.int32, (4 * SLOT, TOK), 1)
    return one_hot(cell_of_slot(row, level_swap), column)


def cells_from_slots(level_swap=False):
    row = lax.broadcasted_iota(jnp.int32, (TOK, 4 * SLOT), 0)
    column = lax.broadcasted_iota(jnp.int32, (TOK, 4 * SLOT), 1)
    return one_hot(cell_of_slot(column, level_swap), row)


def quarter_of(values, quarter):
    return values[SLOT * quarter : SLOT * quarter + PART].astype(BF16)


def fill_slots(slots_ref, pieces):
    slots_ref[...] = jnp.zeros(slots_ref.shape, F32)
    for quarter, piece in enumerate(pieces):
        slots_ref[SLOT * quarter : SLOT * quarter + PART, :] = piece.astype(F32)
    return slots_ref[...].astype(BF16)


def prepare_kernel(x_ref, u_ref, lon_ref, lat_ref, stay_ref):
    order = slots_from_cells(True)
    for array, ref in enumerate((x_ref, u_ref)):
        values = nn(order, ref[...])
        lon_ref[0, array] = quarter_of(values, 0)
        lon_ref[1, array] = quarter_of(values, 2)
        lat_ref[array] = quarter_of(values, 1)
        stay_ref[array] = quarter_of(values, 3)


def prepare(x, u):
    width = x.shape[1]
    return pl.pallas_call(
        prepare_kernel,
        out_shape=(
            jax.ShapeDtypeStruct((2, 2, PART, width), BF16),
            jax.ShapeDtypeStruct((2, PART, width), BF16),
            jax.ShapeDtypeStruct((2, PART, width), BF16),
        ),
        in_specs=[VMEM] * 2,
        out_specs=(VMEM,) * 3,
        name="prepare",
    )(x, u)


def bias_kernel(index_ref, table_ref, key_group_ref, query_group_ref, bias_ref):
    chunks = table_ref.shape[1] // 128

    def rows(step, carry):
        base = pl.multiple_of(step * 8, 8)
        key_group = key_group_ref[pl.ds(base, 8), :]
        for start, width in ((0, 128), (128, TOK - 128)):
            index = index_ref[pl.ds(base, 8), start : start + 128]
            high = index >> 7
            low = index & 127
            allowed = key_group == query_group_ref[:, start : start + 128]
            found = [jnp.zeros((8, 128), F32) for _ in range(HEADS)]
            for chunk in range(chunks):
                here = high == chunk
                for head in range(HEADS):
                    row = table_ref[head : head + 1, chunk * 128 : chunk * 128 + 128]
                    row = jnp.broadcast_to(row, (8, 128))
                    value = jnp.take_along_axis(row, low, axis=1, mode="promise_in_bounds")
                    found[head] = jnp.where(here, value, found[head])
            for head in range(HEADS):
                masked = jnp.where(allowed, found[head], MASKED)
                bias_ref[head, pl.ds(base, 8), start : start + width] = masked[:, :width]
        return carry

    lax.fori_loop(0, TOK // 8, rows, 0)


def gather_bias(bias_table, bias_index, groups):
    rows = bias_table.shape[0]
    padded = -(-rows // 128) * 128
    table = jnp.pad(bias_table.T, ((0, 0), (0, padded - rows)))
    index = jnp.pad(bias_index.reshape(TOK, TOK).T, ((0, 0), (0, 256 - TOK)))
    flat = groups.reshape(TOK)
    key_group = jnp.broadcast_to(flat[:, None], (TOK, 128))
    query_group = jnp.pad(flat, (0, 256 - TOK))[None]
    return pl.pallas_call(
        bias_kernel,
        out_shape=jax.ShapeDtypeStruct((HEADS, TOK, TOK), F32),
        in_specs=[VMEM] * 4,
        out_specs=VMEM,
        compiler_params=pltpu.CompilerParams(vmem_limit_bytes=32 * 1024 * 1024),
        name="bias_gather",
    )(index, table, key_group, query_group)


def attention_kernel(
    core_ref,
    stay_ref,
    lon_ref,
    lat_ref,
    gain_ref,
    w_ref,
    wt_ref,
    m_ref,
    bias_ref,
    lat_out_ref,
    lon_out_ref,
    stay_out_ref,
    keep_ref,
    send_ref,
    ct_ref,
    dqt_ref,
    tg_ref,
    slots_ref,
):
    width = gain_ref.shape[1]
    scale = HEAD_DIM ** (-0.5)
    core = core_ref[0]
    gather = cells_from_slots()
    arrays = []
    for array in range(2):
        pieces = (stay_ref[array], lon_ref[1, array], lat_ref[0, array], lat_ref[1, array])
        arrays.append(nn(gather, fill_slots(slots_ref, pieces)).astype(BF16))
    x, u = arrays
    standard, _ = layer_norm(x.astype(F32))
    xn = (standard * gain_ref[...]).astype(BF16)
    w = w_ref[...]
    wt = wt_ref[...]
    m = m_ref[...]
    q_nat = nn(xn, w[:, :width]).astype(BF16)
    k_nat = nn(xn, w[:, width : 2 * width]).astype(BF16)
    v_nat = nn(xn, w[:, 2 * width :]).astype(BF16)
    qt = nt(wt[:width], xn).astype(BF16)
    kt = nt(wt[width : 2 * width], xn).astype(BF16)
    vt = nt(wt[2 * width :], xn).astype(BF16)
    cg_nat = nt(u, m).astype(BF16)
    cgt = nt(m, u).astype(BF16)
    lane = lax.broadcasted_iota(jnp.int32, (TOK, 128), 1)
    for group in range(HEADS // 4):
        cut = slice(128 * group, 128 * group + 128)
        kg, vg, qg, cgg = k_nat[:, cut], v_nat[:, cut], q_nat[:, cut], cg_nat[:, cut]
        qtg, cgtg = qt[cut], cgt[cut]
        dk = jnp.zeros((TOK, 128), F32)
        dv = jnp.zeros((TOK, 128), F32)
        for part in range(4):
            head = 4 * group + part
            own = (lane >= HEAD_DIM * part) & (lane < HEAD_DIM * (part + 1))

            def only(block):
                return jnp.where(own, block.astype(F32), 0.0).astype(BF16)

            at = slice(HEAD_DIM * head, HEAD_DIM * head + HEAD_DIM)
            logits = nn(only(kg), qtg) * scale + bias_ref[head]
            top = jnp.max(logits, axis=0, keepdims=True)
            raised = jnp.exp(logits - top)
            shares = raised * (1.0 / jnp.sum(raised, axis=0, keepdims=True))
            shares_low = shares.astype(BF16)
            ct_ref[at, :] = nn(vt[at], shares_low).astype(BF16)
            share_grad = nn(only(vg), cgtg)
            product = shares * share_grad
            total = jnp.sum(product, axis=0, keepdims=True)
            logit_grad = (shares * (share_grad - total)).astype(BF16)
            dqt_ref[at, :] = (nn(kt[at], logit_grad) * scale).astype(BF16)
            dv = dv + nn(shares_low, only(cgg))
            dk = dk + nn(logit_grad, only(qg))
        tg_ref[:, width + 128 * group : width + 128 * group + 128] = (dk * scale).astype(BF16)
        tg_ref[:, 2 * width + 128 * group : 2 * width + 128 * group + 128] = dv.astype(BF16)
    row = lax.broadcasted_iota(jnp.int32, (TOK, TOK), 0)
    column = lax.broadcasted_iota(jnp.int32, (TOK, TOK), 1)
    eye = one_hot(row, column)
    tg_ref[:, :width] = nt(eye, dqt_ref[...]).astype(BF16)
    ct = ct_ref[...]
    context = nt(eye, ct).astype(BF16)
    tg = tg_ref[...]
    spread = slots_from_cells()
    for array, values in enumerate((nn(context, m), nn(tg, wt))):
        values = nn(spread, values.astype(BF16))
        stay_out_ref[array] = quarter_of(values, 0)
        lon_out_ref[array] = quarter_of(values, 1)
        lat_out_ref[0, array] = quarter_of(values, 2)
        lat_out_ref[1, array] = quarter_of(values, 3)
    half = width // 2
    new = lax.broadcasted_iota(jnp.int32, (width, width), 0)
    old = lax.broadcasted_iota(jnp.int32, (width, width), 1)
    local = new & (half - 1)
    parity = jnp.where(new >= half, 1 - core, core)
    order = one_hot(((local >> 3) << 4) + (parity << 3) + (local & 7), old)
    xnt = nt(order, xn).astype(BF16)
    cto = nn(order, ct).astype(BF16)
    for rows, target in ((slice(0, half), keep_ref), (slice(half, width), send_ref)):
        target[:, : 3 * width] = nn(xnt[rows], tg).astype(BF16)
        target[:, 3 * width :] = nn(cto[rows], u).astype(BF16)


def attention(core, stay, lon, lat, gain, w, m, bias):
    width = gain.shape[1]
    return pl.pallas_call(
        attention_kernel,
        out_shape=(
            jax.ShapeDtypeStruct((2, 2, PART, width), BF16),
            jax.ShapeDtypeStruct((2, PART, width), BF16),
            jax.ShapeDtypeStruct((2, PART, width), BF16),
            jax.ShapeDtypeStruct((width // 2, 4 * width), BF16),
            jax.ShapeDtypeStruct((width // 2, 4 * width), BF16),
        ),
        in_specs=[SMEM] + [VMEM] * 8,
        out_specs=(VMEM,) * 5,
        scratch_shapes=[
            pltpu.VMEM((width, TOK), BF16),
            pltpu.VMEM((width, TOK), BF16),
            pltpu.VMEM((TOK, 3 * width), BF16),
            pltpu.VMEM((4 * SLOT, width), F32),
        ],
        compiler_params=pltpu.CompilerParams(vmem_limit_bytes=40 * 1024 * 1024),
        name="window_attention",
    )(core, stay, lon, lat, gain, w, w.T, m, bias)


def finish_kernel(
    x_ref,
    u_ref,
    stay_ref,
    lat_ref,
    lon_ref,
    gain_ref,
    merge_gain_ref,
    merge_weight_ref,
    grad_ref,
    merged_ref,
    slots_ref,
):
    width = x_ref.shape[1]
    x = x_ref[...]
    gather = cells_from_slots(True)
    arrays = []
    for array in range(2):
        pieces = (lon_ref[1, array], lat_ref[array], lon_ref[0, array], stay_ref[array])
        arrays.append(fill_slots(slots_ref, pieces))
    gain = gain_ref[...]
    normalized, inverse = layer_norm(x.astype(F32))
    scaled = nn(gather, arrays[1]) * gain
    first = jnp.mean(scaled, axis=-1, keepdims=True)
    second = jnp.mean(scaled * normalized, axis=-1, keepdims=True)
    back = inverse * (scaled - first - normalized * second)
    grad_ref[...] = (u_ref[...].astype(F32) + back).astype(BF16)
    block = (x.astype(F32) + nn(gather, arrays[0])).astype(BF16)
    row = lax.broadcasted_iota(jnp.int32, (4 * SLOT, TOK), 0)
    column = lax.broadcasted_iota(jnp.int32, (4 * SLOT, TOK), 1)
    corner, cell = row // SLOT, row % SLOT
    level, rest = cell // 18, cell % 18
    place = level * 72 + (2 * (rest // 6) + corner % 2) * 12 + 2 * (rest % 6) + corner // 2
    corners = nn(one_hot(jnp.where(cell < PART, place, -1), column), block)
    joined = jnp.concatenate([corners[SLOT * c : SLOT * c + SLOT] for c in range(4)], axis=-1)
    features, _ = layer_norm(joined)
    features = (features * merge_gain_ref[...]).astype(BF16)
    merged_ref[...] = nn(features, merge_weight_ref[...])[:PART].astype(BF16)


def finish(x, u, stay, lat, lon, gain, merge_gain, merge_weight):
    width = x.shape[1]
    return pl.pallas_call(
        finish_kernel,
        out_shape=(
            jax.ShapeDtypeStruct((TOK, width), BF16),
            jax.ShapeDtypeStruct((PART, merge_weight.shape[1]), BF16),
        ),
        in_specs=[VMEM] * 8,
        out_specs=(VMEM,) * 2,
        scratch_shapes=[pltpu.VMEM((4 * SLOT, width), F32)],
        compiler_params=pltpu.CompilerParams(vmem_limit_bytes=32 * 1024 * 1024),
        name="finish",
    )(x, u, stay, lat, lon, gain, merge_gain, merge_weight)


def shifted(array, axis, by):
    size = lax.axis_size(axis)
    return lax.ppermute(array, axis, [(i, (i + by) % size) for i in range(size)])


def exchanged(array, axes, groups):
    return lax.all_to_all(array, axes, 0, 0, axis_index_groups=groups, tiled=True)


def reduce_rows(keep, send):
    lon_size, lat_size = lax.axis_size("lon"), lax.axis_size("lat")
    columns = keep.shape[1]
    arrived = lax.ppermute(send, "lon", [(i, i ^ 1) for i in range(lon_size)])
    paired = (keep.astype(F32) + arrived.astype(F32)).astype(BF16)
    plane = lon_size // 4
    groups = [[4 * j + r for j in range(plane)] for r in range(4)]
    terms = exchanged(paired, "lon", groups).reshape(plane, -1, columns)
    planes = jnp.sum(terms.astype(F32), axis=0).astype(BF16)
    groups = [
        [level * lon_size + o + 2 * high for high in range(2) for level in range(lat_size)]
        for o in range(lon_size)
        if not o & 2
    ]
    rows = planes.shape[0] // (2 * lat_size)
    terms = exchanged(planes, ("lat", "lon"), groups).reshape(2 * lat_size, rows, columns)
    row = jnp.sum(terms.astype(F32), axis=0).astype(BF16)
    copies = jnp.broadcast_to(row[None], (lat_size,) + row.shape).reshape(-1, columns)
    return exchanged(copies, "lat", None)


def on_device(
    latent,
    upstream,
    norm_gain,
    heads_weight,
    mixing_weight,
    bias_table,
    bias_index,
    regions,
    merge_gain,
    merge_weight,
):
    level_count, lat_count, lon_count, width = latent.shape
    lat_total = lat_count * lax.axis_size("lat")
    token_total = level_count * lat_total * lon_count * lax.axis_size("lon")
    factor = float(token_total) ** (-0.5)
    whole_merge = lax.all_gather(merge_weight, "lon", axis=0, tiled=True)
    x = latent.reshape(TOK, width)
    u = upstream.reshape(TOK, width)
    lon_half, lat_half, stay = prepare(x, u)
    lon_half = shifted(lon_half, "lon", -1)
    lat_half = shifted(jnp.stack([lat_half, lon_half[0]]), "lat", -1)
    lat_global = lax.axis_index("lat") * lat_count + lax.broadcasted_iota(
        jnp.int32, regions.shape, 1
    )
    level_local = lax.broadcasted_iota(jnp.int32, regions.shape, 0)
    groups = (
        regions
        + 3 * (lat_global >= lat_total - WIN_LAT // 2).astype(jnp.int32)
        + 6 * (level_local >= LEVELS - 1).astype(jnp.int32)
    )
    bias = gather_bias(bias_table, bias_index, groups)
    core = (lax.axis_index("lon") % 2).astype(jnp.int32).reshape(1)
    gain = norm_gain[None]
    lat_back, lon_back, stay_back, keep, send = attention(
        core, stay, lon_half, lat_half, gain, heads_weight, mixing_weight, bias
    )
    lat_back = shifted(lat_back, "lat", 1)
    lon_back = shifted(jnp.stack([lon_back, lat_back[1]]), "lon", 1)
    rows = reduce_rows(keep, send).astype(F32) * factor
    latent_grad, merged = finish(
        x, u, stay_back, lat_back[0], lon_back, gain, merge_gain[None], whole_merge
    )
    merged = merged.reshape(level_count, lat_count // 2, lon_count // 2, -1)
    return merged, latent_grad.reshape(latent.shape), rows[:, : 3 * width], rows[:, 3 * width :]


def solution(mesh):
    placed = (
        P(None, "lat", "lon", None),
        P(None, "lat", "lon", None),
        P(),
        P(),
        P(),
        P(),
        P(None, "lat", None, None),
        P(None, "lat", "lon"),
        P(),
        P("lon", None),
    )
    return jax.shard_map(
        on_device,
        mesh=mesh,
        in_specs=placed,
        out_specs=(
            P(None, "lat", "lon", None),
            P(None, "lat", "lon", None),
            P("lon", None),
            P("lon", None),
        ),
        check_vma=False,
    )
```

time: 1050 us -> 178 us (0.17)
  the two profiles are of different devices: /device:TPU:2 before, /device:TPU:192 now
where the time goes in v1:
time: 178 us; the launch traced here: 177 us
  starting transfers between devices  62.4 us (35%)
  waiting for transfers between devices  50.4 us (28%)
  Pallas kernels  32.5 us (18%)
  between operations  14.4 us (8%)
  local copies, waits for them, and re-layouts  12.5 us (7%)
  other arithmetic  4.89 us (3%)
    all_to_all x3, starting transfers between devices, exchanged(): lax.all_to_all(array, axes, 0, 0, axis_index_groups=groups, tiled=True)  38 us
    ppermute x4, waiting for transfers between devices, shifted(): lax.ppermute(array, axis, [(i, (i + by) % size) for i in range(size)])  24.6 us
    all_to_all x3, waiting for transfers between devices, exchanged(): lax.all_to_all(array, axes, 0, 0, axis_index_groups=groups, tiled=True)  22.8 us
    ppermute x4, starting transfers between devices, shifted(): lax.ppermute(array, axis, [(i, (i + by) % size) for i in range(size)])  21.7 us
    pallas_call x1, Pallas kernels, gather_bias(): pl.pallas_call(bias_kernel, out_shape=jax.ShapeDtypeStruct((HEADS, TOK, T...  17.5 us
    pallas_call x1, Pallas kernels, attention(): pl.pallas_call(attention_kernel, out_shape=(jax.ShapeDtypeStruct((2, 2, P...  11.6 us
    unnamed x35, local copies, waits for them, and re-layouts  8.04 us
  transfers between devices with their start and end apart: 9, of which 6 were waited for; matrix products, arithmetic and copies ran while one was open for 8% of the time, Pallas kernels for 18%

profile of v1, /device:TPU:192, one launch (start us, length us, event | category | flops | bytes accessed | tf_op | source)
XLA Modules:
  0.0 177.1 jit_solution(16470507559580546994)
XLA Ops:
  7.9 0.9 copy.34
  9.6 0.9 copy.35
  11.2 2.1 %prepare.1 = (bf16[2,2,36,512]{3,2,1,0:T(8,128)(2,1)}, bf16[2,36,512]{2,1,0:T(8,128)(2,1)}, bf16[2,36,512]{2,1,0:T(8,128)(2,1)}) custom-call(bf16[144,512]{1,0:T(8,128)(2,1)} %reshape.51.x_ref, bf16[144,512]{1,0:T(8,128)(2,1)} %reshape.52.u_ref), custom_call_target="tpu_custom_call" | custom-call | tf_op jit(solution)/shard_map/prepare/pallas_call | solution.py:90
  13.3 13.2 %collective-permute-start = (bf16[2,2,36,512]{3,2,1,0:T(8,128)(2,1)}, bf16[2,2,36,512]{3,2,1,0:T(8,128)(2,1)S(1)}, u32[]{:S(2)}, u32[]{:S(2)}) collective-permute-start(bf16[2,2,36,512]{3,2,1,0:T(8,128)(2,1)} %get-tuple-element.15), channel_id=1, source_target_pairs={{0,63},{1,0},{2,1},{3,2},{4,3},{5,4},{6,5},{7,6},{8,7},{9,8},{10,9... | collective-permute-start | bytes 442376 | tf_op jit(solution)/shard_map/ppermute | solution.py:329
  26.5 4.9 %collective-permute-done.lon_ref = bf16[2,2,36,512]{3,2,1,0:T(8,128)(2,1)S(1)} collective-permute-done((bf16[2,2,36,512]{3,2,1,0:T(8,128)(2,1)}, bf16[2,2,36,512]{3,2,1,0:T(8,128)(2,1)S(1)}, u32[]{:S(2)}, u32[]{:S(2)}) %collective-permute-start) | collective-permute-done | bytes 147488 | tf_op jit(solution)/shard_map/ppermute | solution.py:329
  31.5 1.6 pad_maximum_fusion
  33.0 2.8 %collective-permute-start.1 = (bf16[2,2,36,512]{3,2,1,0:T(8,128)(2,1)}, bf16[2,2,36,512]{3,2,1,0:T(8,128)(2,1)}, u32[]{:S(2)}, u32[]{:S(2)}) collective-permute-start(bf16[2,2,36,512]{3,2,1,0:T(8,128)(2,1)} %pad_maximum_fusion), channel_id=1, source_target_pairs={{0,448},{64,0},{128,64},{192,128},{256,192},{320,256},{384,320},{4... | collective-permute-start | bytes 442376 | tf_op jit(solution)/shard_map/ppermute | solution.py:329
  37.0 1.0 pad.13.table_ref
  38.0 17.5 %bias_gather.1.bias_ref = f32[16,144,144]{2,1,0:T(8,128)S(1)} custom-call(s32[144,256]{1,0:T(8,128)S(1)} %pad.12.index_ref, f32[16,3328]{1,0:T(8,128)S(1)} %pad.13.table_ref, s32[144,128]{1,0:T(8,128)S(1)} %broadcast_in_dim.22.key_group_ref, s32[1,256]{1,0:T(1,128)S(1)} %bitcast.23), custom_call_target="tpu_custom_call" | custom-call | tf_op jit(solution)/shard_map/bias_gather/pallas_call | solution.py:138
  56.4 11.6 %window_attention.1 = (bf16[2,2,36,512]{3,2,1,0:T(8,128)(2,1)S(1)}, bf16[2,36,512]{2,1,0:T(8,128)(2,1)S(1)}, bf16[2,36,512]{2,1,0:T(8,128)(2,1)S(1)}, bf16[256,2048]{1,0:T(8,128)(2,1)S(1)}, bf16[256,2048]{1,0:T(8,128)(2,1)S(1)}) custom-call(s32[1]{0:T(128)} %bitcast.core_ref, bf16[2,36,512]{2,1,0:T(8,128)(2,1)S(1)} %copy-done.5, ...), custom_call_target="tpu_custom_call" | custom-call | tf_op jit(solution)/shard_map/window_attention/pallas_call | solution.py:249
  68.1 2.7 %collective-permute-start.4 = (bf16[256,2048]{1,0:T(8,128)(2,1)S(1)}, bf16[256,2048]{1,0:T(8,128)(2,1)S(1)}, u32[]{:S(2)}, u32[]{:S(2)}) collective-permute-start(bf16[256,2048]{1,0:T(8,128)(2,1)S(1)} %get-tuple-element.23), channel_id=1, source_target_pairs={{0,1},{1,0},{2,3},{3,2},{4,5},{5,4},{6,7},{7,6},{8,9},{9,8},{10,11... | collective-permute-start | bytes 3145736 | tf_op jit(solution)/shard_map/ppermute | solution.py:339
  70.8 2.3 %collective-permute-done.4 = bf16[256,2048]{1,0:T(8,128)(2,1)S(1)} collective-permute-done((bf16[256,2048]{1,0:T(8,128)(2,1)S(1)}, bf16[256,2048]{1,0:T(8,128)(2,1)S(1)}, u32[]{:S(2)}, u32[]{:S(2)}) %collective-permute-start.4) | collective-permute-done | bytes 1048608 | tf_op jit(solution)/shard_map/ppermute | solution.py:339
  73.1 1.4 add_convert_fusion
  74.5 7.0 %all-to-all-start = ((bf16[16,16,2048]{2,1,0:T(8,128)(2,1)}), bf16[16,16,2048]{2,1,0:T(8,128)(2,1)S(1)}, u32[]{:S(2)}, u32[]{:S(2)}) async-start(bf16[16,16,2048]{2,1,0:T(8,128)(2,1)} %bitcast.11), calls=%async_computation | async-start | bytes 2097152 | tf_op jit(solution)/shard_map/all_to_all | solution.py:333
  81.5 3.8 %collective-permute-start.2 = (bf16[2,2,36,512]{3,2,1,0:T(8,128)(2,1)S(1)}, bf16[2,2,36,512]{3,2,1,0:T(8,128)(2,1)S(1)}, u32[]{:S(2)}, u32[]{:S(2)}) collective-permute-start(bf16[2,2,36,512]{3,2,1,0:T(8,128)(2,1)S(1)} %copy-done.9), channel_id=1, source_target_pairs={{0,64},{64,128},{128,192},{192,256},{256,320},{320,384},{384,448},... | collective-permute-start | bytes 442376 | tf_op jit(solution)/shard_map/ppermute | solution.py:329
  85.3 14.8 %all-to-all-done = bf16[16,16,2048]{2,1,0:T(8,128)(2,1)S(1)} async-done(((bf16[16,16,2048]{2,1,0:T(8,128)(2,1)}), bf16[16,16,2048]{2,1,0:T(8,128)(2,1)S(1)}, u32[]{:S(2)}, u32[]{:S(2)}) %all-to-all-start) | async-done | bytes 1048608 | tf_op jit(solution)/shard_map/all_to_all | solution.py:333
  102.1 21.5 %all-to-all-start.1 = ((bf16[16,2,1024]{2,1,0:T(2,128)(2,1)}), bf16[16,2,1024]{2,1,0:T(2,128)(2,1)S(1)}, u32[]{:S(2)}, u32[]{:S(2)}) async-start(bf16[16,2,1024]{2,1,0:T(2,128)(2,1)} %reshape.58), calls=%async_computation.1 | async-start | bytes 131072 | tf_op jit(solution)/shard_map/all_to_all | solution.py:333
  123.7 6.7 %all-to-all-done.1 = bf16[16,2,1024]{2,1,0:T(2,128)(2,1)S(1)} async-done(((bf16[16,2,1024]{2,1,0:T(2,128)(2,1)}), bf16[16,2,1024]{2,1,0:T(2,128)(2,1)S(1)}, u32[]{:S(2)}, u32[]{:S(2)}) %all-to-all-start.1) | async-done | bytes 65568 | tf_op jit(solution)/shard_map/all_to_all | solution.py:333
  132.0 9.4 %all-to-all-start.2 = ((bf16[8,2,1024]{2,1,0:T(2,128)(2,1)}), bf16[8,2,1024]{2,1,0:T(2,128)(2,1)S(1)}, u32[]{:S(2)}, u32[]{:S(2)}) async-start(bf16[8,2,1024]{2,1,0:T(2,128)(2,1)} %reshape.60), calls=%async_computation.2 | async-start | bytes 65536 | tf_op jit(solution)/shard_map/all_to_all | solution.py:333
  141.5 1.9 %collective-permute-start.3 = (bf16[2,2,36,512]{3,2,1,0:T(8,128)(2,1)S(1)}, bf16[2,2,36,512]{3,2,1,0:T(8,128)(2,1)S(1)}, u32[]{:S(2)}, u32[]{:S(2)}) collective-permute-start(bf16[2,2,36,512]{3,2,1,0:T(8,128)(2,1)S(1)} %pad_maximum_fusion.1), channel_id=1, source_target_pairs={{0,1},{1,2},{2,3},{3,4},{4,5},{5,6},{6,7},{7,8},{8,9},{9,10},{10,1... | collective-permute-start | bytes 442376 | tf_op jit(solution)/shard_map/ppermute | solution.py:329
  143.4 1.3 all-to-all-done.2
  146.1 19.7 %collective-permute-done.3.lon_ref = bf16[2,2,36,512]{3,2,1,0:T(8,128)(2,1)S(1)} collective-permute-done((bf16[2,2,36,512]{3,2,1,0:T(8,128)(2,1)S(1)}, bf16[2,2,36,512]{3,2,1,0:T(8,128)(2,1)S(1)}, u32[]{:S(2)}, u32[]{:S(2)}) %collective-permute-start.3) | collective-permute-done | bytes 147488 | tf_op jit(solution)/shard_map/ppermute | solution.py:329
  165.8 1.6 copy-done.1
  167.4 1.3 finish.1
  (61 shorter events, 10.7 us)
Async XLA Ops:
  7.2 28.7 %copy-start.11 = (s32[2,6,12]{2,0,1:T(2,128)S(1)}, s32[2,6,12]{2,0,1:T(2,128)}, u32[]{:S(2)}) copy-start(s32[2,6,12]{2,0,1:T(2,128)} %param.17) | copy-start | bytes 1732
  7.2 28.9 %copy-start.10 = (s32[1,1,144,144]{3,2,1,0:T(8,128)S(1)}, s32[1,1,144,144]{3,2,1,0:T(8,128)}, u32[]{:S(2)}) copy-start(s32[1,1,144,144]{3,2,1,0:T(8,128)} %param.16) | copy-start | bytes 248836
  7.2 29.0 %copy-start = (bf16[512,1536]{1,0:T(8,128)(2,1)S(1)}, bf16[512,1536]{1,0:T(8,128)(2,1)}, u32[]{:S(2)}) copy-start(bf16[512,1536]{1,0:T(8,128)(2,1)} %w_ref.1) | copy-start | bytes 4718596
  7.2 158.6 %all-gather.2.cloned.1.call-start = ((), (), s32[]{:S(2)}) async-start(), calls=%async_computation.3 | async-start | bytes 2129920 | tf_op jit(solution)/shard_map/all_gather | solution.py:373
  13.3 18.2 %collective-permute-start = (bf16[2,2,36,512]{3,2,1,0:T(8,128)(2,1)}, bf16[2,2,36,512]{3,2,1,0:T(8,128)(2,1)S(1)}, u32[]{:S(2)}, u32[]{:S(2)}) collective-permute-start(bf16[2,2,36,512]{3,2,1,0:T(8,128)(2,1)} %get-tuple-element.15), channel_id=1, source_target_pairs={{0,63},{1,0},{2,1},{3,2},{4,3},{5,4},{6,5},{7,6},{8,7},{9,8},{10,9... | collective-permute-start | bytes 442376 | tf_op jit(solution)/shard_map/ppermute | solution.py:329
  33.0 22.5 %collective-permute-start.1 = (bf16[2,2,36,512]{3,2,1,0:T(8,128)(2,1)}, bf16[2,2,36,512]{3,2,1,0:T(8,128)(2,1)}, u32[]{:S(2)}, u32[]{:S(2)}) collective-permute-start(bf16[2,2,36,512]{3,2,1,0:T(8,128)(2,1)} %pad_maximum_fusion), channel_id=1, source_target_pairs={{0,448},{64,0},{128,64},{192,128},{256,192},{320,256},{384,320},{4... | collective-permute-start | bytes 442376 | tf_op jit(solution)/shard_map/ppermute | solution.py:329
  36.9 18.6 %copy-start.7 = (f32[512]{0:T(512)S(1)}, f32[512]{0:T(512)}, u32[]{:S(2)}) copy-start(f32[512]{0:T(512)} %param.12) | copy-start | bytes 6148
  36.9 18.6 %copy-start.4 = (bf16[512,512]{1,0:T(8,128)(2,1)S(1)}, bf16[512,512]{1,0:T(8,128)(2,1)}, u32[]{:S(2)}) copy-start(bf16[512,512]{1,0:T(8,128)(2,1)} %m_ref.1) | copy-start | bytes 1572868
  55.5 0.9 copy-start.5
  68.1 6.4 %copy-start.8 = (bf16[2,2,36,512]{3,2,1,0:T(8,128)(2,1)}, bf16[2,2,36,512]{3,2,1,0:T(8,128)(2,1)S(1)}, u32[]{:S(2)}) copy-start(bf16[2,2,36,512]{3,2,1,0:T(8,128)(2,1)S(1)} %get-tuple-element.18) | copy-start | bytes 442372
  68.1 5.0 %collective-permute-start.4 = (bf16[256,2048]{1,0:T(8,128)(2,1)S(1)}, bf16[256,2048]{1,0:T(8,128)(2,1)S(1)}, u32[]{:S(2)}, u32[]{:S(2)}) collective-permute-start(bf16[256,2048]{1,0:T(8,128)(2,1)S(1)} %get-tuple-element.23), channel_id=1, source_target_pairs={{0,1},{1,0},{2,3},{3,2},{4,5},{5,4},{6,7},{7,6},{8,9},{9,8},{10,11... | collective-permute-start | bytes 3145736 | tf_op jit(solution)/shard_map/ppermute | solution.py:339
  74.5 7.1 %copy-start.9 = (bf16[2,2,36,512]{3,2,1,0:T(8,128)(2,1)S(1)}, bf16[2,2,36,512]{3,2,1,0:T(8,128)(2,1)}, u32[]{:S(2)}) copy-start(bf16[2,2,36,512]{3,2,1,0:T(8,128)(2,1)} %copy-done.8) | copy-start | bytes 442372
  74.5 25.7 %all-to-all-start = ((bf16[16,16,2048]{2,1,0:T(8,128)(2,1)}), bf16[16,16,2048]{2,1,0:T(8,128)(2,1)S(1)}, u32[]{:S(2)}, u32[]{:S(2)}) async-start(bf16[16,16,2048]{2,1,0:T(8,128)(2,1)} %bitcast.11), calls=%async_computation | async-start | bytes 2097152 | tf_op jit(solution)/shard_map/all_to_all | solution.py:333
  81.5 84.3 %copy-start.2 = (bf16[144,512]{1,0:T(8,128)(2,1)S(1)}, bf16[144,512]{1,0:T(8,128)(2,1)}, u32[]{:S(2)}) copy-start(bf16[144,512]{1,0:T(8,128)(2,1)} %reshape.51.x_ref) | copy-start | bytes 442372
  81.5 84.3 %copy-start.3 = (bf16[144,512]{1,0:T(8,128)(2,1)S(1)}, bf16[144,512]{1,0:T(8,128)(2,1)}, u32[]{:S(2)}) copy-start(bf16[144,512]{1,0:T(8,128)(2,1)} %reshape.52.u_ref) | copy-start | bytes 442372
  81.5 84.3 %copy-start.6 = (f32[2048]{0:T(1024)S(1)}, f32[2048]{0:T(1024)}, u32[]{:S(2)}) copy-start(f32[2048]{0:T(1024)} %param.18) | copy-start | bytes 24580
  81.5 42.1 %collective-permute-start.2 = (bf16[2,2,36,512]{3,2,1,0:T(8,128)(2,1)S(1)}, bf16[2,2,36,512]{3,2,1,0:T(8,128)(2,1)S(1)}, u32[]{:S(2)}, u32[]{:S(2)}) collective-permute-start(bf16[2,2,36,512]{3,2,1,0:T(8,128)(2,1)S(1)} %copy-done.9), channel_id=1, source_target_pairs={{0,64},{64,128},{128,192},{192,256},{256,320},{320,384},{384,448},... | collective-permute-start | bytes 442376 | tf_op jit(solution)/shard_map/ppermute | solution.py:329
  102.1 28.2 %all-to-all-start.1 = ((bf16[16,2,1024]{2,1,0:T(2,128)(2,1)}), bf16[16,2,1024]{2,1,0:T(2,128)(2,1)S(1)}, u32[]{:S(2)}, u32[]{:S(2)}) async-start(bf16[16,2,1024]{2,1,0:T(2,128)(2,1)} %reshape.58), calls=%async_computation.1 | async-start | bytes 131072 | tf_op jit(solution)/shard_map/all_to_all | solution.py:333
  132.0 12.7 %all-to-all-start.2 = ((bf16[8,2,1024]{2,1,0:T(2,128)(2,1)}), bf16[8,2,1024]{2,1,0:T(2,128)(2,1)S(1)}, u32[]{:S(2)}, u32[]{:S(2)}) async-start(bf16[8,2,1024]{2,1,0:T(2,128)(2,1)} %reshape.60), calls=%async_computation.2 | async-start | bytes 65536 | tf_op jit(solution)/shard_map/all_to_all | solution.py:333
  141.5 24.4 %collective-permute-start.3 = (bf16[2,2,36,512]{3,2,1,0:T(8,128)(2,1)S(1)}, bf16[2,2,36,512]{3,2,1,0:T(8,128)(2,1)S(1)}, u32[]{:S(2)}, u32[]{:S(2)}) collective-permute-start(bf16[2,2,36,512]{3,2,1,0:T(8,128)(2,1)S(1)} %pad_maximum_fusion.1), channel_id=1, source_target_pairs={{0,1},{1,2},{2,3},{3,4},{4,5},{5,6},{6,7},{7,8},{8,9},{9,10},{10,1... | collective-permute-start | bytes 442376 | tf_op jit(solution)/shard_map/ppermute | solution.py:329
  165.8 1.6 copy-start.1
Sparse Core Ops, SparseCore 0:
  12.4 109.2 all-gather.1

commit v2 on v1

v2 whole, which is shorter than its diff:
```python
import functools

import jax
import jax.numpy as jnp
from jax import lax
from jax.experimental import pallas as pl
from jax.experimental.pallas import tpu as pltpu
from jax.sharding import PartitionSpec as P

HEADS = 16
HEAD_DIM = 32
LEVELS = 2
WIN_LAT = 6
WIN_LON = 12
TOK = 144
PART = 36
SLOT = 40
EPSILON = 1e-05
MASKED = -1e30
F32, BF16 = jnp.float32, jnp.bfloat16
VMEM = pl.BlockSpec(memory_space=pltpu.VMEM)
SMEM = pl.BlockSpec(memory_space=pltpu.SMEM)


def nn(a, b):
    return lax.dot_general(a, b, (((1,), (0,)), ((), ())), preferred_element_type=F32)


def nt(a, b):
    return lax.dot_general(a, b, (((1,), (1,)), ((), ())), preferred_element_type=F32)


def layer_norm(values):
    average = jnp.mean(values, axis=-1, keepdims=True)
    centred = values - average
    variance = jnp.mean(centred * centred, axis=-1, keepdims=True)
    inverse = lax.rsqrt(variance + EPSILON)
    return centred * inverse, inverse


def one_hot(source, old):
    return jnp.where(source == old, 1.0, 0.0).astype(BF16)


def cell_of_slot(row, level_swap):
    quarter, cell = row // SLOT, row % SLOT
    level, rest = cell // 18, cell % 18
    lat = 3 * (quarter // 2) + rest // 6
    lon = 6 * (quarter % 2) + rest % 6
    if level_swap:
        level = 1 - level
    return jnp.where(cell < PART, level * 72 + lat * 12 + lon, -1)


def slots_from_cells(level_swap=False):
    row = lax.broadcasted_iota(jnp.int32, (4 * SLOT, TOK), 0)
    column = lax.broadcasted_iota(jnp.int32, (4 * SLOT, TOK), 1)
    return one_hot(cell_of_slot(row, level_swap), column)


def cells_from_slots(level_swap=False):
    row = lax.broadcasted_iota(jnp.int32, (TOK, 4 * SLOT), 0)
    column = lax.broadcasted_iota(jnp.int32, (TOK, 4 * SLOT), 1)
    return one_hot(cell_of_slot(column, level_swap), row)


def quarters_of(values):
    return [values[SLOT * q : SLOT * q + SLOT] for q in range(4)]


def stacked(pieces):
    return jnp.concatenate(pieces, axis=0).astype(BF16)


def row_of_place(place):
    level, rest = place // (TOK // 2), place % (TOK // 2)
    return jnp.where(place < 0, -1, 2 * rest + level)


def prepare_kernel(x_ref, u_ref, lon_ref, lat_ref, stay_ref):
    row = lax.broadcasted_iota(jnp.int32, (4 * SLOT, TOK), 0)
    column = lax.broadcasted_iota(jnp.int32, (4 * SLOT, TOK), 1)
    order = one_hot(row_of_place(cell_of_slot(row, True)), column)
    x = quarters_of(nn(order, x_ref[...]))
    u = quarters_of(nn(order, u_ref[...]))
    lon_ref[...] = stacked([x[0], u[0], x[2], u[2]])
    lat_ref[...] = stacked([x[1], u[1]])
    stay_ref[...] = stacked([x[3], u[3]])


def prepare(x, u):
    width = x.shape[-1]
    return pl.pallas_call(
        prepare_kernel,
        out_shape=(
            jax.ShapeDtypeStruct((4 * SLOT, width), BF16),
            jax.ShapeDtypeStruct((2 * SLOT, width), BF16),
            jax.ShapeDtypeStruct((2 * SLOT, width), BF16),
        ),
        in_specs=[VMEM] * 2,
        out_specs=(VMEM,) * 3,
        name="prepare",
    )(x, u)


def lookup(index, table_ref):
    high, low = index >> 7, index & 127
    found = [jnp.zeros(index.shape, F32) for _ in range(HEADS)]
    for chunk in range(table_ref.shape[1] // 128):
        here = high == chunk
        for head in range(HEADS):
            row = table_ref[head : head + 1, chunk * 128 : chunk * 128 + 128]
            row = jnp.broadcast_to(row, index.shape)
            value = jnp.take_along_axis(row, low, axis=1, mode="promise_in_bounds")
            found[head] = jnp.where(here, value, found[head])
    return found


def bias_kernel(index_ref, table_ref, key_group_ref, query_group_ref, bias_ref, tail_ref):
    rest = TOK - 128
    per_row = 128 // rest

    def allowed(base, start):
        return key_group_ref[pl.ds(base, 8), :] == query_group_ref[:, start : start + 128]

    def main_rows(step, carry):
        base = pl.multiple_of(step * 8, 8)
        open_pairs = allowed(base, 0)
        for head, value in enumerate(lookup(index_ref[pl.ds(base, 8), :], table_ref)):
            bias_ref[head, pl.ds(base, 8), :128] = jnp.where(open_pairs, value, MASKED)
        return carry

    def tail_rows(step, carry):
        base = pl.multiple_of(step * 8, 8)
        for head, value in enumerate(lookup(index_ref[pl.ds(TOK + base, 8), :], table_ref)):
            tail_ref[head, pl.ds(base, 8), :] = value
        return carry

    def spread_rows(step, carry):
        base = pl.multiple_of(step * 8, 8)
        open_pairs = allowed(base, 128)
        sublane = lax.broadcasted_iota(jnp.int32, (8, 128), 0)
        lane = lax.broadcasted_iota(jnp.int32, (8, 128), 1)
        place = sublane * rest + (lane & (rest - 1))
        for head in range(HEADS):
            row = jnp.broadcast_to(tail_ref[head, pl.ds(step, 1), :], (8, 128))
            value = jnp.take_along_axis(row, place, axis=1, mode="promise_in_bounds")
            value = jnp.where(open_pairs, value, MASKED)
            bias_ref[head, pl.ds(base, 8), 128:] = value[:, :rest]
        return carry

    lax.fori_loop(0, TOK // 8, main_rows, 0)
    lax.fori_loop(0, tail_ref.shape[1] // 8, tail_rows, 0)
    lax.fori_loop(0, TOK // per_row, spread_rows, 0)


def bias_operands(bias_table, bias_index, groups):
    rows = bias_table.shape[0]
    padded = -(-rows // 128) * 128
    table = jnp.pad(bias_table.T, ((0, 0), (0, padded - rows)))
    index = bias_index.reshape(TOK, TOK).T
    tail = index[:, 128:].reshape(-1, 128)
    tail = jnp.pad(tail, ((0, -tail.shape[0] % 8), (0, 0)))
    index = jnp.concatenate([index[:, :128], tail])
    flat = groups.reshape(TOK)
    key_group = jnp.broadcast_to(flat[:, None], (TOK, 128))
    query_group = jnp.pad(flat, (0, 256 - TOK))[None]
    return index, table, key_group, query_group


def gather_bias(operands):
    tail = operands[0].shape[0] - TOK
    return pl.pallas_call(
        bias_kernel,
        out_shape=jax.ShapeDtypeStruct((HEADS, TOK, TOK), F32),
        in_specs=[VMEM] * 4,
        out_specs=VMEM,
        scratch_shapes=[pltpu.VMEM((HEADS, tail, 128), F32)],
        compiler_params=pltpu.CompilerParams(vmem_limit_bytes=12 * 1024 * 1024),
        name="bias_gather",
    )(*operands)


def attention_kernel(
    core_ref,
    stay_ref,
    lon_ref,
    lat_ref,
    gain_ref,
    w_ref,
    m_ref,
    bias_ref,
    lat_out_ref,
    lon_out_ref,
    stay_out_ref,
    keep_ref,
    send_ref,
    ct_ref,
    dqt_ref,
    tg_ref,
):
    width = gain_ref.shape[1]
    scale = HEAD_DIM ** (-0.5)
    core = core_ref[0]
    gather = cells_from_slots()
    stay, lon, lat = (r[...].astype(F32) for r in (stay_ref, lon_ref, lat_ref))
    arrays = []
    for array in range(2):
        at = slice(SLOT * array, SLOT * array + SLOT)
        later = slice(SLOT * array + 2 * SLOT, SLOT * array + 3 * SLOT)
        slots = stacked([stay[at], lon[later], lat[at], lat[later]])
        arrays.append(nn(gather, slots).astype(BF16))
    x, u = arrays
    standard, _ = layer_norm(x.astype(F32))
    xn = (standard * gain_ref[...]).astype(BF16)
    w = w_ref[...]
    m = m_ref[...]
    q_nat = nn(xn, w[:, :width]).astype(BF16)
    k_nat = nn(xn, w[:, width : 2 * width]).astype(BF16)
    v_nat = nn(xn, w[:, 2 * width :]).astype(BF16)
    row = lax.broadcasted_iota(jnp.int32, (width, width), 0)
    column = lax.broadcasted_iota(jnp.int32, (width, width), 1)
    wide_eye = one_hot(row, column)
    qt, kt, vt = (nt(wide_eye, block).astype(BF16) for block in (q_nat, k_nat, v_nat))
    cg_nat = nt(u, m).astype(BF16)
    cgt = nt(m, u).astype(BF16)
    lane = lax.broadcasted_iota(jnp.int32, (TOK, 128), 1)
    for group in range(HEADS // 4):
        cut = slice(128 * group, 128 * group + 128)
        kg, vg, qg, cgg = k_nat[:, cut], v_nat[:, cut], q_nat[:, cut], cg_nat[:, cut]
        qtg, cgtg = qt[cut], cgt[cut]
        dk = jnp.zeros((TOK, 128), F32)
        dv = jnp.zeros((TOK, 128), F32)
        for part in range(4):
            head = 4 * group + part
            own = (lane >= HEAD_DIM * part) & (lane < HEAD_DIM * (part + 1))

            def only(block):
                return jnp.where(own, block.astype(F32), 0.0).astype(BF16)

            at = slice(HEAD_DIM * head, HEAD_DIM * head + HEAD_DIM)
            logits = nn(only(kg), qtg) * scale + bias_ref[head]
            top = jnp.max(logits, axis=0, keepdims=True)
            raised = jnp.exp(logits - top)
            shares = raised * (1.0 / jnp.sum(raised, axis=0, keepdims=True))
            shares_low = shares.astype(BF16)
            ct_ref[at, :] = nn(vt[at], shares_low).astype(BF16)
            share_grad = nn(only(vg), cgtg)
            product = shares * share_grad
            total = jnp.sum(product, axis=0, keepdims=True)
            logit_grad = (shares * (share_grad - total)).astype(BF16)
            dqt_ref[at, :] = (nn(kt[at], logit_grad) * scale).astype(BF16)
            dv = dv + nn(shares_low, only(cgg))
            dk = dk + nn(logit_grad, only(qg))
        tg_ref[:, width + 128 * group : width + 128 * group + 128] = (dk * scale).astype(BF16)
        tg_ref[:, 2 * width + 128 * group : 2 * width + 128 * group + 128] = dv.astype(BF16)
    row = lax.broadcasted_iota(jnp.int32, (TOK, TOK), 0)
    column = lax.broadcasted_iota(jnp.int32, (TOK, TOK), 1)
    eye = one_hot(row, column)
    tg_ref[:, :width] = nt(eye, dqt_ref[...]).astype(BF16)
    ct = ct_ref[...]
    context = nt(eye, ct).astype(BF16)
    tg = tg_ref[...]
    spread = slots_from_cells()
    back = [quarters_of(nn(spread, v.astype(BF16))) for v in (nn(context, m), nt(tg, w))]
    stay_out_ref[...] = stacked([back[0][0], back[1][0]])
    lon_out_ref[...] = stacked([back[0][1], back[1][1], back[0][3], back[1][3]])
    lat_out_ref[...] = stacked([back[0][2], back[1][2]])
    half = width // 2
    new = lax.broadcasted_iota(jnp.int32, (width, width), 0)
    old = lax.broadcasted_iota(jnp.int32, (width, width), 1)
    local = new & (half - 1)
    parity = jnp.where(new >= half, 1 - core, core)
    order = one_hot(((local >> 3) << 4) + (parity << 3) + (local & 7), old)
    xnt = nt(order, xn).astype(BF16)
    cto = nn(order, ct).astype(BF16)
    for rows, target in ((slice(0, half), keep_ref), (slice(half, width), send_ref)):
        target[:, : 3 * width] = nn(xnt[rows], tg).astype(BF16)
        target[:, 3 * width :] = nn(cto[rows], u).astype(BF16)


def attention(core, stay, lon, lat, gain, w, m, bias):
    width = gain.shape[1]
    return pl.pallas_call(
        attention_kernel,
        out_shape=(
            jax.ShapeDtypeStruct((2 * SLOT, width), BF16),
            jax.ShapeDtypeStruct((4 * SLOT, width), BF16),
            jax.ShapeDtypeStruct((2 * SLOT, width), BF16),
            jax.ShapeDtypeStruct((width // 2, 4 * width), BF16),
            jax.ShapeDtypeStruct((width // 2, 4 * width), BF16),
        ),
        in_specs=[SMEM] + [VMEM] * 7,
        out_specs=(VMEM,) * 5,
        scratch_shapes=[
            pltpu.VMEM((width, TOK), BF16),
            pltpu.VMEM((width, TOK), BF16),
            pltpu.VMEM((TOK, 3 * width), BF16),
        ],
        compiler_params=pltpu.CompilerParams(vmem_limit_bytes=56 * 1024 * 1024),
        name="window_attention",
    )(core, stay, lon, lat, gain, w, m, bias)


def finish_kernel(
    place_ref,
    x_ref,
    u_ref,
    stay_ref,
    lat_ref,
    lon_ref,
    gain_ref,
    merge_gain_ref,
    own_weight_ref,
    other_weight_ref,
    grad_ref,
    merged_ref,
):
    width = x_ref.shape[-1]
    x = x_ref[...].astype(F32)
    row = lax.broadcasted_iota(jnp.int32, (TOK, 4 * SLOT), 0)
    column = lax.broadcasted_iota(jnp.int32, (TOK, 4 * SLOT), 1)
    gather = one_hot(row_of_place(cell_of_slot(column, True)), row)
    stay, lon, lat = (r[...].astype(F32) for r in (stay_ref, lon_ref, lat_ref))
    arrays = []
    for array in range(2):
        at = slice(SLOT * array, SLOT * array + SLOT)
        later = slice(SLOT * array + 2 * SLOT, SLOT * array + 3 * SLOT)
        arrays.append(nn(gather, stacked([lat[later], lat[at], lon[at], stay[at]])))
    normalized, inverse = layer_norm(x)
    scaled = arrays[1] * gain_ref[...]
    first = jnp.mean(scaled, axis=-1, keepdims=True)
    second = jnp.mean(scaled * normalized, axis=-1, keepdims=True)
    back = inverse * (scaled - first - normalized * second)
    block = (x + arrays[0]).astype(BF16)
    grad_ref[...] = (u_ref[...].astype(F32) + back).astype(BF16)
    new = lax.broadcasted_iota(jnp.int32, (width, width), 1)
    old = lax.broadcasted_iota(jnp.int32, (width, width), 0)
    half = width // 2
    odd = (new >= half).astype(jnp.int32)
    local = new & (half - 1)
    block = nn(block, one_hot(((local >> 6) << 7) + (odd << 6) + (local & 63), old)).astype(BF16)
    row = lax.broadcasted_iota(jnp.int32, (4 * SLOT, TOK), 0)
    column = lax.broadcasted_iota(jnp.int32, (4 * SLOT, TOK), 1)
    corner, cell = row // SLOT, row % SLOT
    pair, level = cell // 2, cell % 2
    lat_at, lon_at = 2 * (pair // 6) + corner % 2, 2 * (pair % 6) + corner // 2
    place = (lat_at * WIN_LON + lon_at) * 2 + level
    corners = quarters_of(nn(one_hot(jnp.where(cell < PART, place, -1), column), block))
    joined = jnp.concatenate([c[:, :half] for c in corners] + [c[:, half:] for c in corners], axis=-1)
    features, _ = layer_norm(joined)
    features = features * merge_gain_ref[...]
    even, odds = features[:, : 2 * width], features[:, 2 * width :]
    moved = jnp.concatenate([even[:, 64:], even[:, :64]], axis=-1)

    def blocks(start):
        return jnp.where(start == 0, even, jnp.where(start == 1, odds, moved)).astype(BF16)

    core, high = place_ref[0], place_ref[1]
    merged = nn(blocks(high + core), own_weight_ref[...])
    merged = merged + nn(blocks(high + 1 - core), other_weight_ref[...])
    merged_ref[...] = merged[:PART].astype(BF16)


def finish(place, x, u, stay, lat, lon, gain, merge_gain, own_weight, other_weight):
    width = x.shape[1]
    merge_gain = merge_gain.reshape(4, width // 128, 2, 64).transpose(2, 0, 1, 3).reshape(1, -1)
    return pl.pallas_call(
        finish_kernel,
        out_shape=(
            jax.ShapeDtypeStruct(x.shape, BF16),
            jax.ShapeDtypeStruct((PART, own_weight.shape[1]), BF16),
        ),
        in_specs=[SMEM] + [VMEM] * 9,
        out_specs=(VMEM,) * 2,
        compiler_params=pltpu.CompilerParams(vmem_limit_bytes=16 * 1024 * 1024),
        name="finish",
    )(place, x, u, stay, lat, lon, gain, merge_gain, own_weight, other_weight)


def shifted(array, axis, by):
    size = lax.axis_size(axis)
    return lax.ppermute(array, axis, [(i, (i + by) % size) for i in range(size)])


def exchanged(array, axes, groups):
    return lax.all_to_all(array, axes, 0, 0, axis_index_groups=groups, tiled=True)


def plane_groups(lon_size):
    return [[4 * j + r for j in range(lon_size // 4)] for r in range(4)]


def reduce_over_planes(paired):
    lon_size = lax.axis_size("lon")
    terms = exchanged(paired, "lon", plane_groups(lon_size))
    return terms.reshape(lon_size // 4, 2, -1, paired.shape[1])


def reduce_along_z(terms):
    lon_size, lat_size = lax.axis_size("lon"), lax.axis_size("lat")
    _, _, rows, columns = terms.shape
    planes = jnp.sum(terms.astype(F32), axis=0).astype(BF16)
    planes = planes.reshape(2, rows, lat_size, columns // lat_size).transpose(0, 2, 1, 3)
    planes = planes.reshape(2 * lat_size, rows, columns // lat_size)
    groups = [
        [level * lon_size + o + 2 * high for high in range(2) for level in range(lat_size)]
        for o in range(lon_size)
        if not o & 2
    ]
    terms = exchanged(planes, ("lat", "lon"), groups)
    return jnp.sum(terms.astype(F32), axis=0).astype(BF16)


def spread_over_lat(part):
    lat_size, rows = lax.axis_size("lat"), part.shape[0]
    parts = exchanged(jnp.broadcast_to(part[None], (lat_size,) + part.shape), "lat", None)
    return parts.transpose(1, 0, 2).reshape(rows, -1)


def on_device(
    latent,
    upstream,
    norm_gain,
    heads_weight,
    mixing_weight,
    bias_table,
    bias_index,
    regions,
    merge_gain,
    merge_weight,
):
    level_count, lat_count, lon_count, width = latent.shape
    lat_total = lat_count * lax.axis_size("lat")
    token_total = level_count * lat_total * lon_count * lax.axis_size("lon")
    factor = float(token_total) ** (-0.5)
    lon_size = lax.axis_size("lon")
    lon_at = lax.axis_index("lon")
    core = (lon_at % 2).astype(jnp.int32)
    high = (lon_at // 2 % 2).astype(jnp.int32)
    first_core = core == 0
    between_cores = [(i, i ^ 1) for i in range(lon_size)]
    to_chip = [(i, (i - 1) % lon_size) for i in range(0, lon_size, 2)]
    to_core = [(i, i - 1) for i in range(1, lon_size, 2)]
    x = latent.transpose(1, 2, 0, 3).reshape(TOK, width)
    u = upstream.transpose(1, 2, 0, 3).reshape(TOK, width)
    lon_half, lat_half, stay = prepare(x, u)
    lat_global = lax.axis_index("lat") * lat_count + lax.broadcasted_iota(
        jnp.int32, regions.shape, 1
    )
    level_local = lax.broadcasted_iota(jnp.int32, regions.shape, 0)
    groups = (
        regions
        + 3 * (lat_global >= lat_total - WIN_LAT // 2).astype(jnp.int32)
        + 6 * (level_local >= LEVELS - 1).astype(jnp.int32)
    )
    operands = bias_operands(bias_table, bias_index, groups)
    with jax.named_scope("weight_core"):
        other = lax.ppermute(merge_weight, "lon", between_cores)
    pair = jnp.concatenate(
        [jnp.where(first_core, merge_weight, other), jnp.where(first_core, other, merge_weight)]
    )
    with jax.named_scope("lon_core"):
        from_core = lax.ppermute(lon_half, "lon", to_core)
    with jax.named_scope("lon_cross"):
        from_chip = lax.ppermute(jnp.concatenate([lon_half, pair]), "lon", to_chip)
    bias = gather_bias(operands)
    half_rows = lon_half.shape[0]
    lon_half = jnp.where(first_core, from_core, from_chip[:half_rows])
    pair = jnp.where(first_core, pair, from_chip[half_rows:])
    lat_half = jnp.concatenate([lat_half, lon_half[: 2 * SLOT]])
    lat_half, pair, bias = lax.optimization_barrier((lat_half, pair, bias))
    with jax.named_scope("lat_roll"):
        lat_half = shifted(lat_half, "lat", -1)
    pair = jnp.broadcast_to(pair[None], (lon_size // 4,) + pair.shape).reshape(-1, width)
    with jax.named_scope("weight_plane"):
        own_weight = exchanged(pair, "lon", plane_groups(lon_size))
    gain = norm_gain[None]
    lat_back, lon_back, stay_back, keep, send = attention(
        core.reshape(1), stay, lon_half, lat_half, gain, heads_weight, mixing_weight, bias
    )
    send, own_weight = lax.optimization_barrier((send, own_weight))
    with jax.named_scope("term_core"):
        arrived = lax.ppermute(send, "lon", between_cores)
    with jax.named_scope("weight_other"):
        other_weight = lax.ppermute(own_weight, "lon", between_cores)
    paired = (keep.astype(F32) + arrived.astype(F32)).astype(BF16)
    with jax.named_scope("term_plane"):
        terms = reduce_over_planes(paired)
    with jax.named_scope("lon_back"):
        lon_back = shifted(lon_back, "lon", 1)
    with jax.named_scope("lat_back"):
        lat_back = shifted(jnp.concatenate([lat_back, lon_back[2 * SLOT :]]), "lat", 1)
    latent_grad, merged = finish(
        jnp.stack([core, high]),
        x,
        u,
        stay_back,
        lat_back,
        lon_back[: 2 * SLOT],
        gain,
        merge_gain,
        own_weight,
        other_weight,
    )
    with jax.named_scope("term_z"):
        part = reduce_along_z(terms)
    with jax.named_scope("term_lat"):
        rows = spread_over_lat(part).astype(F32) * factor
    merged = merged.reshape(lat_count // 2, lon_count // 2, level_count, -1).transpose(2, 0, 1, 3)
    latent_grad = latent_grad.reshape(lat_count, lon_count, level_count, width)
    latent_grad = latent_grad.transpose(2, 0, 1, 3)
    return merged, latent_grad, rows[:, : 3 * width], rows[:, 3 * width :]


def solution(mesh):
    placed = (
        P(None, "lat", "lon", None),
        P(None, "lat", "lon", None),
        P(),
        P(),
        P(),
        P(),
        P(None, "lat", None, None),
        P(None, "lat", "lon"),
        P(),
        P("lon", None),
    )
    return jax.shard_map(
        on_device,
        mesh=mesh,
        in_specs=placed,
        out_specs=(
            P(None, "lat", "lon", None),
            P(None, "lat", "lon", None),
            P("lon", None),
            P("lon", None),
        ),
        check_vma=False,
    )
```

time: 178 us -> 152 us (0.85)
  the two profiles are of different devices: /device:TPU:192 before, /device:TPU:2 now
where the time goes in v2:
time: 152 us
  starting transfers between devices  65.6 us (43%)
  waiting for transfers between devices  35 us (23%)
  Pallas kernels  31.4 us (21%)
  local copies, waits for them, and re-layouts  11.2 us (7%)
  other arithmetic  7.25 us (5%)
    all_to_all x4, starting transfers between devices, exchanged(): lax.all_to_all(array, axes, 0, 0, axis_index_groups=groups, tiled=True)  29.9 us
    all_to_all x4, waiting for transfers between devices, exchanged(): lax.all_to_all(array, axes, 0, 0, axis_index_groups=groups, tiled=True)  28.4 us
    ppermute x1, starting transfers between devices, on_device(): from_chip = lax.ppermute(jnp.concatenate([lon_half, pair]), 'lon', to_chip)  15.7 us
    pallas_call x1, Pallas kernels, attention(): pl.pallas_call(attention_kernel, out_shape=(jax.ShapeDtypeStruct((2 * SLO...  14.6 us
    pallas_call x1, Pallas kernels, gather_bias(): pl.pallas_call(bias_kernel, out_shape=jax.ShapeDtypeStruct((HEADS, TOK, T...  12.6 us
    ppermute x3, starting transfers between devices, shifted(): lax.ppermute(array, axis, [(i, (i + by) % size) for i in range(size)])  11.9 us
    unnamed x25, local copies, waits for them, and re-layouts  3.14 us
    ppermute x1, starting transfers between devices, on_device(): other = lax.ppermute(merge_weight, 'lon', between_cores)  3.04 us
  transfers between devices with their start and end apart: 12, of which 6 were waited for; matrix products, arithmetic and copies ran while one was open for 5% of the time, Pallas kernels for 19%

profile of v2, /device:TPU:2, one launch (start us, length us, event | category | flops | bytes accessed | tf_op | source)
XLA Modules:
  0.0 151.5 jit_solution(5268753815915116872)
XLA Ops:
  0.6 1.7 %reshape.57.x_ref = bf16[144,512]{1,0:T(8,128)(2,1)} reshape(bf16[6,12,2,512]{3,2,1,0:T(2,128)(2,1)} %bitcast.33) | data formatting | bytes 294912 | tf_op jit(solution)/shard_map/reshape | solution.py:445
  2.3 1.6 %reshape.58.u_ref = bf16[144,512]{1,0:T(8,128)(2,1)} reshape(bf16[6,12,2,512]{3,2,1,0:T(2,128)(2,1)} %bitcast.34) | data formatting | bytes 294912 | tf_op jit(solution)/shard_map/reshape | solution.py:446
  3.9 2.2 %prepare.1 = (bf16[160,512]{1,0:T(8,128)(2,1)}, bf16[80,512]{1,0:T(8,128)(2,1)}, bf16[80,512]{1,0:T(8,128)(2,1)}) custom-call(bf16[144,512]{1,0:T(8,128)(2,1)} %reshape.57.x_ref, bf16[144,512]{1,0:T(8,128)(2,1)} %reshape.58.u_ref), custom_call_target="tpu_custom_call" | custom-call | tf_op jit(solution)/shard_map/prepare/pallas_call | solution.py:93
  7.5 3.0 %collective-permute-start.1 = (bf16[32,512]{1,0:T(8,128)(2,1)}, bf16[32,512]{1,0:T(8,128)(2,1)S(1)}, u32[]{:S(2)}, u32[]{:S(2)}) collective-permute-start(bf16[32,512]{1,0:T(8,128)(2,1)} %param.19), channel_id=1, source_target_pairs={{0,1},{1,0},{2,3},{3,2},{4,5},{5,4},{6,7},{7,6},{8,9},{9,8},{10,11... | collective-permute-start | bytes 98312 | tf_op jit(solution)/shard_map/weight_core/ppermute | solution.py:459
  13.3 15.7 %collective-permute-start.2 = (bf16[224,512]{1,0:T(8,128)(2,1)S(1)}, bf16[224,512]{1,0:T(8,128)(2,1)S(1)}, u32[]{:S(2)}, u32[]{:S(2)}) collective-permute-start(bf16[224,512]{1,0:T(8,128)(2,1)S(1)} %pad_maximum_fusion), channel_id=1, source_target_pairs={{0,63},{2,1},{4,3},{6,5},{8,7},{10,9},{12,11},{14,13},{16,15},{18,... | collective-permute-start | bytes 688136 | tf_op jit(solution)/shard_map/lon_cross/ppermute | solution.py:466
  31.1 12.6 %bias_gather.1.bias_ref = f32[16,144,144]{2,1,0:T(8,128)S(1)} custom-call(s32[168,128]{1,0:T(8,128)S(1)} %pad_add_fusion.index_ref, f32[16,3328]{1,0:T(8,128)S(1)} %pad.13.table_ref, s32[144,128]{1,0:T(8,128)S(1)} %broadcast_in_dim.26.key_group_ref, s32[1,256]{1,0:T(1,128)S(1)} %bitcast.27), custom_call_target="tpu_custom_call" | custom-call | tf_op jit(solution)/shard_map/bias_gather/pallas_call | solution.py:173
  46.4 8.6 %all-to-all-start = ((bf16[16,64,512]{2,1,0:T(8,128)(2,1)}), bf16[16,64,512]{2,1,0:T(8,128)(2,1)S(1)}, u32[]{:S(2)}, u32[]{:S(2)}) async-start(bf16[16,64,512]{2,1,0:T(8,128)(2,1)} %broadcast_in_dim.29), calls=%async_computation | async-start | bytes 2097152 | tf_op jit(solution)/shard_map/weight_plane/all_to_all | solution.py:387
  55.0 5.6 %collective-permute-start.3 = (bf16[160,512]{1,0:T(8,128)(2,1)S(1)}, bf16[160,512]{1,0:T(8,128)(2,1)S(1)}, u32[]{:S(2)}, u32[]{:S(2)}) collective-permute-start(bf16[160,512]{1,0:T(8,128)(2,1)S(1)} %pad_maximum_fusion.1), channel_id=1, source_target_pairs={{0,448},{64,0},{128,64},{192,128},{256,192},{320,256},{384,320},{4... | collective-permute-start | bytes 491528 | tf_op jit(solution)/shard_map/lat_roll/ppermute | solution.py:383
  60.7 2.8 %collective-permute-done.3.lat_ref = bf16[160,512]{1,0:T(8,128)(2,1)S(1)} collective-permute-done((bf16[160,512]{1,0:T(8,128)(2,1)S(1)}, bf16[160,512]{1,0:T(8,128)(2,1)S(1)}, u32[]{:S(2)}, u32[]{:S(2)}) %collective-permute-start.3) | collective-permute-done | bytes 163872 | tf_op jit(solution)/shard_map/lat_roll/ppermute | solution.py:383
  64.2 14.6 %window_attention.1 = (bf16[80,512]{1,0:T(8,128)(2,1)}, bf16[160,512]{1,0:T(8,128)(2,1)}, bf16[80,512]{1,0:T(8,128)(2,1)}, bf16[256,2048]{1,0:T(8,128)(2,1)}, bf16[256,2048]{1,0:T(8,128)(2,1)}) custom-call(s32[1]{0:T(128)} %bitcast.core_ref, bf16[80,512]{1,0:T(8,128)(2,1)} %get-tuple-element.19.stay_ref, bf16[160,512]{1,0:T(8,128)(2,1)} %copy-done.5, ...), custom_call_target="tpu_custom_call" | custom-call | tf_op jit(solution)/shard_map/window_attention/pallas_call | solution.py:284
  78.8 1.9 %collective-permute-start.7 = (bf16[256,2048]{1,0:T(8,128)(2,1)}, bf16[256,2048]{1,0:T(8,128)(2,1)S(1)}, u32[]{:S(2)}, u32[]{:S(2)}) collective-permute-start(bf16[256,2048]{1,0:T(8,128)(2,1)} %get-tuple-element.33), channel_id=1, source_target_pairs={{0,1},{1,0},{2,3},{3,2},{4,5},{5,4},{6,7},{7,6},{8,9},{9,8},{10,11... | collective-permute-start | bytes 3145736 | tf_op jit(solution)/shard_map/term_core/ppermute | solution.py:484
  80.7 2.8 %collective-permute-done.7 = bf16[256,2048]{1,0:T(8,128)(2,1)S(1)} collective-permute-done((bf16[256,2048]{1,0:T(8,128)(2,1)}, bf16[256,2048]{1,0:T(8,128)(2,1)S(1)}, u32[]{:S(2)}, u32[]{:S(2)}) %collective-permute-start.7) | collective-permute-done | bytes 1048608 | tf_op jit(solution)/shard_map/term_core/ppermute | solution.py:484
  83.5 2.6 %add_convert_fusion = bf16[256,2048]{1,0:T(8,128)(2,1)} fusion(bf16[256,2048]{1,0:T(8,128)(2,1)S(1)} %collective-permute-done.7, bf16[256,2048]{1,0:T(8,128)(2,1)} %get-tuple-element.32), kind=kLoop, calls=%fused_computation | loop fusion | flops 2097152 | bytes 3145728 | tf_op jit(solution)/shard_map/convert_element_type | solution.py:487
  86.2 7.4 %all-to-all-start.1 = ((bf16[16,16,2048]{2,1,0:T(8,128)(2,1)}), bf16[16,16,2048]{2,1,0:T(8,128)(2,1)}, u32[]{:S(2)}, u32[]{:S(2)}) async-start(bf16[16,16,2048]{2,1,0:T(8,128)(2,1)} %bitcast.14), calls=%async_computation.1 | async-start | bytes 2097152 | tf_op jit(solution)/shard_map/term_plane/all_to_all | solution.py:387
  93.6 1.9 %collective-permute-start.6 = (bf16[1024,512]{1,0:T(8,128)(2,1)S(1)}, bf16[1024,512]{1,0:T(8,128)(2,1)S(1)}, u32[]{:S(2)}, u32[]{:S(2)}) collective-permute-start(bf16[1024,512]{1,0:T(8,128)(2,1)S(1)} %bitcast.23), channel_id=1, source_target_pairs={{0,1},{1,0},{2,3},{3,2},{4,5},{5,4},{6,7},{7,6},{8,9},{9,8},{10,11... | collective-permute-start | bytes 3145736 | tf_op jit(solution)/shard_map/weight_other/ppermute | solution.py:486
  95.5 2.4 %collective-permute-start.4 = (bf16[160,512]{1,0:T(8,128)(2,1)S(1)}, bf16[160,512]{1,0:T(8,128)(2,1)S(1)}, u32[]{:S(2)}, u32[]{:S(2)}) collective-permute-start(bf16[160,512]{1,0:T(8,128)(2,1)S(1)} %copy-done.11), channel_id=1, source_target_pairs={{0,1},{1,2},{2,3},{3,4},{4,5},{5,6},{6,7},{7,8},{8,9},{9,10},{10,1... | collective-permute-start | bytes 491528 | tf_op jit(solution)/shard_map/lon_back/ppermute | solution.py:383
  97.9 11.9 %all-to-all-done.1 = bf16[16,16,2048]{2,1,0:T(8,128)(2,1)} async-done(((bf16[16,16,2048]{2,1,0:T(8,128)(2,1)}), bf16[16,16,2048]{2,1,0:T(8,128)(2,1)}, u32[]{:S(2)}, u32[]{:S(2)}) %all-to-all-start.1) | async-done | bytes 1048608 | tf_op jit(solution)/shard_map/term_plane/all_to_all | solution.py:387
  109.8 2.0 %reduce_sum.24 = bf16[16,2048]{1,0:T(8,128)(2,1)} reduce(bf16[16,16,2048]{2,1,0:T(8,128)(2,1)} %all-to-all-done.1, bf16[]{:T(256)} %constant.54.clone.1), dimensions={0}, to_apply=%region_0.1 | reduce | flops 491520 | bytes 1114114 | tf_op jit(solution)/shard_map/term_z/reduce_sum | solution.py:403
  111.8 10.5 %all-to-all-start.2 = ((bf16[16,8,256]{2,1,0:T(8,128)(2,1)}), bf16[16,8,256]{2,1,0:T(8,128)(2,1)S(1)}, u32[]{:S(2)}, u32[]{:S(2)}) async-start(bf16[16,8,256]{2,1,0:T(8,128)(2,1)} %bitcast.17), calls=%async_computation.2 | async-start | bytes 131072 | tf_op jit(solution)/shard_map/term_z/all_to_all | solution.py:387
  122.3 3.8 %collective-permute-start.5 = (bf16[160,512]{1,0:T(8,128)(2,1)S(1)}, bf16[160,512]{1,0:T(8,128)(2,1)S(1)}, u32[]{:S(2)}, u32[]{:S(2)}) collective-permute-start(bf16[160,512]{1,0:T(8,128)(2,1)S(1)} %pad_maximum_fusion.2), channel_id=1, source_target_pairs={{0,64},{64,128},{128,192},{192,256},{256,320},{320,384},{384,448},... | collective-permute-start | bytes 491528 | tf_op jit(solution)/shard_map/lat_back/ppermute | solution.py:383
  126.2 9.6 %all-to-all-done.2 = bf16[16,8,256]{2,1,0:T(8,128)(2,1)S(1)} async-done(((bf16[16,8,256]{2,1,0:T(8,128)(2,1)}), bf16[16,8,256]{2,1,0:T(8,128)(2,1)S(1)}, u32[]{:S(2)}, u32[]{:S(2)}) %all-to-all-start.2) | async-done | bytes 65568 | tf_op jit(solution)/shard_map/term_z/all_to_all | solution.py:387
  136.4 3.3 %all-to-all-start.3 = ((bf16[8,8,256]{2,1,0:T(8,128)(2,1)}), bf16[8,8,256]{2,1,0:T(8,128)(2,1)S(1)}, u32[]{:S(2)}, u32[]{:S(2)}) async-start(bf16[8,8,256]{2,1,0:T(8,128)(2,1)} %broadcast_in_dim.30), calls=%async_computation.3 | async-start | bytes 65536 | tf_op jit(solution)/shard_map/term_lat/all_to_all | solution.py:387
  140.1 1.9 %finish.1 = (bf16[144,512]{1,0:T(8,128)(2,1)S(1)}, bf16[36,512]{1,0:T(8,128)(2,1)S(1)}) custom-call(s32[2]{0:T(128)S(1)} %pad_add_fusion.1.place_ref, bf16[144,512]{1,0:T(8,128)(2,1)S(1)} %copy-done.1, bf16[144,512]{1,0:T(8,128)(2,1)S(1)} %copy-done.2, bf16[80,512]{1,0:T(8,128)(2,1)S(1)} %copy-done.3, bf16[160,512]{1,0:T(8,128)(2,1)S(1)} %collective-permute-done.5.lat_ref, ...), custom_call_target="tpu_custom_call" | custom-call | tf_op jit(solution)/shard_map/finish/pallas_call | solution.py:368
  143.4 6.9 %all-to-all-done.3 = bf16[8,8,256]{2,1,0:T(8,128)(2,1)S(1)} async-done(((bf16[8,8,256]{2,1,0:T(8,128)(2,1)}), bf16[8,8,256]{2,1,0:T(8,128)(2,1)S(1)}, u32[]{:S(2)}, u32[]{:S(2)}) %all-to-all-start.3) | async-done | bytes 32800 | tf_op jit(solution)/shard_map/term_lat/all_to_all | solution.py:387
  (65 shorter events, 12.9 us)
Async XLA Ops:
  0.6 30.3 %copy-start.6 = (f32[3312,16]{0,1:T(8,128)S(1)}, f32[3312,16]{0,1:T(8,128)}, u32[]{:S(2)}) copy-start(f32[3312,16]{0,1:T(8,128)} %param.15) | copy-start | bytes 635908
  6.2 39.0 %collective-permute-start = (bf16[160,512]{1,0:T(8,128)(2,1)}, bf16[160,512]{1,0:T(8,128)(2,1)S(1)}, u32[]{:S(2)}, u32[]{:S(2)}) collective-permute-start(bf16[160,512]{1,0:T(8,128)(2,1)} %get-tuple-element.20), channel_id=1, source_target_pairs={{1,0},{3,2},{5,4},{7,6},{9,8},{11,10},{13,12},{15,14},{17,16},{19,... | collective-permute-start | bytes 491528 | tf_op jit(solution)/shard_map/lon_core/ppermute | solution.py:464
  7.5 4.1 %collective-permute-start.1 = (bf16[32,512]{1,0:T(8,128)(2,1)}, bf16[32,512]{1,0:T(8,128)(2,1)S(1)}, u32[]{:S(2)}, u32[]{:S(2)}) collective-permute-start(bf16[32,512]{1,0:T(8,128)(2,1)} %param.19), channel_id=1, source_target_pairs={{0,1},{1,0},{2,3},{3,2},{4,5},{5,4},{6,7},{7,6},{8,9},{9,8},{10,11... | collective-permute-start | bytes 98312 | tf_op jit(solution)/shard_map/weight_core/ppermute | solution.py:459
  13.3 31.9 %collective-permute-start.2 = (bf16[224,512]{1,0:T(8,128)(2,1)S(1)}, bf16[224,512]{1,0:T(8,128)(2,1)S(1)}, u32[]{:S(2)}, u32[]{:S(2)}) collective-permute-start(bf16[224,512]{1,0:T(8,128)(2,1)S(1)} %pad_maximum_fusion), channel_id=1, source_target_pairs={{0,63},{2,1},{4,3},{6,5},{8,7},{10,9},{12,11},{14,13},{16,15},{18,... | collective-permute-start | bytes 688136 | tf_op jit(solution)/shard_map/lon_cross/ppermute | solution.py:466
  30.8 14.5 %copy-start.8 = (bf16[80,512]{1,0:T(8,128)(2,1)S(1)}, bf16[80,512]{1,0:T(8,128)(2,1)}, u32[]{:S(2)}) copy-start(bf16[80,512]{1,0:T(8,128)(2,1)} %get-tuple-element.21) | copy-start | bytes 245764
  43.7 1.4 copy-start
  45.2 18.3 %copy-start.5 = (bf16[160,512]{1,0:T(8,128)(2,1)}, bf16[160,512]{1,0:T(8,128)(2,1)S(1)}, u32[]{:S(2)}) copy-start(bf16[160,512]{1,0:T(8,128)(2,1)S(1)} %slice_select_fusion.lon_ref) | copy-start | bytes 491524
  46.4 32.4 %all-to-all-start = ((bf16[16,64,512]{2,1,0:T(8,128)(2,1)}), bf16[16,64,512]{2,1,0:T(8,128)(2,1)S(1)}, u32[]{:S(2)}, u32[]{:S(2)}) async-start(bf16[16,64,512]{2,1,0:T(8,128)(2,1)} %broadcast_in_dim.29), calls=%async_computation | async-start | bytes 2097152 | tf_op jit(solution)/shard_map/weight_plane/all_to_all | solution.py:387
  55.0 8.5 %collective-permute-start.3 = (bf16[160,512]{1,0:T(8,128)(2,1)S(1)}, bf16[160,512]{1,0:T(8,128)(2,1)S(1)}, u32[]{:S(2)}, u32[]{:S(2)}) collective-permute-start(bf16[160,512]{1,0:T(8,128)(2,1)S(1)} %pad_maximum_fusion.1), channel_id=1, source_target_pairs={{0,448},{64,0},{128,64},{192,128},{256,192},{320,256},{384,320},{4... | collective-permute-start | bytes 491528 | tf_op jit(solution)/shard_map/lat_roll/ppermute | solution.py:383
  63.5 0.7 copy-start.7
  78.8 4.8 %collective-permute-start.7 = (bf16[256,2048]{1,0:T(8,128)(2,1)}, bf16[256,2048]{1,0:T(8,128)(2,1)S(1)}, u32[]{:S(2)}, u32[]{:S(2)}) collective-permute-start(bf16[256,2048]{1,0:T(8,128)(2,1)} %get-tuple-element.33), channel_id=1, source_target_pairs={{0,1},{1,0},{2,3},{3,2},{4,5},{5,4},{6,7},{7,6},{8,9},{9,8},{10,11... | collective-permute-start | bytes 3145736 | tf_op jit(solution)/shard_map/term_core/ppermute | solution.py:484
  83.5 12.0 %copy-start.11 = (bf16[160,512]{1,0:T(8,128)(2,1)S(1)}, bf16[160,512]{1,0:T(8,128)(2,1)}, u32[]{:S(2)}) copy-start(bf16[160,512]{1,0:T(8,128)(2,1)} %get-tuple-element.26) | copy-start | bytes 491524
  86.1 36.2 %copy-start.9 = (bf16[80,512]{1,0:T(8,128)(2,1)S(1)}, bf16[80,512]{1,0:T(8,128)(2,1)}, u32[]{:S(2)}) copy-start(bf16[80,512]{1,0:T(8,128)(2,1)} %get-tuple-element.25) | copy-start | bytes 245764
  86.1 53.6 %copy-start.10 = (f32[2048]{0:T(1024)S(1)}, f32[2048]{0:T(1024)}, u32[]{:S(2)}) copy-start(f32[2048]{0:T(1024)} %param.18) | copy-start | bytes 24580
  86.1 53.9 %copy-start.1 = (bf16[144,512]{1,0:T(8,128)(2,1)S(1)}, bf16[144,512]{1,0:T(8,128)(2,1)}, u32[]{:S(2)}) copy-start(bf16[144,512]{1,0:T(8,128)(2,1)} %reshape.57.x_ref) | copy-start | bytes 442372
  86.1 53.9 %copy-start.2 = (bf16[144,512]{1,0:T(8,128)(2,1)S(1)}, bf16[144,512]{1,0:T(8,128)(2,1)}, u32[]{:S(2)}) copy-start(bf16[144,512]{1,0:T(8,128)(2,1)} %reshape.58.u_ref) | copy-start | bytes 442372
  86.1 53.9 %copy-start.3 = (bf16[80,512]{1,0:T(8,128)(2,1)S(1)}, bf16[80,512]{1,0:T(8,128)(2,1)}, u32[]{:S(2)}) copy-start(bf16[80,512]{1,0:T(8,128)(2,1)} %get-tuple-element.24.stay_ref) | copy-start | bytes 245764
  86.2 53.9 %copy-start.4 = (f32[512]{0:T(512)S(1)}, f32[512]{0:T(512)}, u32[]{:S(2)}) copy-start(f32[512]{0:T(512)} %param.12) | copy-start | bytes 6148
  86.2 23.6 %all-to-all-start.1 = ((bf16[16,16,2048]{2,1,0:T(8,128)(2,1)}), bf16[16,16,2048]{2,1,0:T(8,128)(2,1)}, u32[]{:S(2)}, u32[]{:S(2)}) async-start(bf16[16,16,2048]{2,1,0:T(8,128)(2,1)} %bitcast.14), calls=%async_computation.1 | async-start | bytes 2097152 | tf_op jit(solution)/shard_map/term_plane/all_to_all | solution.py:387
  93.6 46.4 %collective-permute-start.6 = (bf16[1024,512]{1,0:T(8,128)(2,1)S(1)}, bf16[1024,512]{1,0:T(8,128)(2,1)S(1)}, u32[]{:S(2)}, u32[]{:S(2)}) collective-permute-start(bf16[1024,512]{1,0:T(8,128)(2,1)S(1)} %bitcast.23), channel_id=1, source_target_pairs={{0,1},{1,0},{2,3},{3,2},{4,5},{5,4},{6,7},{7,6},{8,9},{9,8},{10,11... | collective-permute-start | bytes 3145736 | tf_op jit(solution)/shard_map/weight_other/ppermute | solution.py:486
  95.5 26.7 %collective-permute-start.4 = (bf16[160,512]{1,0:T(8,128)(2,1)S(1)}, bf16[160,512]{1,0:T(8,128)(2,1)S(1)}, u32[]{:S(2)}, u32[]{:S(2)}) collective-permute-start(bf16[160,512]{1,0:T(8,128)(2,1)S(1)} %copy-done.11), channel_id=1, source_target_pairs={{0,1},{1,2},{2,3},{3,4},{4,5},{5,6},{6,7},{7,8},{8,9},{9,10},{10,1... | collective-permute-start | bytes 491528 | tf_op jit(solution)/shard_map/lon_back/ppermute | solution.py:383
  111.8 23.9 %all-to-all-start.2 = ((bf16[16,8,256]{2,1,0:T(8,128)(2,1)}), bf16[16,8,256]{2,1,0:T(8,128)(2,1)S(1)}, u32[]{:S(2)}, u32[]{:S(2)}) async-start(bf16[16,8,256]{2,1,0:T(8,128)(2,1)} %bitcast.17), calls=%async_computation.2 | async-start | bytes 131072 | tf_op jit(solution)/shard_map/term_z/all_to_all | solution.py:387
  122.3 17.7 %collective-permute-start.5 = (bf16[160,512]{1,0:T(8,128)(2,1)S(1)}, bf16[160,512]{1,0:T(8,128)(2,1)S(1)}, u32[]{:S(2)}, u32[]{:S(2)}) collective-permute-start(bf16[160,512]{1,0:T(8,128)(2,1)S(1)} %pad_maximum_fusion.2), channel_id=1, source_target_pairs={{0,64},{64,128},{128,192},{192,256},{256,320},{320,384},{384,448},... | collective-permute-start | bytes 491528 | tf_op jit(solution)/shard_map/lat_back/ppermute | solution.py:383
  136.4 13.9 %all-to-all-start.3 = ((bf16[8,8,256]{2,1,0:T(8,128)(2,1)}), bf16[8,8,256]{2,1,0:T(8,128)(2,1)S(1)}, u32[]{:S(2)}, u32[]{:S(2)}) async-start(bf16[8,8,256]{2,1,0:T(8,128)(2,1)} %broadcast_in_dim.30), calls=%async_computation.3 | async-start | bytes 65536 | tf_op jit(solution)/shard_map/term_lat/all_to_all | solution.py:387

commit v3 on v2

--- a/solution.py
+++ b/solution.py
@@ -13,6 +13,8 @@
 WIN_LAT = 6
 WIN_LON = 12
 TOK = 144
+HALF_LAT = 3
+HALF_LON = 6
 PART = 36
 SLOT = 40
 EPSILON = 1e-05
@@ -42,65 +44,27 @@
     return jnp.where(source == old, 1.0, 0.0).astype(BF16)
 
 
-def cell_of_slot(row, level_swap):
-    quarter, cell = row // SLOT, row % SLOT
-    level, rest = cell // 18, cell % 18
-    lat = 3 * (quarter // 2) + rest // 6
-    lon = 6 * (quarter % 2) + rest % 6
-    if level_swap:
-        level = 1 - level
-    return jnp.where(cell < PART, level * 72 + lat * 12 + lon, -1)
-
-
-def slots_from_cells(level_swap=False):
-    row = lax.broadcasted_iota(jnp.int32, (4 * SLOT, TOK), 0)
-    column = lax.broadcasted_iota(jnp.int32, (4 * SLOT, TOK), 1)
-    return one_hot(cell_of_slot(row, level_swap), column)
-
-
-def cells_from_slots(level_swap=False):
-    row = lax.broadcasted_iota(jnp.int32, (TOK, 4 * SLOT), 0)
-    column = lax.broadcasted_iota(jnp.int32, (TOK, 4 * SLOT), 1)
-    return one_hot(cell_of_slot(column, level_swap), row)
-
-
-def quarters_of(values):
-    return [values[SLOT * q : SLOT * q + SLOT] for q in range(4)]
-
-
-def stacked(pieces):
-    return jnp.concatenate(pieces, axis=0).astype(BF16)
-
-
-def row_of_place(place):
+def own_cell(row):
+    cell, level = row // 2, row % 2
+    return cell // WIN_LON, cell % WIN_LON, level
+
+
+def window_cell(place):
     level, rest = place // (TOK // 2), place % (TOK // 2)
-    return jnp.where(place < 0, -1, 2 * rest + level)
-
-
-def prepare_kernel(x_ref, u_ref, lon_ref, lat_ref, stay_ref):
-    row = lax.broadcasted_iota(jnp.int32, (4 * SLOT, TOK), 0)
-    column = lax.broadcasted_iota(jnp.int32, (4 * SLOT, TOK), 1)
-    order = one_hot(row_of_place(cell_of_slot(row, True)), column)
-    x = quarters_of(nn(order, x_ref[...]))
-    u = quarters_of(nn(order, u_ref[...]))
-    lon_ref[...] = stacked([x[0], u[0], x[2], u[2]])
-    lat_ref[...] = stacked([x[1], u[1]])
-    stay_ref[...] = stacked([x[3], u[3]])
-
-
-def prepare(x, u):
-    width = x.shape[-1]
-    return pl.pallas_call(
-        prepare_kernel,
-        out_shape=(
-            jax.ShapeDtypeStruct((4 * SLOT, width), BF16),
-            jax.ShapeDtypeStruct((2 * SLOT, width), BF16),
-            jax.ShapeDtypeStruct((2 * SLOT, width), BF16),
-        ),
-        in_specs=[VMEM] * 2,
-        out_specs=(VMEM,) * 3,
-        name="prepare",
-    )(x, u)
+    lat, lon = rest // WIN_LON, rest % WIN_LON
+    return lat // HALF_LAT, lon // HALF_LON, lat % HALF_LAT, lon % HALF_LON, 1 - level
+
+
+def picks(size, columns, source):
+    row = lax.broadcasted_iota(jnp.int32, (size, 1), 0)
+    column = lax.broadcasted_iota(jnp.int32, (size, columns), 1)
+    return one_hot(source(row), column)
+
+
+def picked_into(size, columns, target):
+    row = lax.broadcasted_iota(jnp.int32, (size, columns), 0)
+    column = lax.broadcasted_iota(jnp.int32, (1, columns), 1)
+    return one_hot(row, target(column))
 
 
 def lookup(index, table_ref):
@@ -116,7 +80,9 @@
     return found
 
 
-def bias_kernel(index_ref, table_ref, key_group_ref, query_group_ref, bias_ref, tail_ref):
+def bias_kernel(turn_ref, index_ref, table_ref, key_group_ref, query_group_ref, *refs):
+    given_ref = refs[0] if len(refs) == 3 else None
+    bias_ref, tail_ref = refs[-2:]
     rest = TOK - 128
     per_row = 128 // rest
 
@@ -149,9 +115,18 @@
             bias_ref[head, pl.ds(base, 8), 128:] = value[:, :rest]
         return carry
 
-    lax.fori_loop(0, TOK // 8, main_rows, 0)
-    lax.fori_loop(0, tail_ref.shape[1] // 8, tail_rows, 0)
-    lax.fori_loop(0, TOK // per_row, spread_rows, 0)
+    @pl.when(turn_ref[0] == 1)
+    def _():
+        lax.fori_loop(0, TOK // 8, main_rows, 0)
+        lax.fori_loop(0, tail_ref.shape[1] // 8, tail_rows, 0)
+        lax.fori_loop(0, TOK // per_row, spread_rows, 0)
+
+    if given_ref is not None:
+
+        @pl.when(turn_ref[0] != 1)
+        def _():
+            for head in range(HEADS):
+                bias_ref[head] = given_ref[head]
 
 
 def bias_operands(bias_table, bias_index, groups):
@@ -168,22 +143,23 @@
     return index, table, key_group, query_group
 
 
-def gather_bias(operands):
+def gather_bias(turn, operands, *given):
     tail = operands[0].shape[0] - TOK
     return pl.pallas_call(
         bias_kernel,
         out_shape=jax.ShapeDtypeStruct((HEADS, TOK, TOK), F32),
-        in_specs=[VMEM] * 4,
+        in_specs=[SMEM] + [VMEM] * (4 + len(given)),
         out_specs=VMEM,
         scratch_shapes=[pltpu.VMEM((HEADS, tail, 128), F32)],
         compiler_params=pltpu.CompilerParams(vmem_limit_bytes=12 * 1024 * 1024),
         name="bias_gather",
-    )(*operands)
+    )(turn, *operands, *given)
 
 
 def attention_kernel(
     core_ref,
-    stay_ref,
+    x_ref,
+    u_ref,
     lon_ref,
     lat_ref,
     gain_ref,
@@ -202,14 +178,28 @@
     width = gain_ref.shape[1]
     scale = HEAD_DIM ** (-0.5)
     core = core_ref[0]
-    gather = cells_from_slots()
-    stay, lon, lat = (r[...].astype(F32) for r in (stay_ref, lon_ref, lat_ref))
+
+    def from_own(place):
+        south, east, lat, lon, level = window_cell(place)
+        row = ((lat + HALF_LAT) * WIN_LON + lon + HALF_LON) * 2 + level
+        return jnp.where(south + east == 0, row, -1)
+
+    def from_lon(array, place):
+        south, east, lat, lon, level = window_cell(place)
+        row = ((lat + HALF_LAT) * HALF_LON + lon) * 2 + level + 2 * PART * array
+        return jnp.where((south == 0) & (east == 1), row, -1)
+
+    def from_lat(array, place):
+        south, east, lat, lon, level = window_cell(place)
+        row = (lat * HALF_LON + lon) * 2 + level + PART * array + 2 * PART * east
+        return jnp.where(south == 1, row, -1)
+
     arrays = []
-    for array in range(2):
-        at = slice(SLOT * array, SLOT * array + SLOT)
-        later = slice(SLOT * array + 2 * SLOT, SLOT * array + 3 * SLOT)
-        slots = stacked([stay[at], lon[later], lat[at], lat[later]])
-        arrays.append(nn(gather, slots).astype(BF16))
+    for array, own_ref in enumerate((x_ref, u_ref)):
+        values = nn(picks(TOK, TOK, from_own), own_ref[...])
+        values += nn(picks(TOK, TOK, functools.partial(from_lon, array)), lon_ref[...])
+        values += nn(picks(TOK, TOK, functools.partial(from_lat, array)), lat_ref[...])
+        arrays.append(values.astype(BF16))
     x, u = arrays
     standard, _ = layer_norm(x.astype(F32))
     xn = (standard * gain_ref[...]).astype(BF16)
@@ -221,7 +211,7 @@
     row = lax.broadcasted_iota(jnp.int32, (width, width), 0)
     column = lax.broadcasted_iota(jnp.int32, (width, width), 1)
     wide_eye = one_hot(row, column)
-    qt, kt, vt = (nt(wide_eye, block).astype(BF16) for block in (q_nat, k_nat, v_nat))
+    qt, kt, vt = (block.astype(F32).T.astype(BF16) for block in (q_nat, k_nat, v_nat))
     cg_nat = nt(u, m).astype(BF16)
     cgt = nt(m, u).astype(BF16)
     lane = lax.broadcasted_iota(jnp.int32, (TOK, 128), 1)
@@ -229,6 +219,14 @@
         cut = slice(128 * group, 128 * group + 128)
         kg, vg, qg, cgg = k_nat[:, cut], v_nat[:, cut], q_nat[:, cut], cg_nat[:, cut]
         qtg, cgtg = qt[cut], cgt[cut]
+        masks = [(lane >= HEAD_DIM * p) & (lane < HEAD_DIM * (p + 1)) for p in range(4)]
+
+        def spread_heads(block):
+            block = block.astype(F32)
+            return jnp.concatenate([jnp.where(m_, block, 0.0) for m_ in masks]).astype(BF16)
+
+        group_logits = nn(spread_heads(kg), qtg)
+        group_grads = nn(spread_heads(vg), cgtg)
         dk = jnp.zeros((TOK, 128), F32)
         dv = jnp.zeros((TOK, 128), F32)
         for part in range(4):
@@ -239,13 +237,13 @@
                 return jnp.where(own, block.astype(F32), 0.0).astype(BF16)
 
             at = slice(HEAD_DIM * head, HEAD_DIM * head + HEAD_DIM)
-            logits = nn(only(kg), qtg) * scale + bias_ref[head]
+            logits = group_logits[TOK * part : TOK * part + TOK] * scale + bias_ref[head]
             top = jnp.max(logits, axis=0, keepdims=True)
             raised = jnp.exp(logits - top)
             shares = raised * (1.0 / jnp.sum(raised, axis=0, keepdims=True))
             shares_low = shares.astype(BF16)
             ct_ref[at, :] = nn(vt[at], shares_low).astype(BF16)
-            share_grad = nn(only(vg), cgtg)
+            share_grad = group_grads[TOK * part : TOK * part + TOK]
             product = shares * share_grad
             total = jnp.sum(product, axis=0, keepdims=True)
             logit_grad = (shares * (share_grad - total)).astype(BF16)
@@ -257,17 +255,34 @@
     row = lax.broadcasted_iota(jnp.int32, (TOK, TOK), 0)
     column = lax.broadcasted_iota(jnp.int32, (TOK, TOK), 1)
     eye = one_hot(row, column)
-    tg_ref[:, :width] = nt(eye, dqt_ref[...]).astype(BF16)
+    tg_ref[:, :width] = dqt_ref[...].astype(F32).T.astype(BF16)
     ct = ct_ref[...]
-    context = nt(eye, ct).astype(BF16)
+    context = ct.astype(F32).T.astype(BF16)
     tg = tg_ref[...]
-    spread = slots_from_cells()
-    back = [quarters_of(nn(spread, v.astype(BF16))) for v in (nn(context, m), nt(tg, w))]
-    stay_out_ref[...] = stacked([back[0][0], back[1][0]])
-    lon_out_ref[...] = stacked([back[0][1], back[1][1], back[0][3], back[1][3]])
-    lat_out_ref[...] = stacked([back[0][2], back[1][2]])
+
+    def to_stay(array, place):
+        south, east, lat, lon, level = window_cell(place)
+        row = (lat * HALF_LON + lon) * 2 + level + PART * array
+        return jnp.where(south + east == 0, row, -1)
+
+    def to_lon(array, place):
+        south, east, lat, lon, level = window_cell(place)
+        row = ((lat + HALF_LAT * south) * HALF_LON + lon) * 2 + level + 2 * PART * array
+        return jnp.where(east == 1, row, -1)
+
+    def to_lat(array, place):
+        south, east, lat, lon, level = window_cell(place)
+        row = (lat * HALF_LON + lon) * 2 + level + PART * array
+        return jnp.where((south == 1) & (east == 0), row, -1)
+
+    results = [values.astype(BF16) for values in (nn(context, m), nt(tg, w))]
+    for target, place in ((stay_out_ref, to_stay), (lon_out_ref, to_lon), (lat_out_ref, to_lat)):
+        rows = target.shape[0]
+        values = nn(picked_into(rows, TOK, functools.partial(place, 0)), results[0])
+        values += nn(picked_into(rows, TOK, functools.partial(place, 1)), results[1])
+        target[...] = values.astype(BF16)
     half = width // 2
-    new = lax.broadcasted_iota(jnp.int32, (width, width), 0)
+    new = lax.broadcasted_iota(jnp.int32, (width, 1), 0)
     old = lax.broadcasted_iota(jnp.int32, (width, width), 1)
     local = new & (half - 1)
     parity = jnp.where(new >= half, 1 - core, core)
@@ -279,18 +294,18 @@
         target[:, 3 * width :] = nn(cto[rows], u).astype(BF16)
 
 
-def attention(core, stay, lon, lat, gain, w, m, bias):
+def attention(core, x, u, lon, lat, gain, w, m, bias):
     width = gain.shape[1]
     return pl.pallas_call(
         attention_kernel,
         out_shape=(
-            jax.ShapeDtypeStruct((2 * SLOT, width), BF16),
-            jax.ShapeDtypeStruct((4 * SLOT, width), BF16),
-            jax.ShapeDtypeStruct((2 * SLOT, width), BF16),
+            jax.ShapeDtypeStruct((2 * PART, width), BF16),
+            jax.ShapeDtypeStruct((4 * PART, width), BF16),
+            jax.ShapeDtypeStruct((2 * PART, width), BF16),
             jax.ShapeDtypeStruct((width // 2, 4 * width), BF16),
             jax.ShapeDtypeStruct((width // 2, 4 * width), BF16),
         ),
-        in_specs=[SMEM] + [VMEM] * 7,
+        in_specs=[SMEM] + [VMEM] * 8,
         out_specs=(VMEM,) * 5,
         scratch_shapes=[
             pltpu.VMEM((width, TOK), BF16),
@@ -299,7 +314,7 @@
         ],
         compiler_params=pltpu.CompilerParams(vmem_limit_bytes=56 * 1024 * 1024),
         name="window_attention",
-    )(core, stay, lon, lat, gain, w, m, bias)
+    )(core, x, u, lon, lat, gain, w, m, bias)
 
 
 def finish_kernel(
@@ -318,15 +333,31 @@
 ):
     width = x_ref.shape[-1]
     x = x_ref[...].astype(F32)
-    row = lax.broadcasted_iota(jnp.int32, (TOK, 4 * SLOT), 0)
-    column = lax.broadcasted_iota(jnp.int32, (TOK, 4 * SLOT), 1)
-    gather = one_hot(row_of_place(cell_of_slot(column, True)), row)
-    stay, lon, lat = (r[...].astype(F32) for r in (stay_ref, lon_ref, lat_ref))
+
+    def from_stay(array, row):
+        lat, lon, level = own_cell(row)
+        source = ((lat - HALF_LAT) * HALF_LON + lon - HALF_LON) * 2 + level + PART * array
+        return jnp.where((lat >= HALF_LAT) & (lon >= HALF_LON), source, -1)
+
+    def from_lon(array, row):
+        lat, lon, level = own_cell(row)
+        source = ((lat - HALF_LAT) * HALF_LON + lon) * 2 + level + 2 * PART * array
+        return jnp.where((lat >= HALF_LAT) & (lon < HALF_LON), source, -1)
+
+    def from_lat(array, row):
+        lat, lon, level = own_cell(row)
+        west = (lon < HALF_LON).astype(jnp.int32)
+        place = lon - HALF_LON * (1 - west)
+        source = (lat * HALF_LON + place) * 2 + level + PART * array + 2 * PART * west
+        return jnp.where(lat < HALF_LAT, source, -1)
+
     arrays = []
     for array in range(2):
-        at = slice(SLOT * array, SLOT * array + SLOT)
-        later = slice(SLOT * array + 2 * SLOT, SLOT * array + 3 * SLOT)
-        arrays.append(nn(gather, stacked([lat[later], lat[at], lon[at], stay[at]])))
+        values = 0.0
+        for ref, source in ((stay_ref, from_stay), (lon_ref, from_lon), (lat_ref, from_lat)):
+            taken = picks(TOK, ref.shape[0], functools.partial(source, array))
+            values = values + nn(taken, ref[...])
+        arrays.append(values)
     normalized, inverse = layer_norm(x)
     scaled = arrays[1] * gain_ref[...]
     first = jnp.mean(scaled, axis=-1, keepdims=True)
@@ -334,19 +365,20 @@
     back = inverse * (scaled - first - normalized * second)
     block = (x + arrays[0]).astype(BF16)
     grad_ref[...] = (u_ref[...].astype(F32) + back).astype(BF16)
-    new = lax.broadcasted_iota(jnp.int32, (width, width), 1)
+    new = lax.broadcasted_iota(jnp.int32, (1, width), 1)
     old = lax.broadcasted_iota(jnp.int32, (width, width), 0)
     half = width // 2
     odd = (new >= half).astype(jnp.int32)
     local = new & (half - 1)
     block = nn(block, one_hot(((local >> 6) << 7) + (odd << 6) + (local & 63), old)).astype(BF16)
-    row = lax.broadcasted_iota(jnp.int32, (4 * SLOT, TOK), 0)
+    row = lax.broadcasted_iota(jnp.int32, (4 * SLOT, 1), 0)
     column = lax.broadcasted_iota(jnp.int32, (4 * SLOT, TOK), 1)
     corner, cell = row // SLOT, row % SLOT
     pair, level = cell // 2, cell % 2
     lat_at, lon_at = 2 * (pair // 6) + corner % 2, 2 * (pair % 6) + corner // 2
     place = (lat_at * WIN_LON + lon_at) * 2 + level
-    corners = quarters_of(nn(one_hot(jnp.where(cell < PART, place, -1), column), block))
+    corners = nn(one_hot(jnp.where(cell < PART, place, -1), column), block)
+    corners = [corners[SLOT * c : SLOT * c + SLOT] for c in range(4)]
     joined = jnp.concatenate([c[:, :half] for c in corners] + [c[:, half:] for c in corners], axis=-1)
     features, _ = layer_norm(joined)
     features = features * merge_gain_ref[...]
@@ -442,9 +474,14 @@
     between_cores = [(i, i ^ 1) for i in range(lon_size)]
     to_chip = [(i, (i - 1) % lon_size) for i in range(0, lon_size, 2)]
     to_core = [(i, i - 1) for i in range(1, lon_size, 2)]
-    x = latent.transpose(1, 2, 0, 3).reshape(TOK, width)
-    u = upstream.transpose(1, 2, 0, 3).reshape(TOK, width)
-    lon_half, lat_half, stay = prepare(x, u)
+
+    def rows_of(block):
+        return block.transpose(1, 2, 0, 3).reshape(-1, width)
+
+    x, u = rows_of(latent), rows_of(upstream)
+    lon_half = [rows_of(array[:, :, :HALF_LON]) for array in (latent, upstream)]
+    lat_half = [rows_of(array[:, :HALF_LAT, HALF_LON:]) for array in (latent, upstream)]
+    lon_half = jnp.concatenate(lon_half)
     lat_global = lax.axis_index("lat") * lat_count + lax.broadcasted_iota(
         jnp.int32, regions.shape, 1
     )
@@ -455,20 +492,24 @@
         + 6 * (level_local >= LEVELS - 1).astype(jnp.int32)
     )
     operands = bias_operands(bias_table, bias_index, groups)
+    early = ((core == 0) & (high == 0)).astype(jnp.int32).reshape(1)
+    with jax.named_scope("lon_core"):
+        from_core = lax.ppermute(lon_half, "lon", to_core)
     with jax.named_scope("weight_core"):
         other = lax.ppermute(merge_weight, "lon", between_cores)
-    pair = jnp.concatenate(
-        [jnp.where(first_core, merge_weight, other), jnp.where(first_core, other, merge_weight)]
-    )
-    with jax.named_scope("lon_core"):
-        from_core = lax.ppermute(lon_half, "lon", to_core)
+    pair = [jnp.where(first_core, merge_weight, other), jnp.where(first_core, other, merge_weight)]
+    leaving = jnp.concatenate([lon_half] + pair)
+    early, from_core, leaving = lax.optimization_barrier((early, from_core, leaving))
+    bias = gather_bias(early, operands)
+    leaving, bias = lax.optimization_barrier((leaving, bias))
     with jax.named_scope("lon_cross"):
-        from_chip = lax.ppermute(jnp.concatenate([lon_half, pair]), "lon", to_chip)
-    bias = gather_bias(operands)
+        from_chip = lax.ppermute(leaving, "lon", to_chip)
+    bias = gather_bias(1 - early, operands, bias)
     half_rows = lon_half.shape[0]
     lon_half = jnp.where(first_core, from_core, from_chip[:half_rows])
-    pair = jnp.where(first_core, pair, from_chip[half_rows:])
-    lat_half = jnp.concatenate([lat_half, lon_half[: 2 * SLOT]])
+    pair = jnp.where(first_core, leaving[half_rows:], from_chip[half_rows:])
+    lat_half += [lon_half[:PART], lon_half[2 * PART : 3 * PART]]
+    lat_half = jnp.concatenate(lat_half)
     lat_half, pair, bias = lax.optimization_barrier((lat_half, pair, bias))
     with jax.named_scope("lat_roll"):
         lat_half = shifted(lat_half, "lat", -1)
@@ -477,34 +518,34 @@
         own_weight = exchanged(pair, "lon", plane_groups(lon_size))
     gain = norm_gain[None]
     lat_back, lon_back, stay_back, keep, send = attention(
-        core.reshape(1), stay, lon_half, lat_half, gain, heads_weight, mixing_weight, bias
+        core.reshape(1), x, u, lon_half, lat_half, gain, heads_weight, mixing_weight, bias
     )
     send, own_weight = lax.optimization_barrier((send, own_weight))
     with jax.named_scope("term_core"):
         arrived = lax.ppermute(send, "lon", between_cores)
-    with jax.named_scope("weight_other"):
-        other_weight = lax.ppermute(own_weight, "lon", between_cores)
     paired = (keep.astype(F32) + arrived.astype(F32)).astype(BF16)
     with jax.named_scope("term_plane"):
         terms = reduce_over_planes(paired)
     with jax.named_scope("lon_back"):
         lon_back = shifted(lon_back, "lon", 1)
     with jax.named_scope("lat_back"):
-        lat_back = shifted(jnp.concatenate([lat_back, lon_back[2 * SLOT :]]), "lat", 1)
+        lat_back = shifted(jnp.concatenate([lat_back, lon_back[PART : 2 * PART], lon_back[3 * PART :]]), "lat", 1)
+    with jax.named_scope("term_z"):
+        part = reduce_along_z(terms)
+    with jax.named_scope("weight_other"):
+        other_weight = lax.ppermute(own_weight, "lon", between_cores)
     latent_grad, merged = finish(
         jnp.stack([core, high]),
         x,
         u,
         stay_back,
         lat_back,
-        lon_back[: 2 * SLOT],
+        lon_back,
         gain,
         merge_gain,
         own_weight,
         other_weight,
     )
-    with jax.named_scope("term_z"):
-        part = reduce_along_z(terms)
     with jax.named_scope("term_lat"):
         rows = spread_over_lat(part).astype(F32) * factor
     merged = merged.reshape(lat_count // 2, lon_count // 2, level_count, -1).transpose(2, 0, 1, 3)

time: 152 us -> 140 us (0.921)
  starting transfers between devices: 65.6 us -> 55.3 us
  Pallas kernels: 31.4 us -> 23.9 us
  waiting for transfers between devices: 35 us -> 40.5 us
  other arithmetic: 7.25 us -> 5.68 us
    ppermute x1, starting transfers between devices: 15.7 us -> 3.93 us  [on_device(): from_chip = lax.ppermute(leaving, 'lon', to_chip)]
    pallas_call x2 -> x1, Pallas kernels: 16.9 us -> 9.17 us  [attention(): pl.pallas_call(attention_kernel, out_shape=(jax.ShapeDtypeStruct((2 * PAR...]
    ppermute x1, waiting for transfers between devices: 0.01 us -> 7.4 us  [on_device(): from_chip = lax.ppermute(leaving, 'lon', to_chip)]
    all_to_all x4, starting transfers between devices: 29.9 us -> 33.2 us  [exchanged(): lax.all_to_all(array, axes, 0, 0, axis_index_groups=groups, tiled=True)]
    transpose x0 -> x4, local copies, waits for them, and re-layouts: none -> 2.71 us  [rows_of(): return block.transpose(1, 2, 0, 3).reshape(-1, width)]
    reshape x2 -> x6, local copies, waits for them, and re-layouts: 3.3 us -> 1.55 us  [rows_of(): return block.transpose(1, 2, 0, 3).reshape(-1, width)]
    unnamed x25 -> x33, local copies, waits for them, and re-layouts: 3.14 us -> 3.71 us
    pallas_call x1 -> x2, Pallas kernels: 12.6 us -> 12.7 us  [gather_bias(): pl.pallas_call(bias_kernel, out_shape=jax.ShapeDtypeStruct((HEADS, TOK, T...]
  transfers between devices with their start and end apart: 12 -> 12, of which waited for: 6 -> 6; matrix products, arithmetic and copies ran while one was open for 5% -> 8% of each run, Pallas kernels for 19% -> 8%
where the time goes in v3:
time: 140 us; the launch traced here: 139 us
  starting transfers between devices  55.3 us (40%)
  waiting for transfers between devices  40.5 us (29%)
  Pallas kernels  23.9 us (17%)
  local copies, waits for them, and re-layouts  12.7 us (9%)
  other arithmetic  5.68 us (4%)
    all_to_all x4, starting transfers between devices, exchanged(): lax.all_to_all(array, axes, 0, 0, axis_index_groups=groups, tiled=True)  33.2 us
    all_to_all x4, waiting for transfers between devices, exchanged(): lax.all_to_all(array, axes, 0, 0, axis_index_groups=groups, tiled=True)  28.2 us
    pallas_call x2, Pallas kernels, gather_bias(): pl.pallas_call(bias_kernel, out_shape=jax.ShapeDtypeStruct((HEADS, TOK, T...  12.7 us
    ppermute x3, starting transfers between devices, shifted(): lax.ppermute(array, axis, [(i, (i + by) % size) for i in range(size)])  11 us
    pallas_call x1, Pallas kernels, attention(): pl.pallas_call(attention_kernel, out_shape=(jax.ShapeDtypeStruct((2 * PAR...  9.17 us
    ppermute x1, waiting for transfers between devices, on_device(): from_chip = lax.ppermute(leaving, 'lon', to_chip)  7.4 us
    ppermute x1, starting transfers between devices, on_device(): from_chip = lax.ppermute(leaving, 'lon', to_chip)  3.93 us
    unnamed x33, local copies, waits for them, and re-layouts  3.71 us
  transfers between devices with their start and end apart: 12, of which 6 were waited for; matrix products, arithmetic and copies ran while one was open for 8% of the time, Pallas kernels for 8%

profile of v3, /device:TPU:2, one launch (start us, length us, event | category | flops | bytes accessed | tf_op | source)
XLA Modules:
  0.0 139.3 jit_solution(17099551510458123456)
XLA Ops:
  0.7 2.1 %collective-permute-start.1 = (bf16[32,512]{1,0:T(8,128)(2,1)}, bf16[32,512]{1,0:T(8,128)(2,1)S(1)}, u32[]{:S(2)}, u32[]{:S(2)}) collective-permute-start(bf16[32,512]{1,0:T(8,128)(2,1)} %param.19), channel_id=1, source_target_pairs={{0,1},{1,0},{2,3},{3,2},{4,5},{5,4},{6,7},{7,6},{8,9},{9,8},{10,11... | collective-permute-start | bytes 98312 | tf_op jit(solution)/shard_map/weight_core/ppermute | solution.py:499
  4.7 1.3 collective-permute-start
  9.8 12.5 %bias_gather.2.refs_0_ = f32[16,144,144]{2,1,0:T(8,128)S(1)} custom-call(s32[1]{0:T(128)} %bitcast.4.turn_ref, s32[168,128]{1,0:T(8,128)S(1)} %pad_add_fusion.index_ref, f32[16,3328]{1,0:T(8,128)S(1)} %pad.13.table_ref, s32[144,128]{1,0:T(8,128)S(1)} %broadcast_in_dim.26.key_group_ref, s32[1,256]{1,0:T(1,128)S(1)} %bitcast.34), custom_call_target="tpu_custom_call" | custom-call | tf_op jit(solution)/shard_map/bias_gather/pallas_call | solution.py:148
  22.3 3.9 %collective-permute-start.2 = (bf16[208,512]{1,0:T(8,128)(2,1)S(1)}, bf16[208,512]{1,0:T(8,128)(2,1)S(1)}, u32[]{:S(2)}, u32[]{:S(2)}) collective-permute-start(bf16[208,512]{1,0:T(8,128)(2,1)S(1)} %pad_maximum_fusion), channel_id=1, source_target_pairs={{0,63},{2,1},{4,3},{6,5},{8,7},{10,9},{12,11},{14,13},{16,15},{18,... | collective-permute-start | bytes 638984 | tf_op jit(solution)/shard_map/lon_cross/ppermute | solution.py:506
  26.5 1.4 %copy-done = f32[16,144,144]{2,1,0:T(8,128)} copy-done((f32[16,144,144]{2,1,0:T(8,128)}, f32[16,144,144]{2,1,0:T(8,128)S(1)}, u32[]{:S(2)}) %copy-start) | copy-done | bytes 1327128
  27.9 7.4 %collective-permute-done.2 = bf16[208,512]{1,0:T(8,128)(2,1)S(1)} collective-permute-done((bf16[208,512]{1,0:T(8,128)(2,1)S(1)}, bf16[208,512]{1,0:T(8,128)(2,1)S(1)}, u32[]{:S(2)}, u32[]{:S(2)}) %collective-permute-start.2) | collective-permute-done | bytes 213024 | tf_op jit(solution)/shard_map/lon_cross/ppermute | solution.py:506
  36.5 7.5 %all-to-all-start = ((bf16[16,64,512]{2,1,0:T(8,128)(2,1)}), bf16[16,64,512]{2,1,0:T(8,128)(2,1)S(1)}, u32[]{:S(2)}, u32[]{:S(2)}) async-start(bf16[16,64,512]{2,1,0:T(8,128)(2,1)} %broadcast_in_dim.29), calls=%async_computation | async-start | bytes 2097152 | tf_op jit(solution)/shard_map/weight_plane/all_to_all | solution.py:419
  43.9 4.8 %collective-permute-start.3 = (bf16[144,512]{1,0:T(8,128)(2,1)S(1)}, bf16[144,512]{1,0:T(8,128)(2,1)S(1)}, u32[]{:S(2)}, u32[]{:S(2)}) collective-permute-start(bf16[144,512]{1,0:T(8,128)(2,1)S(1)} %pad_maximum_fusion.2), channel_id=1, source_target_pairs={{0,448},{64,0},{128,64},{192,128},{256,192},{320,256},{384,320},{4... | collective-permute-start | bytes 442376 | tf_op jit(solution)/shard_map/lat_roll/ppermute | solution.py:415
  50.2 2.1 %collective-permute-done.3.lat_ref = bf16[144,512]{1,0:T(8,128)(2,1)S(1)} collective-permute-done((bf16[144,512]{1,0:T(8,128)(2,1)S(1)}, bf16[144,512]{1,0:T(8,128)(2,1)S(1)}, u32[]{:S(2)}, u32[]{:S(2)}) %collective-permute-start.3) | collective-permute-done | bytes 147488 | tf_op jit(solution)/shard_map/lat_roll/ppermute | solution.py:415
  52.9 9.2 %window_attention.1 = (bf16[72,512]{1,0:T(8,128)(2,1)}, bf16[144,512]{1,0:T(8,128)(2,1)}, bf16[72,512]{1,0:T(8,128)(2,1)}, bf16[256,2048]{1,0:T(8,128)(2,1)}, bf16[256,2048]{1,0:T(8,128)(2,1)}) custom-call(s32[1]{0:T(128)} %bitcast.core_ref, bf16[144,512]{1,0:T(8,128)(2,1)} %reshape.75.x_ref, bf16[144,512]{1,0:T(8,128)(2,1)} %reshape.76.u_ref, ...), custom_call_target="tpu_custom_call" | custom-call | tf_op jit(solution)/shard_map/window_attention/pallas_call | solution.py:299
  62.1 1.9 %collective-permute-start.7 = (bf16[256,2048]{1,0:T(8,128)(2,1)}, bf16[256,2048]{1,0:T(8,128)(2,1)S(1)}, u32[]{:S(2)}, u32[]{:S(2)}) collective-permute-start(bf16[256,2048]{1,0:T(8,128)(2,1)} %get-tuple-element.37), channel_id=1, source_target_pairs={{0,1},{1,0},{2,3},{3,2},{4,5},{5,4},{6,7},{7,6},{8,9},{9,8},{10,11... | collective-permute-start | bytes 3145736 | tf_op jit(solution)/shard_map/term_core/ppermute | solution.py:525
  64.0 2.8 %collective-permute-done.7 = bf16[256,2048]{1,0:T(8,128)(2,1)S(1)} collective-permute-done((bf16[256,2048]{1,0:T(8,128)(2,1)}, bf16[256,2048]{1,0:T(8,128)(2,1)S(1)}, u32[]{:S(2)}, u32[]{:S(2)}) %collective-permute-start.7) | collective-permute-done | bytes 1048608 | tf_op jit(solution)/shard_map/term_core/ppermute | solution.py:525
  66.8 2.6 %add_convert_fusion = bf16[256,2048]{1,0:T(8,128)(2,1)} fusion(bf16[256,2048]{1,0:T(8,128)(2,1)S(1)} %collective-permute-done.7, bf16[256,2048]{1,0:T(8,128)(2,1)} %get-tuple-element.36), kind=kLoop, calls=%fused_computation | loop fusion | flops 2097152 | bytes 3145728 | tf_op jit(solution)/shard_map/convert_element_type | solution.py:526
  69.5 7.4 %all-to-all-start.1 = ((bf16[16,16,2048]{2,1,0:T(8,128)(2,1)}), bf16[16,16,2048]{2,1,0:T(8,128)(2,1)}, u32[]{:S(2)}, u32[]{:S(2)}) async-start(bf16[16,16,2048]{2,1,0:T(8,128)(2,1)} %bitcast.19), calls=%async_computation.1 | async-start | bytes 2097152 | tf_op jit(solution)/shard_map/term_plane/all_to_all | solution.py:419
  76.9 1.9 %collective-permute-start.6 = (bf16[1024,512]{1,0:T(8,128)(2,1)S(1)}, bf16[1024,512]{1,0:T(8,128)(2,1)S(1)}, u32[]{:S(2)}, u32[]{:S(2)}) collective-permute-start(bf16[1024,512]{1,0:T(8,128)(2,1)S(1)} %bitcast.32), channel_id=1, source_target_pairs={{0,1},{1,0},{2,3},{3,2},{4,5},{5,4},{6,7},{7,6},{8,9},{9,8},{10,11... | collective-permute-start | bytes 3145736 | tf_op jit(solution)/shard_map/weight_other/ppermute | solution.py:536
  78.8 2.4 %collective-permute-start.4 = (bf16[144,512]{1,0:T(8,128)(2,1)S(1)}, bf16[144,512]{1,0:T(8,128)(2,1)S(1)}, u32[]{:S(2)}, u32[]{:S(2)}) collective-permute-start(bf16[144,512]{1,0:T(8,128)(2,1)S(1)} %copy-done.15), channel_id=1, source_target_pairs={{0,1},{1,2},{2,3},{3,4},{4,5},{5,6},{6,7},{7,8},{8,9},{9,10},{10,1... | collective-permute-start | bytes 442376 | tf_op jit(solution)/shard_map/lon_back/ppermute | solution.py:415
  81.2 11.9 %all-to-all-done.1 = bf16[16,16,2048]{2,1,0:T(8,128)(2,1)} async-done(((bf16[16,16,2048]{2,1,0:T(8,128)(2,1)}), bf16[16,16,2048]{2,1,0:T(8,128)(2,1)}, u32[]{:S(2)}, u32[]{:S(2)}) %all-to-all-start.1) | async-done | bytes 1048608 | tf_op jit(solution)/shard_map/term_plane/all_to_all | solution.py:419
  93.1 2.0 %reduce_sum.24 = bf16[16,2048]{1,0:T(8,128)(2,1)} reduce(bf16[16,16,2048]{2,1,0:T(8,128)(2,1)} %all-to-all-done.1, bf16[]{:T(256)} %constant.56.clone.1), dimensions={0}, to_apply=%region_0.1 | reduce | flops 491520 | bytes 1114114 | tf_op jit(solution)/shard_map/term_z/reduce_sum | solution.py:435
  95.1 15.0 %all-to-all-start.2 = ((bf16[16,8,256]{2,1,0:T(8,128)(2,1)}), bf16[16,8,256]{2,1,0:T(8,128)(2,1)S(1)}, u32[]{:S(2)}, u32[]{:S(2)}) async-start(bf16[16,8,256]{2,1,0:T(8,128)(2,1)} %bitcast.22), calls=%async_computation.2 | async-start | bytes 131072 | tf_op jit(solution)/shard_map/term_z/all_to_all | solution.py:419
  110.1 3.8 %collective-permute-start.5 = (bf16[144,512]{1,0:T(8,128)(2,1)S(1)}, bf16[144,512]{1,0:T(8,128)(2,1)S(1)}, u32[]{:S(2)}, u32[]{:S(2)}) collective-permute-start(bf16[144,512]{1,0:T(8,128)(2,1)S(1)} %pad_maximum_fusion.3), channel_id=1, source_target_pairs={{0,64},{64,128},{128,192},{192,256},{256,320},{320,384},{384,448},... | collective-permute-start | bytes 442376 | tf_op jit(solution)/shard_map/lat_back/ppermute | solution.py:415
  114.0 9.6 %all-to-all-done.2 = bf16[16,8,256]{2,1,0:T(8,128)(2,1)S(1)} async-done(((bf16[16,8,256]{2,1,0:T(8,128)(2,1)}), bf16[16,8,256]{2,1,0:T(8,128)(2,1)S(1)}, u32[]{:S(2)}, u32[]{:S(2)}) %all-to-all-start.2) | async-done | bytes 65568 | tf_op jit(solution)/shard_map/term_z/all_to_all | solution.py:419
  124.2 3.3 %all-to-all-start.3 = ((bf16[8,8,256]{2,1,0:T(8,128)(2,1)}), bf16[8,8,256]{2,1,0:T(8,128)(2,1)S(1)}, u32[]{:S(2)}, u32[]{:S(2)}) async-start(bf16[8,8,256]{2,1,0:T(8,128)(2,1)} %broadcast_in_dim.30), calls=%async_computation.3 | async-start | bytes 65536 | tf_op jit(solution)/shard_map/term_lat/all_to_all | solution.py:419
  127.8 2.1 %finish.1 = (bf16[144,512]{1,0:T(8,128)(2,1)S(1)}, bf16[36,512]{1,0:T(8,128)(2,1)S(1)}) custom-call(s32[2]{0:T(128)S(1)} %pad_add_fusion.1.place_ref, bf16[144,512]{1,0:T(8,128)(2,1)S(1)} %copy-done.1, bf16[144,512]{1,0:T(8,128)(2,1)S(1)} %copy-done.2, bf16[72,512]{1,0:T(8,128)(2,1)S(1)} %copy-done.3, bf16[144,512]{1,0:T(8,128)(2,1)S(1)} %collective-permute-done.5.lat_ref, ...), custom_call_target="tpu_custom_call" | custom-call | tf_op jit(solution)/shard_map/finish/pallas_call | solution.py:400
  131.3 6.8 %all-to-all-done.3 = bf16[8,8,256]{2,1,0:T(8,128)(2,1)S(1)} async-done(((bf16[8,8,256]{2,1,0:T(8,128)(2,1)}), bf16[8,8,256]{2,1,0:T(8,128)(2,1)S(1)}, u32[]{:S(2)}, u32[]{:S(2)}) %all-to-all-start.3) | async-done | bytes 32800 | tf_op jit(solution)/shard_map/term_lat/all_to_all | solution.py:419
  (82 shorter events, 12.6 us)
Async XLA Ops:
  0.6 8.4 %copy-start.13 = (bf16[32,512]{1,0:T(8,128)(2,1)S(1)}, bf16[32,512]{1,0:T(8,128)(2,1)}, u32[]{:S(2)}) copy-start(bf16[32,512]{1,0:T(8,128)(2,1)} %param.19) | copy-start | bytes 98308
  0.7 8.4 %collective-permute-start.1 = (bf16[32,512]{1,0:T(8,128)(2,1)}, bf16[32,512]{1,0:T(8,128)(2,1)S(1)}, u32[]{:S(2)}, u32[]{:S(2)}) collective-permute-start(bf16[32,512]{1,0:T(8,128)(2,1)} %param.19), channel_id=1, source_target_pairs={{0,1},{1,0},{2,3},{3,2},{4,5},{5,4},{6,7},{7,6},{8,9},{9,8},{10,11... | collective-permute-start | bytes 98312 | tf_op jit(solution)/shard_map/weight_core/ppermute | solution.py:499
  4.7 4.4 %collective-permute-start = (bf16[144,512]{1,0:T(8,128)(2,1)S(1)}, bf16[144,512]{1,0:T(8,128)(2,1)S(1)}, u32[]{:S(2)}, u32[]{:S(2)}) collective-permute-start(bf16[144,512]{1,0:T(8,128)(2,1)S(1)} %pad_maximum_fusion.1), channel_id=1, source_target_pairs={{1,0},{3,2},{5,4},{7,6},{9,8},{11,10},{13,12},{15,14},{17,16},{19,... | collective-permute-start | bytes 442376 | tf_op jit(solution)/shard_map/lon_core/ppermute | solution.py:497
  8.0 18.2 %copy-start.7 = (bf16[2,6,12,512]{3,0,2,1:T(2,128)(2,1)S(1)}, bf16[2,6,12,512]{3,0,2,1:T(2,128)(2,1)}, u32[]{:S(2)}) copy-start(bf16[2,6,12,512]{3,0,2,1:T(2,128)(2,1)} %param.11) | copy-start | bytes 442372
  22.3 13.0 %collective-permute-start.2 = (bf16[208,512]{1,0:T(8,128)(2,1)S(1)}, bf16[208,512]{1,0:T(8,128)(2,1)S(1)}, u32[]{:S(2)}, u32[]{:S(2)}) collective-permute-start(bf16[208,512]{1,0:T(8,128)(2,1)S(1)} %pad_maximum_fusion), channel_id=1, source_target_pairs={{0,63},{2,1},{4,3},{6,5},{8,7},{10,9},{12,11},{14,13},{16,15},{18,... | collective-permute-start | bytes 638984 | tf_op jit(solution)/shard_map/lon_cross/ppermute | solution.py:506
  26.3 9.0 %copy-start.11 = (bf16[144,512]{1,0:T(8,128)(2,1)S(1)}, bf16[144,512]{1,0:T(8,128)(2,1)}, u32[]{:S(2)}) copy-start(bf16[144,512]{1,0:T(8,128)(2,1)} %copy-done.10) | copy-start | bytes 442372
  27.9 20.8 %copy-start.6 = (bf16[2,6,12,512]{3,0,2,1:T(2,128)(2,1)S(1)}, bf16[2,6,12,512]{3,0,2,1:T(2,128)(2,1)}, u32[]{:S(2)}) copy-start(bf16[2,6,12,512]{3,0,2,1:T(2,128)(2,1)} %param.10) | copy-start | bytes 442372
  35.3 14.9 %copy-start.5 = (bf16[144,512]{1,0:T(8,128)(2,1)}, bf16[144,512]{1,0:T(8,128)(2,1)S(1)}, u32[]{:S(2)}) copy-start(bf16[144,512]{1,0:T(8,128)(2,1)S(1)} %slice_select_fusion.lon_ref) | copy-start | bytes 442372
  36.5 25.6 %all-to-all-start = ((bf16[16,64,512]{2,1,0:T(8,128)(2,1)}), bf16[16,64,512]{2,1,0:T(8,128)(2,1)S(1)}, u32[]{:S(2)}, u32[]{:S(2)}) async-start(bf16[16,64,512]{2,1,0:T(8,128)(2,1)} %broadcast_in_dim.29), calls=%async_computation | async-start | bytes 2097152 | tf_op jit(solution)/shard_map/weight_plane/all_to_all | solution.py:419
  43.9 8.3 %collective-permute-start.3 = (bf16[144,512]{1,0:T(8,128)(2,1)S(1)}, bf16[144,512]{1,0:T(8,128)(2,1)S(1)}, u32[]{:S(2)}, u32[]{:S(2)}) collective-permute-start(bf16[144,512]{1,0:T(8,128)(2,1)S(1)} %pad_maximum_fusion.2), channel_id=1, source_target_pairs={{0,448},{64,0},{128,64},{192,128},{256,192},{320,256},{384,320},{4... | collective-permute-start | bytes 442376 | tf_op jit(solution)/shard_map/lat_roll/ppermute | solution.py:415
  62.1 4.8 %collective-permute-start.7 = (bf16[256,2048]{1,0:T(8,128)(2,1)}, bf16[256,2048]{1,0:T(8,128)(2,1)S(1)}, u32[]{:S(2)}, u32[]{:S(2)}) collective-permute-start(bf16[256,2048]{1,0:T(8,128)(2,1)} %get-tuple-element.37), channel_id=1, source_target_pairs={{0,1},{1,0},{2,3},{3,2},{4,5},{5,4},{6,7},{7,6},{8,9},{9,8},{10,11... | collective-permute-start | bytes 3145736 | tf_op jit(solution)/shard_map/term_core/ppermute | solution.py:525
  66.8 12.0 %copy-start.15 = (bf16[144,512]{1,0:T(8,128)(2,1)S(1)}, bf16[144,512]{1,0:T(8,128)(2,1)}, u32[]{:S(2)}) copy-start(bf16[144,512]{1,0:T(8,128)(2,1)} %get-tuple-element.30) | copy-start | bytes 442372
  69.4 40.7 %copy-start.12 = (bf16[72,512]{1,0:T(8,128)(2,1)S(1)}, bf16[72,512]{1,0:T(8,128)(2,1)}, u32[]{:S(2)}) copy-start(bf16[72,512]{1,0:T(8,128)(2,1)} %get-tuple-element.29) | copy-start | bytes 221188
  69.4 58.1 %copy-start.14 = (f32[2048]{0:T(1024)S(1)}, f32[2048]{0:T(1024)}, u32[]{:S(2)}) copy-start(f32[2048]{0:T(1024)} %param.18) | copy-start | bytes 24580
  69.4 58.4 %copy-start.1 = (bf16[144,512]{1,0:T(8,128)(2,1)S(1)}, bf16[144,512]{1,0:T(8,128)(2,1)}, u32[]{:S(2)}) copy-start(bf16[144,512]{1,0:T(8,128)(2,1)} %reshape.75.x_ref) | copy-start | bytes 442372
  69.4 58.4 %copy-start.2 = (bf16[144,512]{1,0:T(8,128)(2,1)S(1)}, bf16[144,512]{1,0:T(8,128)(2,1)}, u32[]{:S(2)}) copy-start(bf16[144,512]{1,0:T(8,128)(2,1)} %reshape.76.u_ref) | copy-start | bytes 442372
  69.4 58.4 %copy-start.3 = (bf16[72,512]{1,0:T(8,128)(2,1)S(1)}, bf16[72,512]{1,0:T(8,128)(2,1)}, u32[]{:S(2)}) copy-start(bf16[72,512]{1,0:T(8,128)(2,1)} %get-tuple-element.28.stay_ref) | copy-start | bytes 221188
  69.4 58.4 %copy-start.4 = (f32[512]{0:T(512)S(1)}, f32[512]{0:T(512)}, u32[]{:S(2)}) copy-start(f32[512]{0:T(512)} %param.12) | copy-start | bytes 6148
  69.5 23.6 %all-to-all-start.1 = ((bf16[16,16,2048]{2,1,0:T(8,128)(2,1)}), bf16[16,16,2048]{2,1,0:T(8,128)(2,1)}, u32[]{:S(2)}, u32[]{:S(2)}) async-start(bf16[16,16,2048]{2,1,0:T(8,128)(2,1)} %bitcast.19), calls=%async_computation.1 | async-start | bytes 2097152 | tf_op jit(solution)/shard_map/term_plane/all_to_all | solution.py:419
  76.9 50.9 %collective-permute-start.6 = (bf16[1024,512]{1,0:T(8,128)(2,1)S(1)}, bf16[1024,512]{1,0:T(8,128)(2,1)S(1)}, u32[]{:S(2)}, u32[]{:S(2)}) collective-permute-start(bf16[1024,512]{1,0:T(8,128)(2,1)S(1)} %bitcast.32), channel_id=1, source_target_pairs={{0,1},{1,0},{2,3},{3,2},{4,5},{5,4},{6,7},{7,6},{8,9},{9,8},{10,11... | collective-permute-start | bytes 3145736 | tf_op jit(solution)/shard_map/weight_other/ppermute | solution.py:536
  78.8 31.3 %collective-permute-start.4 = (bf16[144,512]{1,0:T(8,128)(2,1)S(1)}, bf16[144,512]{1,0:T(8,128)(2,1)S(1)}, u32[]{:S(2)}, u32[]{:S(2)}) collective-permute-start(bf16[144,512]{1,0:T(8,128)(2,1)S(1)} %copy-done.15), channel_id=1, source_target_pairs={{0,1},{1,2},{2,3},{3,4},{4,5},{5,6},{6,7},{7,8},{8,9},{9,10},{10,1... | collective-permute-start | bytes 442376 | tf_op jit(solution)/shard_map/lon_back/ppermute | solution.py:415
  95.1 28.4 %all-to-all-start.2 = ((bf16[16,8,256]{2,1,0:T(8,128)(2,1)}), bf16[16,8,256]{2,1,0:T(8,128)(2,1)S(1)}, u32[]{:S(2)}, u32[]{:S(2)}) async-start(bf16[16,8,256]{2,1,0:T(8,128)(2,1)} %bitcast.22), calls=%async_computation.2 | async-start | bytes 131072 | tf_op jit(solution)/shard_map/term_z/all_to_all | solution.py:419
  110.1 17.7 %collective-permute-start.5 = (bf16[144,512]{1,0:T(8,128)(2,1)S(1)}, bf16[144,512]{1,0:T(8,128)(2,1)S(1)}, u32[]{:S(2)}, u32[]{:S(2)}) collective-permute-start(bf16[144,512]{1,0:T(8,128)(2,1)S(1)} %pad_maximum_fusion.3), channel_id=1, source_target_pairs={{0,64},{64,128},{128,192},{192,256},{256,320},{320,384},{384,448},... | collective-permute-start | bytes 442376 | tf_op jit(solution)/shard_map/lat_back/ppermute | solution.py:415
  124.2 13.9 %all-to-all-start.3 = ((bf16[8,8,256]{2,1,0:T(8,128)(2,1)}), bf16[8,8,256]{2,1,0:T(8,128)(2,1)S(1)}, u32[]{:S(2)}, u32[]{:S(2)}) async-start(bf16[8,8,256]{2,1,0:T(8,128)(2,1)} %broadcast_in_dim.30), calls=%async_computation.3 | async-start | bytes 65536 | tf_op jit(solution)/shard_map/term_lat/all_to_all | solution.py:419
  (4 other events, 11.1 us)

commit v4 on v3

--- a/solution.py
+++ b/solution.py
@@ -80,9 +80,9 @@
     return found
 
 
-def bias_kernel(turn_ref, index_ref, table_ref, key_group_ref, query_group_ref, *refs):
-    given_ref = refs[0] if len(refs) == 3 else None
-    bias_ref, tail_ref = refs[-2:]
+def bias_kernel(turn_ref, index_ref, table_in_ref, key_group_ref, query_group_ref, *refs):
+    given_ref = refs[0] if len(refs) == 4 else None
+    bias_ref, tail_ref, table_ref = refs[-3:]
     rest = TOK - 128
     per_row = 128 // rest
 
@@ -117,6 +117,7 @@
 
     @pl.when(turn_ref[0] == 1)
     def _():
+        table_ref[:, : table_in_ref.shape[1]] = table_in_ref[...]
         lax.fori_loop(0, TOK // 8, main_rows, 0)
         lax.fori_loop(0, tail_ref.shape[1] // 8, tail_rows, 0)
         lax.fori_loop(0, TOK // per_row, spread_rows, 0)
@@ -130,9 +131,7 @@
 
 
 def bias_operands(bias_table, bias_index, groups):
-    rows = bias_table.shape[0]
-    padded = -(-rows // 128) * 128
-    table = jnp.pad(bias_table.T, ((0, 0), (0, padded - rows)))
+    table = bias_table.T
     index = bias_index.reshape(TOK, TOK).T
     tail = index[:, 128:].reshape(-1, 128)
     tail = jnp.pad(tail, ((0, -tail.shape[0] % 8), (0, 0)))
@@ -145,12 +144,16 @@
 
 def gather_bias(turn, operands, *given):
     tail = operands[0].shape[0] - TOK
+    table_width = -(-operands[1].shape[1] // 128) * 128
     return pl.pallas_call(
         bias_kernel,
         out_shape=jax.ShapeDtypeStruct((HEADS, TOK, TOK), F32),
         in_specs=[SMEM] + [VMEM] * (4 + len(given)),
         out_specs=VMEM,
-        scratch_shapes=[pltpu.VMEM((HEADS, tail, 128), F32)],
+        scratch_shapes=[
+            pltpu.VMEM((HEADS, tail, 128), F32),
+            pltpu.VMEM((HEADS, table_width), F32),
+        ],
         compiler_params=pltpu.CompilerParams(vmem_limit_bytes=12 * 1024 * 1024),
         name="bias_gather",
     )(turn, *operands, *given)
@@ -478,10 +481,7 @@
     def rows_of(block):
         return block.transpose(1, 2, 0, 3).reshape(-1, width)
 
-    x, u = rows_of(latent), rows_of(upstream)
-    lon_half = [rows_of(array[:, :, :HALF_LON]) for array in (latent, upstream)]
-    lat_half = [rows_of(array[:, :HALF_LAT, HALF_LON:]) for array in (latent, upstream)]
-    lon_half = jnp.concatenate(lon_half)
+    lon_half = jnp.concatenate([rows_of(array[:, :, :HALF_LON]) for array in (latent, upstream)])
     lat_global = lax.axis_index("lat") * lat_count + lax.broadcasted_iota(
         jnp.int32, regions.shape, 1
     )
@@ -501,7 +501,9 @@
     leaving = jnp.concatenate([lon_half] + pair)
     early, from_core, leaving = lax.optimization_barrier((early, from_core, leaving))
     bias = gather_bias(early, operands)
-    leaving, bias = lax.optimization_barrier((leaving, bias))
+    leaving, bias, latent, upstream = lax.optimization_barrier((leaving, bias, latent, upstream))
+    x, u = rows_of(latent), rows_of(upstream)
+    lat_half = [rows_of(array[:, :HALF_LAT, HALF_LON:]) for array in (latent, upstream)]
     with jax.named_scope("lon_cross"):
         from_chip = lax.ppermute(leaving, "lon", to_chip)
     bias = gather_bias(1 - early, operands, bias)

time: 140 us -> 139 us (level)
    ppermute x1, waiting for transfers between devices: 7.4 us -> 5.97 us  [on_device(): from_chip = lax.ppermute(leaving, 'lon', to_chip)]
    unnamed x33 -> x31, local copies, waits for them, and re-layouts: 3.71 us -> 3.71 us
  transfers between devices with their start and end apart: 12 -> 12, of which waited for: 6 -> 6; matrix products, arithmetic and copies ran while one was open for 8% -> 9% of each run, Pallas kernels for 8% -> 8%
where the time goes in v4:
time: 139 us; the launch traced here: 138 us
  starting transfers between devices  54.3 us (39%)
  waiting for transfers between devices  39.1 us (28%)
  Pallas kernels  23.9 us (17%)
  local copies, waits for them, and re-layouts  13.3 us (10%)
  other arithmetic  6.4 us (5%)
    all_to_all x4, starting transfers between devices, exchanged(): lax.all_to_all(array, axes, 0, 0, axis_index_groups=groups, tiled=True)  32.2 us
    all_to_all x4, waiting for transfers between devices, exchanged(): lax.all_to_all(array, axes, 0, 0, axis_index_groups=groups, tiled=True)  28.2 us
    pallas_call x2, Pallas kernels, gather_bias(): pl.pallas_call(bias_kernel, out_shape=jax.ShapeDtypeStruct((HEADS, TOK, T...  12.7 us
    ppermute x3, starting transfers between devices, shifted(): lax.ppermute(array, axis, [(i, (i + by) % size) for i in range(size)])  11 us
    pallas_call x1, Pallas kernels, attention(): pl.pallas_call(attention_kernel, out_shape=(jax.ShapeDtypeStruct((2 * PAR...  9.17 us
    ppermute x1, waiting for transfers between devices, on_device(): from_chip = lax.ppermute(leaving, 'lon', to_chip)  5.97 us
    ppermute x1, starting transfers between devices, on_device(): from_chip = lax.ppermute(leaving, 'lon', to_chip)  3.92 us
    unnamed x31, local copies, waits for them, and re-layouts  3.71 us
  transfers between devices with their start and end apart: 12, of which 6 were waited for; matrix products, arithmetic and copies ran while one was open for 9% of the time, Pallas kernels for 8%

profile of v4, /device:TPU:2, one launch (start us, length us, event | category | flops | bytes accessed | tf_op | source)
XLA Modules:
  0.0 138.2 jit_solution(2306809023449025367)
XLA Ops:
  0.6 2.1 %collective-permute-start.1 = (bf16[32,512]{1,0:T(8,128)(2,1)}, bf16[32,512]{1,0:T(8,128)(2,1)S(1)}, u32[]{:S(2)}, u32[]{:S(2)}) collective-permute-start(bf16[32,512]{1,0:T(8,128)(2,1)} %param.19), channel_id=1, source_target_pairs={{0,1},{1,0},{2,3},{3,2},{4,5},{5,4},{6,7},{7,6},{8,9},{9,8},{10,11... | collective-permute-start | bytes 98312 | tf_op jit(solution)/shard_map/weight_core/ppermute | solution.py:499
  4.7 1.3 collective-permute-start
  9.6 12.5 %bias_gather.2.refs_0_ = f32[16,144,144]{2,1,0:T(8,128)S(1)} custom-call(s32[1]{0:T(128)} %bitcast.2.turn_ref, s32[168,128]{1,0:T(8,128)S(1)} %pad_add_fusion.index_ref, f32[16,3312]{1,0:T(8,128)S(1)} %bitcast.34, s32[144,128]{1,0:T(8,128)S(1)} %broadcast_in_dim.26.key_group_ref, s32[1,256]{1,0:T(1,128)S(1)} %bitcast.36), custom_call_target="tpu_custom_call" | custom-call | tf_op jit(solution)/shard_map/bias_gather/pallas_call | solution.py:148
  22.1 3.9 %collective-permute-start.2 = (bf16[208,512]{1,0:T(8,128)(2,1)S(1)}, bf16[208,512]{1,0:T(8,128)(2,1)S(1)}, u32[]{:S(2)}, u32[]{:S(2)}) collective-permute-start(bf16[208,512]{1,0:T(8,128)(2,1)S(1)} %pad_maximum_fusion), channel_id=1, source_target_pairs={{0,63},{2,1},{4,3},{6,5},{8,7},{10,9},{12,11},{14,13},{16,15},{18,... | collective-permute-start | bytes 638984 | tf_op jit(solution)/shard_map/lon_cross/ppermute | solution.py:508
  27.7 1.4 %copy-done = f32[16,144,144]{2,1,0:T(8,128)} copy-done((f32[16,144,144]{2,1,0:T(8,128)}, f32[16,144,144]{2,1,0:T(8,128)S(1)}, u32[]{:S(2)}) %copy-start) | copy-done | bytes 1327128
  29.1 6.0 %collective-permute-done.2 = bf16[208,512]{1,0:T(8,128)(2,1)S(1)} collective-permute-done((bf16[208,512]{1,0:T(8,128)(2,1)S(1)}, bf16[208,512]{1,0:T(8,128)(2,1)S(1)}, u32[]{:S(2)}, u32[]{:S(2)}) %collective-permute-start.2) | collective-permute-done | bytes 213024 | tf_op jit(solution)/shard_map/lon_cross/ppermute | solution.py:508
  36.3 7.5 %all-to-all-start = ((bf16[16,64,512]{2,1,0:T(8,128)(2,1)}), bf16[16,64,512]{2,1,0:T(8,128)(2,1)S(1)}, u32[]{:S(2)}, u32[]{:S(2)}) async-start(bf16[16,64,512]{2,1,0:T(8,128)(2,1)} %broadcast_in_dim.29), calls=%async_computation | async-start | bytes 2097152 | tf_op jit(solution)/shard_map/weight_plane/all_to_all | solution.py:422
  43.8 4.8 %collective-permute-start.3 = (bf16[144,512]{1,0:T(8,128)(2,1)S(1)}, bf16[144,512]{1,0:T(8,128)(2,1)S(1)}, u32[]{:S(2)}, u32[]{:S(2)}) collective-permute-start(bf16[144,512]{1,0:T(8,128)(2,1)S(1)} %pad_maximum_fusion.2), channel_id=1, source_target_pairs={{0,448},{64,0},{128,64},{192,128},{256,192},{320,256},{384,320},{4... | collective-permute-start | bytes 442376 | tf_op jit(solution)/shard_map/lat_roll/ppermute | solution.py:418
  50.0 2.1 %collective-permute-done.3.lat_ref = bf16[144,512]{1,0:T(8,128)(2,1)S(1)} collective-permute-done((bf16[144,512]{1,0:T(8,128)(2,1)S(1)}, bf16[144,512]{1,0:T(8,128)(2,1)S(1)}, u32[]{:S(2)}, u32[]{:S(2)}) %collective-permute-start.3) | collective-permute-done | bytes 147488 | tf_op jit(solution)/shard_map/lat_roll/ppermute | solution.py:418
  52.7 9.2 %window_attention.1 = (bf16[72,512]{1,0:T(8,128)(2,1)}, bf16[144,512]{1,0:T(8,128)(2,1)}, bf16[72,512]{1,0:T(8,128)(2,1)}, bf16[256,2048]{1,0:T(8,128)(2,1)}, bf16[256,2048]{1,0:T(8,128)(2,1)}) custom-call(s32[1]{0:T(128)} %bitcast.core_ref, bf16[144,512]{1,0:T(8,128)(2,1)} %reshape.81.x_ref, bf16[144,512]{1,0:T(8,128)(2,1)} %reshape.82.u_ref, ...), custom_call_target="tpu_custom_call" | custom-call | tf_op jit(solution)/shard_map/window_attention/pallas_call | solution.py:302
  61.9 1.9 %collective-permute-start.7 = (bf16[256,2048]{1,0:T(8,128)(2,1)}, bf16[256,2048]{1,0:T(8,128)(2,1)S(1)}, u32[]{:S(2)}, u32[]{:S(2)}) collective-permute-start(bf16[256,2048]{1,0:T(8,128)(2,1)} %get-tuple-element.41), channel_id=1, source_target_pairs={{0,1},{1,0},{2,3},{3,2},{4,5},{5,4},{6,7},{7,6},{8,9},{9,8},{10,11... | collective-permute-start | bytes 3145736 | tf_op jit(solution)/shard_map/term_core/ppermute | solution.py:527
  63.8 2.8 %collective-permute-done.7 = bf16[256,2048]{1,0:T(8,128)(2,1)S(1)} collective-permute-done((bf16[256,2048]{1,0:T(8,128)(2,1)}, bf16[256,2048]{1,0:T(8,128)(2,1)S(1)}, u32[]{:S(2)}, u32[]{:S(2)}) %collective-permute-start.7) | collective-permute-done | bytes 1048608 | tf_op jit(solution)/shard_map/term_core/ppermute | solution.py:527
  66.6 2.6 %add_convert_fusion = bf16[256,2048]{1,0:T(8,128)(2,1)} fusion(bf16[256,2048]{1,0:T(8,128)(2,1)S(1)} %collective-permute-done.7, bf16[256,2048]{1,0:T(8,128)(2,1)} %get-tuple-element.40), kind=kLoop, calls=%fused_computation | loop fusion | flops 2097152 | bytes 3145728 | tf_op jit(solution)/shard_map/convert_element_type | solution.py:528
  69.3 7.4 %all-to-all-start.1 = ((bf16[16,16,2048]{2,1,0:T(8,128)(2,1)}), bf16[16,16,2048]{2,1,0:T(8,128)(2,1)}, u32[]{:S(2)}, u32[]{:S(2)}) async-start(bf16[16,16,2048]{2,1,0:T(8,128)(2,1)} %bitcast.19), calls=%async_computation.1 | async-start | bytes 2097152 | tf_op jit(solution)/shard_map/term_plane/all_to_all | solution.py:422
  76.7 1.9 %collective-permute-start.6 = (bf16[1024,512]{1,0:T(8,128)(2,1)S(1)}, bf16[1024,512]{1,0:T(8,128)(2,1)S(1)}, u32[]{:S(2)}, u32[]{:S(2)}) collective-permute-start(bf16[1024,512]{1,0:T(8,128)(2,1)S(1)} %bitcast.32), channel_id=1, source_target_pairs={{0,1},{1,0},{2,3},{3,2},{4,5},{5,4},{6,7},{7,6},{8,9},{9,8},{10,11... | collective-permute-start | bytes 3145736 | tf_op jit(solution)/shard_map/weight_other/ppermute | solution.py:538
  78.6 2.4 %collective-permute-start.4 = (bf16[144,512]{1,0:T(8,128)(2,1)S(1)}, bf16[144,512]{1,0:T(8,128)(2,1)S(1)}, u32[]{:S(2)}, u32[]{:S(2)}) collective-permute-start(bf16[144,512]{1,0:T(8,128)(2,1)S(1)} %copy-done.14), channel_id=1, source_target_pairs={{0,1},{1,2},{2,3},{3,4},{4,5},{5,6},{6,7},{7,8},{8,9},{9,10},{10,1... | collective-permute-start | bytes 442376 | tf_op jit(solution)/shard_map/lon_back/ppermute | solution.py:418
  81.0 11.9 %all-to-all-done.1 = bf16[16,16,2048]{2,1,0:T(8,128)(2,1)} async-done(((bf16[16,16,2048]{2,1,0:T(8,128)(2,1)}), bf16[16,16,2048]{2,1,0:T(8,128)(2,1)}, u32[]{:S(2)}, u32[]{:S(2)}) %all-to-all-start.1) | async-done | bytes 1048608 | tf_op jit(solution)/shard_map/term_plane/all_to_all | solution.py:422
  92.9 2.0 %reduce_sum.24 = bf16[16,2048]{1,0:T(8,128)(2,1)} reduce(bf16[16,16,2048]{2,1,0:T(8,128)(2,1)} %all-to-all-done.1, bf16[]{:T(256)} %constant.54.clone.1), dimensions={0}, to_apply=%region_0.1 | reduce | flops 491520 | bytes 1114114 | tf_op jit(solution)/shard_map/term_z/reduce_sum | solution.py:438
  94.9 14.0 %all-to-all-start.2 = ((bf16[16,8,256]{2,1,0:T(8,128)(2,1)}), bf16[16,8,256]{2,1,0:T(8,128)(2,1)S(1)}, u32[]{:S(2)}, u32[]{:S(2)}) async-start(bf16[16,8,256]{2,1,0:T(8,128)(2,1)} %bitcast.22), calls=%async_computation.2 | async-start | bytes 131072 | tf_op jit(solution)/shard_map/term_z/all_to_all | solution.py:422
  109.0 3.8 %collective-permute-start.5 = (bf16[144,512]{1,0:T(8,128)(2,1)S(1)}, bf16[144,512]{1,0:T(8,128)(2,1)S(1)}, u32[]{:S(2)}, u32[]{:S(2)}) collective-permute-start(bf16[144,512]{1,0:T(8,128)(2,1)S(1)} %pad_maximum_fusion.3), channel_id=1, source_target_pairs={{0,64},{64,128},{128,192},{192,256},{256,320},{320,384},{384,448},... | collective-permute-start | bytes 442376 | tf_op jit(solution)/shard_map/lat_back/ppermute | solution.py:418
  112.8 9.6 %all-to-all-done.2 = bf16[16,8,256]{2,1,0:T(8,128)(2,1)S(1)} async-done(((bf16[16,8,256]{2,1,0:T(8,128)(2,1)}), bf16[16,8,256]{2,1,0:T(8,128)(2,1)S(1)}, u32[]{:S(2)}, u32[]{:S(2)}) %all-to-all-start.2) | async-done | bytes 65568 | tf_op jit(solution)/shard_map/term_z/all_to_all | solution.py:422
  123.0 3.3 %all-to-all-start.3 = ((bf16[8,8,256]{2,1,0:T(8,128)(2,1)}), bf16[8,8,256]{2,1,0:T(8,128)(2,1)S(1)}, u32[]{:S(2)}, u32[]{:S(2)}) async-start(bf16[8,8,256]{2,1,0:T(8,128)(2,1)} %broadcast_in_dim.30), calls=%async_computation.3 | async-start | bytes 65536 | tf_op jit(solution)/shard_map/term_lat/all_to_all | solution.py:422
  126.7 2.1 %finish.1 = (bf16[144,512]{1,0:T(8,128)(2,1)S(1)}, bf16[36,512]{1,0:T(8,128)(2,1)S(1)}) custom-call(s32[2]{0:T(128)S(1)} %pad_add_fusion.1.place_ref, bf16[144,512]{1,0:T(8,128)(2,1)S(1)} %copy-done.1, bf16[144,512]{1,0:T(8,128)(2,1)S(1)} %copy-done.2, bf16[72,512]{1,0:T(8,128)(2,1)S(1)} %copy-done.4, bf16[144,512]{1,0:T(8,128)(2,1)S(1)} %collective-permute-done.5.lat_ref, ...), custom_call_target="tpu_custom_call" | custom-call | tf_op jit(solution)/shard_map/finish/pallas_call | solution.py:403
  130.1 6.8 %all-to-all-done.3 = bf16[8,8,256]{2,1,0:T(8,128)(2,1)S(1)} async-done(((bf16[8,8,256]{2,1,0:T(8,128)(2,1)}), bf16[8,8,256]{2,1,0:T(8,128)(2,1)S(1)}, u32[]{:S(2)}, u32[]{:S(2)}) %all-to-all-start.3) | async-done | bytes 32800 | tf_op jit(solution)/shard_map/term_lat/all_to_all | solution.py:422
  (78 shorter events, 13.9 us)
Async XLA Ops:
  0.6 9.0 %copy-start.3 = (f32[3312,16]{0,1:T(8,128)S(1)}, f32[3312,16]{0,1:T(8,128)}, u32[]{:S(2)}) copy-start(f32[3312,16]{0,1:T(8,128)} %param.15) | copy-start | bytes 635908
  0.6 7.5 %collective-permute-start.1 = (bf16[32,512]{1,0:T(8,128)(2,1)}, bf16[32,512]{1,0:T(8,128)(2,1)S(1)}, u32[]{:S(2)}, u32[]{:S(2)}) collective-permute-start(bf16[32,512]{1,0:T(8,128)(2,1)} %param.19), channel_id=1, source_target_pairs={{0,1},{1,0},{2,3},{3,2},{4,5},{5,4},{6,7},{7,6},{8,9},{9,8},{10,11... | collective-permute-start | bytes 98312 | tf_op jit(solution)/shard_map/weight_core/ppermute | solution.py:499
  4.7 4.2 %collective-permute-start = (bf16[144,512]{1,0:T(8,128)(2,1)S(1)}, bf16[144,512]{1,0:T(8,128)(2,1)S(1)}, u32[]{:S(2)}, u32[]{:S(2)}) collective-permute-start(bf16[144,512]{1,0:T(8,128)(2,1)S(1)} %pad_maximum_fusion.1), channel_id=1, source_target_pairs={{1,0},{3,2},{5,4},{7,6},{9,8},{11,10},{13,12},{15,14},{17,16},{19,... | collective-permute-start | bytes 442376 | tf_op jit(solution)/shard_map/lon_core/ppermute | solution.py:497
  7.0 19.0 %copy-start.7 = (bf16[2,6,12,512]{3,0,2,1:T(2,128)(2,1)S(1)}, bf16[2,6,12,512]{3,0,2,1:T(2,128)(2,1)}, u32[]{:S(2)}) copy-start(bf16[2,6,12,512]{3,0,2,1:T(2,128)(2,1)} %param.10) | copy-start | bytes 442372
  7.0 19.0 %copy-start.8 = (bf16[2,6,12,512]{3,0,2,1:T(2,128)(2,1)S(1)}, bf16[2,6,12,512]{3,0,2,1:T(2,128)(2,1)}, u32[]{:S(2)}) copy-start(bf16[2,6,12,512]{3,0,2,1:T(2,128)(2,1)} %param.11) | copy-start | bytes 442372
  22.1 13.0 %collective-permute-start.2 = (bf16[208,512]{1,0:T(8,128)(2,1)S(1)}, bf16[208,512]{1,0:T(8,128)(2,1)S(1)}, u32[]{:S(2)}, u32[]{:S(2)}) collective-permute-start(bf16[208,512]{1,0:T(8,128)(2,1)S(1)} %pad_maximum_fusion), channel_id=1, source_target_pairs={{0,63},{2,1},{4,3},{6,5},{8,7},{10,9},{12,11},{14,13},{16,15},{18,... | collective-permute-start | bytes 638984 | tf_op jit(solution)/shard_map/lon_cross/ppermute | solution.py:508
  27.5 7.6 %copy-start.11 = (bf16[144,512]{1,0:T(8,128)(2,1)S(1)}, bf16[144,512]{1,0:T(8,128)(2,1)}, u32[]{:S(2)}) copy-start(bf16[144,512]{1,0:T(8,128)(2,1)} %copy-done.10) | copy-start | bytes 442372
  35.1 14.9 %copy-start.6 = (bf16[144,512]{1,0:T(8,128)(2,1)}, bf16[144,512]{1,0:T(8,128)(2,1)S(1)}, u32[]{:S(2)}) copy-start(bf16[144,512]{1,0:T(8,128)(2,1)S(1)} %slice_select_fusion.lon_ref) | copy-start | bytes 442372
  36.3 25.6 %all-to-all-start = ((bf16[16,64,512]{2,1,0:T(8,128)(2,1)}), bf16[16,64,512]{2,1,0:T(8,128)(2,1)S(1)}, u32[]{:S(2)}, u32[]{:S(2)}) async-start(bf16[16,64,512]{2,1,0:T(8,128)(2,1)} %broadcast_in_dim.29), calls=%async_computation | async-start | bytes 2097152 | tf_op jit(solution)/shard_map/weight_plane/all_to_all | solution.py:422
  43.8 8.3 %collective-permute-start.3 = (bf16[144,512]{1,0:T(8,128)(2,1)S(1)}, bf16[144,512]{1,0:T(8,128)(2,1)S(1)}, u32[]{:S(2)}, u32[]{:S(2)}) collective-permute-start(bf16[144,512]{1,0:T(8,128)(2,1)S(1)} %pad_maximum_fusion.2), channel_id=1, source_target_pairs={{0,448},{64,0},{128,64},{192,128},{256,192},{320,256},{384,320},{4... | collective-permute-start | bytes 442376 | tf_op jit(solution)/shard_map/lat_roll/ppermute | solution.py:418
  61.9 4.8 %collective-permute-start.7 = (bf16[256,2048]{1,0:T(8,128)(2,1)}, bf16[256,2048]{1,0:T(8,128)(2,1)S(1)}, u32[]{:S(2)}, u32[]{:S(2)}) collective-permute-start(bf16[256,2048]{1,0:T(8,128)(2,1)} %get-tuple-element.41), channel_id=1, source_target_pairs={{0,1},{1,0},{2,3},{3,2},{4,5},{5,4},{6,7},{7,6},{8,9},{9,8},{10,11... | collective-permute-start | bytes 3145736 | tf_op jit(solution)/shard_map/term_core/ppermute | solution.py:527
  66.6 12.0 %copy-start.14 = (bf16[144,512]{1,0:T(8,128)(2,1)S(1)}, bf16[144,512]{1,0:T(8,128)(2,1)}, u32[]{:S(2)}) copy-start(bf16[144,512]{1,0:T(8,128)(2,1)} %get-tuple-element.34) | copy-start | bytes 442372
  69.3 39.7 %copy-start.12 = (bf16[72,512]{1,0:T(8,128)(2,1)S(1)}, bf16[72,512]{1,0:T(8,128)(2,1)}, u32[]{:S(2)}) copy-start(bf16[72,512]{1,0:T(8,128)(2,1)} %get-tuple-element.33) | copy-start | bytes 221188
  69.3 57.1 %copy-start.13 = (f32[2048]{0:T(1024)S(1)}, f32[2048]{0:T(1024)}, u32[]{:S(2)}) copy-start(f32[2048]{0:T(1024)} %param.18) | copy-start | bytes 24580
  69.3 57.4 %copy-start.1 = (bf16[144,512]{1,0:T(8,128)(2,1)S(1)}, bf16[144,512]{1,0:T(8,128)(2,1)}, u32[]{:S(2)}) copy-start(bf16[144,512]{1,0:T(8,128)(2,1)} %reshape.81.x_ref) | copy-start | bytes 442372
  69.3 57.4 %copy-start.2 = (bf16[144,512]{1,0:T(8,128)(2,1)S(1)}, bf16[144,512]{1,0:T(8,128)(2,1)}, u32[]{:S(2)}) copy-start(bf16[144,512]{1,0:T(8,128)(2,1)} %reshape.82.u_ref) | copy-start | bytes 442372
  69.3 57.4 %copy-start.4 = (bf16[72,512]{1,0:T(8,128)(2,1)S(1)}, bf16[72,512]{1,0:T(8,128)(2,1)}, u32[]{:S(2)}) copy-start(bf16[72,512]{1,0:T(8,128)(2,1)} %get-tuple-element.32.stay_ref) | copy-start | bytes 221188
  69.3 57.4 %copy-start.5 = (f32[512]{0:T(512)S(1)}, f32[512]{0:T(512)}, u32[]{:S(2)}) copy-start(f32[512]{0:T(512)} %param.12) | copy-start | bytes 6148
  69.3 23.6 %all-to-all-start.1 = ((bf16[16,16,2048]{2,1,0:T(8,128)(2,1)}), bf16[16,16,2048]{2,1,0:T(8,128)(2,1)}, u32[]{:S(2)}, u32[]{:S(2)}) async-start(bf16[16,16,2048]{2,1,0:T(8,128)(2,1)} %bitcast.19), calls=%async_computation.1 | async-start | bytes 2097152 | tf_op jit(solution)/shard_map/term_plane/all_to_all | solution.py:422
  76.7 49.9 %collective-permute-start.6 = (bf16[1024,512]{1,0:T(8,128)(2,1)S(1)}, bf16[1024,512]{1,0:T(8,128)(2,1)S(1)}, u32[]{:S(2)}, u32[]{:S(2)}) collective-permute-start(bf16[1024,512]{1,0:T(8,128)(2,1)S(1)} %bitcast.32), channel_id=1, source_target_pairs={{0,1},{1,0},{2,3},{3,2},{4,5},{5,4},{6,7},{7,6},{8,9},{9,8},{10,11... | collective-permute-start | bytes 3145736 | tf_op jit(solution)/shard_map/weight_other/ppermute | solution.py:538
  78.6 30.3 %collective-permute-start.4 = (bf16[144,512]{1,0:T(8,128)(2,1)S(1)}, bf16[144,512]{1,0:T(8,128)(2,1)S(1)}, u32[]{:S(2)}, u32[]{:S(2)}) collective-permute-start(bf16[144,512]{1,0:T(8,128)(2,1)S(1)} %copy-done.14), channel_id=1, source_target_pairs={{0,1},{1,2},{2,3},{3,4},{4,5},{5,6},{6,7},{7,8},{8,9},{9,10},{10,1... | collective-permute-start | bytes 442376 | tf_op jit(solution)/shard_map/lon_back/ppermute | solution.py:418
  94.9 27.4 %all-to-all-start.2 = ((bf16[16,8,256]{2,1,0:T(8,128)(2,1)}), bf16[16,8,256]{2,1,0:T(8,128)(2,1)S(1)}, u32[]{:S(2)}, u32[]{:S(2)}) async-start(bf16[16,8,256]{2,1,0:T(8,128)(2,1)} %bitcast.22), calls=%async_computation.2 | async-start | bytes 131072 | tf_op jit(solution)/shard_map/term_z/all_to_all | solution.py:422
  109.0 17.7 %collective-permute-start.5 = (bf16[144,512]{1,0:T(8,128)(2,1)S(1)}, bf16[144,512]{1,0:T(8,128)(2,1)S(1)}, u32[]{:S(2)}, u32[]{:S(2)}) collective-permute-start(bf16[144,512]{1,0:T(8,128)(2,1)S(1)} %pad_maximum_fusion.3), channel_id=1, source_target_pairs={{0,64},{64,128},{128,192},{192,256},{256,320},{320,384},{384,448},... | collective-permute-start | bytes 442376 | tf_op jit(solution)/shard_map/lat_back/ppermute | solution.py:418
  123.0 13.9 %all-to-all-start.3 = ((bf16[8,8,256]{2,1,0:T(8,128)(2,1)}), bf16[8,8,256]{2,1,0:T(8,128)(2,1)S(1)}, u32[]{:S(2)}, u32[]{:S(2)}) async-start(bf16[8,8,256]{2,1,0:T(8,128)(2,1)} %broadcast_in_dim.30), calls=%async_computation.3 | async-start | bytes 65536 | tf_op jit(solution)/shard_map/term_lat/all_to_all | solution.py:422
  (3 other events, 2.7 us)

commit v5 on v4

--- a/solution.py
+++ b/solution.py
@@ -476,7 +476,6 @@
     first_core = core == 0
     between_cores = [(i, i ^ 1) for i in range(lon_size)]
     to_chip = [(i, (i - 1) % lon_size) for i in range(0, lon_size, 2)]
-    to_core = [(i, i - 1) for i in range(1, lon_size, 2)]
 
     def rows_of(block):
         return block.transpose(1, 2, 0, 3).reshape(-1, width)
@@ -493,13 +492,13 @@
     )
     operands = bias_operands(bias_table, bias_index, groups)
     early = ((core == 0) & (high == 0)).astype(jnp.int32).reshape(1)
+    half_rows = lon_half.shape[0]
     with jax.named_scope("lon_core"):
-        from_core = lax.ppermute(lon_half, "lon", to_core)
-    with jax.named_scope("weight_core"):
-        other = lax.ppermute(merge_weight, "lon", between_cores)
+        between = lax.ppermute(jnp.concatenate([lon_half, merge_weight]), "lon", between_cores)
+    from_core, other = between[:half_rows], between[half_rows:]
     pair = [jnp.where(first_core, merge_weight, other), jnp.where(first_core, other, merge_weight)]
     leaving = jnp.concatenate([lon_half] + pair)
-    early, from_core, leaving = lax.optimization_barrier((early, from_core, leaving))
+    early, leaving = lax.optimization_barrier((early, leaving))
     bias = gather_bias(early, operands)
     leaving, bias, latent, upstream = lax.optimization_barrier((leaving, bias, latent, upstream))
     x, u = rows_of(latent), rows_of(upstream)
@@ -507,7 +506,6 @@
     with jax.named_scope("lon_cross"):
         from_chip = lax.ppermute(leaving, "lon", to_chip)
     bias = gather_bias(1 - early, operands, bias)
-    half_rows = lon_half.shape[0]
     lon_half = jnp.where(first_core, from_core, from_chip[:half_rows])
     pair = jnp.where(first_core, leaving[half_rows:], from_chip[half_rows:])
     lat_half += [lon_half[:PART], lon_half[2 * PART : 3 * PART]]

time: 139 us -> 137 us (0.986)
  starting transfers between devices: 54.3 us -> 52.8 us
    ppermute x2 -> x1, starting transfers between devices: 3.35 us -> 1.92 us  [on_device(): lax.ppermute(jnp.concatenate([lon_half, merge_weight]), 'lon', between_co...]
  transfers between devices with their start and end apart: 12 -> 11, of which waited for: 6 -> 6; matrix products, arithmetic and copies ran while one was open for 9% -> 7% of each run, Pallas kernels for 8% -> 8%
where the time goes in v5:
time: 137 us; the launch traced here: 136 us
  starting transfers between devices  52.8 us (39%)
  waiting for transfers between devices  38.4 us (28%)
  Pallas kernels  23.9 us (17%)
  local copies, waits for them, and re-layouts  12.8 us (9%)
  other arithmetic  7.18 us (5%)
    all_to_all x4, starting transfers between devices, exchanged(): lax.all_to_all(array, axes, 0, 0, axis_index_groups=groups, tiled=True)  32.1 us
    all_to_all x4, waiting for transfers between devices, exchanged(): lax.all_to_all(array, axes, 0, 0, axis_index_groups=groups, tiled=True)  28.2 us
    pallas_call x2, Pallas kernels, gather_bias(): pl.pallas_call(bias_kernel, out_shape=jax.ShapeDtypeStruct((HEADS, TOK, T...  12.7 us
    ppermute x3, starting transfers between devices, shifted(): lax.ppermute(array, axis, [(i, (i + by) % size) for i in range(size)])  11.7 us
    pallas_call x1, Pallas kernels, attention(): pl.pallas_call(attention_kernel, out_shape=(jax.ShapeDtypeStruct((2 * PAR...  9.16 us
    ppermute x1, waiting for transfers between devices, on_device(): from_chip = lax.ppermute(leaving, 'lon', to_chip)  5.93 us
    ppermute x1, starting transfers between devices, on_device(): from_chip = lax.ppermute(leaving, 'lon', to_chip)  3.31 us
    unnamed x31, local copies, waits for them, and re-layouts  3.18 us
  transfers between devices with their start and end apart: 11, of which 6 were waited for; matrix products, arithmetic and copies ran while one was open for 7% of the time, Pallas kernels for 8%

profile of v5, /device:TPU:2, one launch (start us, length us, event | category | flops | bytes accessed | tf_op | source)
XLA Modules:
  0.0 136.2 jit_solution(12581177272097358526)
XLA Ops:
  3.4 1.9 %collective-permute-start = (bf16[176,512]{1,0:T(8,128)(2,1)S(1)}, bf16[176,512]{1,0:T(8,128)(2,1)S(1)}, u32[]{:S(2)}, u32[]{:S(2)}) collective-permute-start(bf16[176,512]{1,0:T(8,128)(2,1)S(1)} %pad_maximum_fusion.1), channel_id=1, source_target_pairs={{0,1},{1,0},{2,3},{3,2},{4,5},{5,4},{6,7},{7,6},{8,9},{9,8},{10,11... | collective-permute-start | bytes 540680 | tf_op jit(solution)/shard_map/lon_core/ppermute | solution.py:497
  8.4 12.5 %bias_gather.2.refs_0_ = f32[16,144,144]{2,1,0:T(8,128)S(1)} custom-call(s32[1]{0:T(128)} %bitcast.2.turn_ref, s32[168,128]{1,0:T(8,128)S(1)} %pad_add_fusion.index_ref, f32[16,3312]{1,0:T(8,128)S(1)} %bitcast.34, s32[144,128]{1,0:T(8,128)S(1)} %broadcast_in_dim.26.key_group_ref, s32[1,256]{1,0:T(1,128)S(1)} %bitcast.36), custom_call_target="tpu_custom_call" | custom-call | tf_op jit(solution)/shard_map/bias_gather/pallas_call | solution.py:148
  20.9 3.3 %collective-permute-start.1 = (bf16[208,512]{1,0:T(8,128)(2,1)S(1)}, bf16[208,512]{1,0:T(8,128)(2,1)S(1)}, u32[]{:S(2)}, u32[]{:S(2)}) collective-permute-start(bf16[208,512]{1,0:T(8,128)(2,1)S(1)} %pad_maximum_fusion), channel_id=1, source_target_pairs={{0,63},{2,1},{4,3},{6,5},{8,7},{10,9},{12,11},{14,13},{16,15},{18,... | collective-permute-start | bytes 638984 | tf_op jit(solution)/shard_map/lon_cross/ppermute | solution.py:507
  26.0 1.4 %copy-done = f32[16,144,144]{2,1,0:T(8,128)} copy-done((f32[16,144,144]{2,1,0:T(8,128)}, f32[16,144,144]{2,1,0:T(8,128)S(1)}, u32[]{:S(2)}) %copy-start) | copy-done | bytes 1327128
  27.4 5.9 %collective-permute-done.1 = bf16[208,512]{1,0:T(8,128)(2,1)S(1)} collective-permute-done((bf16[208,512]{1,0:T(8,128)(2,1)S(1)}, bf16[208,512]{1,0:T(8,128)(2,1)S(1)}, u32[]{:S(2)}, u32[]{:S(2)}) %collective-permute-start.1) | collective-permute-done | bytes 213024 | tf_op jit(solution)/shard_map/lon_cross/ppermute | solution.py:507
  33.4 1.1 broadcast_in_dim.29
  34.5 7.5 %all-to-all-start = ((bf16[16,64,512]{2,1,0:T(8,128)(2,1)}), bf16[16,64,512]{2,1,0:T(8,128)(2,1)S(1)}, u32[]{:S(2)}, u32[]{:S(2)}) async-start(bf16[16,64,512]{2,1,0:T(8,128)(2,1)} %broadcast_in_dim.29), calls=%async_computation | async-start | bytes 2097152 | tf_op jit(solution)/shard_map/weight_plane/all_to_all | solution.py:422
  42.0 5.4 %collective-permute-start.2 = (bf16[144,512]{1,0:T(8,128)(2,1)S(1)}, bf16[144,512]{1,0:T(8,128)(2,1)S(1)}, u32[]{:S(2)}, u32[]{:S(2)}) collective-permute-start(bf16[144,512]{1,0:T(8,128)(2,1)S(1)} %pad_maximum_fusion.2), channel_id=1, source_target_pairs={{0,448},{64,0},{128,64},{192,128},{256,192},{320,256},{384,320},{4... | collective-permute-start | bytes 442376 | tf_op jit(solution)/shard_map/lat_roll/ppermute | solution.py:418
  48.8 1.5 %collective-permute-done.2.lat_ref = bf16[144,512]{1,0:T(8,128)(2,1)S(1)} collective-permute-done((bf16[144,512]{1,0:T(8,128)(2,1)S(1)}, bf16[144,512]{1,0:T(8,128)(2,1)S(1)}, u32[]{:S(2)}, u32[]{:S(2)}) %collective-permute-start.2) | collective-permute-done | bytes 147488 | tf_op jit(solution)/shard_map/lat_roll/ppermute | solution.py:418
  51.0 9.2 %window_attention.1 = (bf16[72,512]{1,0:T(8,128)(2,1)}, bf16[144,512]{1,0:T(8,128)(2,1)}, bf16[72,512]{1,0:T(8,128)(2,1)}, bf16[256,2048]{1,0:T(8,128)(2,1)}, bf16[256,2048]{1,0:T(8,128)(2,1)}) custom-call(s32[1]{0:T(128)} %bitcast.core_ref, bf16[144,512]{1,0:T(8,128)(2,1)} %reshape.81.x_ref, bf16[144,512]{1,0:T(8,128)(2,1)} %reshape.82.u_ref, ...), custom_call_target="tpu_custom_call" | custom-call | tf_op jit(solution)/shard_map/window_attention/pallas_call | solution.py:302
  60.1 1.9 %collective-permute-start.6 = (bf16[256,2048]{1,0:T(8,128)(2,1)}, bf16[256,2048]{1,0:T(8,128)(2,1)S(1)}, u32[]{:S(2)}, u32[]{:S(2)}) collective-permute-start(bf16[256,2048]{1,0:T(8,128)(2,1)} %get-tuple-element.39), channel_id=1, source_target_pairs={{0,1},{1,0},{2,3},{3,2},{4,5},{5,4},{6,7},{7,6},{8,9},{9,8},{10,11... | collective-permute-start | bytes 3145736 | tf_op jit(solution)/shard_map/term_core/ppermute | solution.py:525
  62.0 2.8 %collective-permute-done.6 = bf16[256,2048]{1,0:T(8,128)(2,1)S(1)} collective-permute-done((bf16[256,2048]{1,0:T(8,128)(2,1)}, bf16[256,2048]{1,0:T(8,128)(2,1)S(1)}, u32[]{:S(2)}, u32[]{:S(2)}) %collective-permute-start.6) | collective-permute-done | bytes 1048608 | tf_op jit(solution)/shard_map/term_core/ppermute | solution.py:525
  64.9 2.6 %add_convert_fusion = bf16[256,2048]{1,0:T(8,128)(2,1)} fusion(bf16[256,2048]{1,0:T(8,128)(2,1)S(1)} %collective-permute-done.6, bf16[256,2048]{1,0:T(8,128)(2,1)} %get-tuple-element.38), kind=kLoop, calls=%fused_computation | loop fusion | flops 2097152 | bytes 3145728 | tf_op jit(solution)/shard_map/convert_element_type | solution.py:526
  67.5 7.4 %all-to-all-start.1 = ((bf16[16,16,2048]{2,1,0:T(8,128)(2,1)}), bf16[16,16,2048]{2,1,0:T(8,128)(2,1)}, u32[]{:S(2)}, u32[]{:S(2)}) async-start(bf16[16,16,2048]{2,1,0:T(8,128)(2,1)} %bitcast.19), calls=%async_computation.1 | async-start | bytes 2097152 | tf_op jit(solution)/shard_map/term_plane/all_to_all | solution.py:422
  74.9 1.9 %collective-permute-start.5 = (bf16[1024,512]{1,0:T(8,128)(2,1)S(1)}, bf16[1024,512]{1,0:T(8,128)(2,1)S(1)}, u32[]{:S(2)}, u32[]{:S(2)}) collective-permute-start(bf16[1024,512]{1,0:T(8,128)(2,1)S(1)} %bitcast.32), channel_id=1, source_target_pairs={{0,1},{1,0},{2,3},{3,2},{4,5},{5,4},{6,7},{7,6},{8,9},{9,8},{10,11... | collective-permute-start | bytes 3145736 | tf_op jit(solution)/shard_map/weight_other/ppermute | solution.py:536
  76.9 2.4 %collective-permute-start.3 = (bf16[144,512]{1,0:T(8,128)(2,1)S(1)}, bf16[144,512]{1,0:T(8,128)(2,1)S(1)}, u32[]{:S(2)}, u32[]{:S(2)}) collective-permute-start(bf16[144,512]{1,0:T(8,128)(2,1)S(1)} %copy-done.14), channel_id=1, source_target_pairs={{0,1},{1,2},{2,3},{3,4},{4,5},{5,6},{6,7},{7,8},{8,9},{9,10},{10,1... | collective-permute-start | bytes 442376 | tf_op jit(solution)/shard_map/lon_back/ppermute | solution.py:418
  79.3 11.9 %all-to-all-done.1 = bf16[16,16,2048]{2,1,0:T(8,128)(2,1)} async-done(((bf16[16,16,2048]{2,1,0:T(8,128)(2,1)}), bf16[16,16,2048]{2,1,0:T(8,128)(2,1)}, u32[]{:S(2)}, u32[]{:S(2)}) %all-to-all-start.1) | async-done | bytes 1048608 | tf_op jit(solution)/shard_map/term_plane/all_to_all | solution.py:422
  91.1 2.0 %reduce_sum.24 = bf16[16,2048]{1,0:T(8,128)(2,1)} reduce(bf16[16,16,2048]{2,1,0:T(8,128)(2,1)} %all-to-all-done.1, bf16[]{:T(256)} %constant.54.clone.1), dimensions={0}, to_apply=%region_0.1 | reduce | flops 491520 | bytes 1114114 | tf_op jit(solution)/shard_map/term_z/reduce_sum | solution.py:438
  93.1 13.8 %all-to-all-start.2 = ((bf16[16,8,256]{2,1,0:T(8,128)(2,1)}), bf16[16,8,256]{2,1,0:T(8,128)(2,1)S(1)}, u32[]{:S(2)}, u32[]{:S(2)}) async-start(bf16[16,8,256]{2,1,0:T(8,128)(2,1)} %bitcast.22), calls=%async_computation.2 | async-start | bytes 131072 | tf_op jit(solution)/shard_map/term_z/all_to_all | solution.py:422
  107.0 3.8 %collective-permute-start.4 = (bf16[144,512]{1,0:T(8,128)(2,1)S(1)}, bf16[144,512]{1,0:T(8,128)(2,1)S(1)}, u32[]{:S(2)}, u32[]{:S(2)}) collective-permute-start(bf16[144,512]{1,0:T(8,128)(2,1)S(1)} %pad_maximum_fusion.3), channel_id=1, source_target_pairs={{0,64},{64,128},{128,192},{192,256},{256,320},{320,384},{384,448},... | collective-permute-start | bytes 442376 | tf_op jit(solution)/shard_map/lat_back/ppermute | solution.py:418
  110.9 9.5 %all-to-all-done.2 = bf16[16,8,256]{2,1,0:T(8,128)(2,1)S(1)} async-done(((bf16[16,8,256]{2,1,0:T(8,128)(2,1)}), bf16[16,8,256]{2,1,0:T(8,128)(2,1)S(1)}, u32[]{:S(2)}, u32[]{:S(2)}) %all-to-all-start.2) | async-done | bytes 65568 | tf_op jit(solution)/shard_map/term_z/all_to_all | solution.py:422
  121.0 3.3 %all-to-all-start.3 = ((bf16[8,8,256]{2,1,0:T(8,128)(2,1)}), bf16[8,8,256]{2,1,0:T(8,128)(2,1)S(1)}, u32[]{:S(2)}, u32[]{:S(2)}) async-start(bf16[8,8,256]{2,1,0:T(8,128)(2,1)} %broadcast_in_dim.30), calls=%async_computation.3 | async-start | bytes 65536 | tf_op jit(solution)/shard_map/term_lat/all_to_all | solution.py:422
  124.7 2.1 %finish.1 = (bf16[144,512]{1,0:T(8,128)(2,1)S(1)}, bf16[36,512]{1,0:T(8,128)(2,1)S(1)}) custom-call(s32[2]{0:T(128)S(1)} %pad_add_fusion.1.place_ref, bf16[144,512]{1,0:T(8,128)(2,1)S(1)} %copy-done.1, bf16[144,512]{1,0:T(8,128)(2,1)S(1)} %copy-done.2, bf16[72,512]{1,0:T(8,128)(2,1)S(1)} %copy-done.4, bf16[144,512]{1,0:T(8,128)(2,1)S(1)} %collective-permute-done.4.lat_ref, ...), custom_call_target="tpu_custom_call" | custom-call | tf_op jit(solution)/shard_map/finish/pallas_call | solution.py:403
  128.2 6.8 %all-to-all-done.3 = bf16[8,8,256]{2,1,0:T(8,128)(2,1)S(1)} async-done(((bf16[8,8,256]{2,1,0:T(8,128)(2,1)}), bf16[8,8,256]{2,1,0:T(8,128)(2,1)S(1)}, u32[]{:S(2)}, u32[]{:S(2)}) %all-to-all-start.3) | async-done | bytes 32800 | tf_op jit(solution)/shard_map/term_lat/all_to_all | solution.py:422
  (76 shorter events, 13.1 us)
Async XLA Ops:
  0.6 7.8 %copy-start.3 = (f32[3312,16]{0,1:T(8,128)S(1)}, f32[3312,16]{0,1:T(8,128)}, u32[]{:S(2)}) copy-start(f32[3312,16]{0,1:T(8,128)} %param.15) | copy-start | bytes 635908
  3.4 4.1 %collective-permute-start = (bf16[176,512]{1,0:T(8,128)(2,1)S(1)}, bf16[176,512]{1,0:T(8,128)(2,1)S(1)}, u32[]{:S(2)}, u32[]{:S(2)}) collective-permute-start(bf16[176,512]{1,0:T(8,128)(2,1)S(1)} %pad_maximum_fusion.1), channel_id=1, source_target_pairs={{0,1},{1,0},{2,3},{3,2},{4,5},{5,4},{6,7},{7,6},{8,9},{9,8},{10,11... | collective-permute-start | bytes 540680 | tf_op jit(solution)/shard_map/lon_core/ppermute | solution.py:497
  6.2 18.1 %copy-start.7 = (bf16[2,6,12,512]{3,0,2,1:T(2,128)(2,1)S(1)}, bf16[2,6,12,512]{3,0,2,1:T(2,128)(2,1)}, u32[]{:S(2)}) copy-start(bf16[2,6,12,512]{3,0,2,1:T(2,128)(2,1)} %param.10) | copy-start | bytes 442372
  6.2 18.1 %copy-start.8 = (bf16[2,6,12,512]{3,0,2,1:T(2,128)(2,1)S(1)}, bf16[2,6,12,512]{3,0,2,1:T(2,128)(2,1)}, u32[]{:S(2)}) copy-start(bf16[2,6,12,512]{3,0,2,1:T(2,128)(2,1)} %param.11) | copy-start | bytes 442372
  20.9 12.4 %collective-permute-start.1 = (bf16[208,512]{1,0:T(8,128)(2,1)S(1)}, bf16[208,512]{1,0:T(8,128)(2,1)S(1)}, u32[]{:S(2)}, u32[]{:S(2)}) collective-permute-start(bf16[208,512]{1,0:T(8,128)(2,1)S(1)} %pad_maximum_fusion), channel_id=1, source_target_pairs={{0,63},{2,1},{4,3},{6,5},{8,7},{10,9},{12,11},{14,13},{16,15},{18,... | collective-permute-start | bytes 638984 | tf_op jit(solution)/shard_map/lon_cross/ppermute | solution.py:507
  25.8 7.5 %copy-start.10 = (bf16[176,512]{1,0:T(8,128)(2,1)S(1)}, bf16[176,512]{1,0:T(8,128)(2,1)}, u32[]{:S(2)}) copy-start(bf16[176,512]{1,0:T(8,128)(2,1)} %copy-done.9) | copy-start | bytes 540676
  25.9 1.4 %copy-start = (f32[16,144,144]{2,1,0:T(8,128)}, f32[16,144,144]{2,1,0:T(8,128)S(1)}, u32[]{:S(2)}) copy-start(f32[16,144,144]{2,1,0:T(8,128)S(1)} %bias_gather.3.bias_ref) | copy-start | bytes 3981316
  33.3 15.5 %copy-start.6 = (bf16[144,512]{1,0:T(8,128)(2,1)}, bf16[144,512]{1,0:T(8,128)(2,1)S(1)}, u32[]{:S(2)}) copy-start(bf16[144,512]{1,0:T(8,128)(2,1)S(1)} %slice_select_fusion.lon_ref) | copy-start | bytes 442372
  34.5 25.6 %all-to-all-start = ((bf16[16,64,512]{2,1,0:T(8,128)(2,1)}), bf16[16,64,512]{2,1,0:T(8,128)(2,1)S(1)}, u32[]{:S(2)}, u32[]{:S(2)}) async-start(bf16[16,64,512]{2,1,0:T(8,128)(2,1)} %broadcast_in_dim.29), calls=%async_computation | async-start | bytes 2097152 | tf_op jit(solution)/shard_map/weight_plane/all_to_all | solution.py:422
  42.0 8.3 %collective-permute-start.2 = (bf16[144,512]{1,0:T(8,128)(2,1)S(1)}, bf16[144,512]{1,0:T(8,128)(2,1)S(1)}, u32[]{:S(2)}, u32[]{:S(2)}) collective-permute-start(bf16[144,512]{1,0:T(8,128)(2,1)S(1)} %pad_maximum_fusion.2), channel_id=1, source_target_pairs={{0,448},{64,0},{128,64},{192,128},{256,192},{320,256},{384,320},{4... | collective-permute-start | bytes 442376 | tf_op jit(solution)/shard_map/lat_roll/ppermute | solution.py:418
  60.1 4.8 %collective-permute-start.6 = (bf16[256,2048]{1,0:T(8,128)(2,1)}, bf16[256,2048]{1,0:T(8,128)(2,1)S(1)}, u32[]{:S(2)}, u32[]{:S(2)}) collective-permute-start(bf16[256,2048]{1,0:T(8,128)(2,1)} %get-tuple-element.39), channel_id=1, source_target_pairs={{0,1},{1,0},{2,3},{3,2},{4,5},{5,4},{6,7},{7,6},{8,9},{9,8},{10,11... | collective-permute-start | bytes 3145736 | tf_op jit(solution)/shard_map/term_core/ppermute | solution.py:525
  64.9 12.0 %copy-start.14 = (bf16[144,512]{1,0:T(8,128)(2,1)S(1)}, bf16[144,512]{1,0:T(8,128)(2,1)}, u32[]{:S(2)}) copy-start(bf16[144,512]{1,0:T(8,128)(2,1)} %get-tuple-element.32) | copy-start | bytes 442372
  67.5 39.5 %copy-start.12 = (bf16[72,512]{1,0:T(8,128)(2,1)S(1)}, bf16[72,512]{1,0:T(8,128)(2,1)}, u32[]{:S(2)}) copy-start(bf16[72,512]{1,0:T(8,128)(2,1)} %get-tuple-element.31) | copy-start | bytes 221188
  67.5 56.9 %copy-start.13 = (f32[2048]{0:T(1024)S(1)}, f32[2048]{0:T(1024)}, u32[]{:S(2)}) copy-start(f32[2048]{0:T(1024)} %param.18) | copy-start | bytes 24580
  67.5 57.2 %copy-start.1 = (bf16[144,512]{1,0:T(8,128)(2,1)S(1)}, bf16[144,512]{1,0:T(8,128)(2,1)}, u32[]{:S(2)}) copy-start(bf16[144,512]{1,0:T(8,128)(2,1)} %reshape.81.x_ref) | copy-start | bytes 442372
  67.5 57.2 %copy-start.2 = (bf16[144,512]{1,0:T(8,128)(2,1)S(1)}, bf16[144,512]{1,0:T(8,128)(2,1)}, u32[]{:S(2)}) copy-start(bf16[144,512]{1,0:T(8,128)(2,1)} %reshape.82.u_ref) | copy-start | bytes 442372
  67.5 57.2 %copy-start.4 = (bf16[72,512]{1,0:T(8,128)(2,1)S(1)}, bf16[72,512]{1,0:T(8,128)(2,1)}, u32[]{:S(2)}) copy-start(bf16[72,512]{1,0:T(8,128)(2,1)} %get-tuple-element.30.stay_ref) | copy-start | bytes 221188
  67.5 57.2 %copy-start.5 = (f32[512]{0:T(512)S(1)}, f32[512]{0:T(512)}, u32[]{:S(2)}) copy-start(f32[512]{0:T(512)} %param.12) | copy-start | bytes 6148
  67.5 23.6 %all-to-all-start.1 = ((bf16[16,16,2048]{2,1,0:T(8,128)(2,1)}), bf16[16,16,2048]{2,1,0:T(8,128)(2,1)}, u32[]{:S(2)}, u32[]{:S(2)}) async-start(bf16[16,16,2048]{2,1,0:T(8,128)(2,1)} %bitcast.19), calls=%async_computation.1 | async-start | bytes 2097152 | tf_op jit(solution)/shard_map/term_plane/all_to_all | solution.py:422
  74.9 49.7 %collective-permute-start.5 = (bf16[1024,512]{1,0:T(8,128)(2,1)S(1)}, bf16[1024,512]{1,0:T(8,128)(2,1)S(1)}, u32[]{:S(2)}, u32[]{:S(2)}) collective-permute-start(bf16[1024,512]{1,0:T(8,128)(2,1)S(1)} %bitcast.32), channel_id=1, source_target_pairs={{0,1},{1,0},{2,3},{3,2},{4,5},{5,4},{6,7},{7,6},{8,9},{9,8},{10,11... | collective-permute-start | bytes 3145736 | tf_op jit(solution)/shard_map/weight_other/ppermute | solution.py:536
  76.9 30.1 %collective-permute-start.3 = (bf16[144,512]{1,0:T(8,128)(2,1)S(1)}, bf16[144,512]{1,0:T(8,128)(2,1)S(1)}, u32[]{:S(2)}, u32[]{:S(2)}) collective-permute-start(bf16[144,512]{1,0:T(8,128)(2,1)S(1)} %copy-done.14), channel_id=1, source_target_pairs={{0,1},{1,2},{2,3},{3,4},{4,5},{5,6},{6,7},{7,8},{8,9},{9,10},{10,1... | collective-permute-start | bytes 442376 | tf_op jit(solution)/shard_map/lon_back/ppermute | solution.py:418
  93.1 27.3 %all-to-all-start.2 = ((bf16[16,8,256]{2,1,0:T(8,128)(2,1)}), bf16[16,8,256]{2,1,0:T(8,128)(2,1)S(1)}, u32[]{:S(2)}, u32[]{:S(2)}) async-start(bf16[16,8,256]{2,1,0:T(8,128)(2,1)} %bitcast.22), calls=%async_computation.2 | async-start | bytes 131072 | tf_op jit(solution)/shard_map/term_z/all_to_all | solution.py:422
  107.0 17.6 %collective-permute-start.4 = (bf16[144,512]{1,0:T(8,128)(2,1)S(1)}, bf16[144,512]{1,0:T(8,128)(2,1)S(1)}, u32[]{:S(2)}, u32[]{:S(2)}) collective-permute-start(bf16[144,512]{1,0:T(8,128)(2,1)S(1)} %pad_maximum_fusion.3), channel_id=1, source_target_pairs={{0,64},{64,128},{128,192},{192,256},{256,320},{320,384},{384,448},... | collective-permute-start | bytes 442376 | tf_op jit(solution)/shard_map/lat_back/ppermute | solution.py:418
  121.0 13.9 %all-to-all-start.3 = ((bf16[8,8,256]{2,1,0:T(8,128)(2,1)}), bf16[8,8,256]{2,1,0:T(8,128)(2,1)S(1)}, u32[]{:S(2)}, u32[]{:S(2)}) async-start(bf16[8,8,256]{2,1,0:T(8,128)(2,1)} %broadcast_in_dim.30), calls=%async_computation.3 | async-start | bytes 65536 | tf_op jit(solution)/shard_map/term_lat/all_to_all | solution.py:422
  (2 other events, 1.6 us)
